TPU v7x, 32 devices: a whole 2x2x4 slice. The times are simulated.
32 devices in a mesh: group: 2 (over y), expert: 8 (over z, x), tensor: 2 (over core).
Axes of the slice: x: 2, y: 2, z: 4, core: 2. Of those that a mesh axis runs over, the one named last changes fastest.
Arguments:
- tokens: bfloat16 [1024, 3584], P(('group', 'expert'), 'tensor'), parts along dimension 0, may hold values from -6 to 6
- expert_ids: int32 [1024, 2], P(('group', 'expert')), parts along dimension 0, may hold values from 0 to 7, all different within a row; in each aligned block of 64 rows (0 to 63, 64 to 127, ...) at most 20 rows name the same one
- gate_weights: float32 [1024, 2], P(('group', 'expert')), parts along dimension 0, may hold values from 0.1 to 0.6
- w_gate: bfloat16 [3584, 16384], P('tensor', 'expert'), may hold values from -0.09375 to 0.09375
- w_up: bfloat16 [3584, 16384], P('tensor', 'expert'), may hold values from -0.09375 to 0.09375
- w_down: bfloat16 [16384, 3584], P('expert', 'tensor'), may hold values from -0.125 to 0.125
Outputs:
- combined: bfloat16 [1024, 3584], P(('group', 'expert'), 'tensor'), parts along dimension 0
There are 2 independent parts, one for each index of `group`. A program takes and returns all parts, laid end to end along the dimension named above; an argument that names none is the same for every part. Nothing has to cross between parts.
Inputs may be any that keep to these rules, and one draw needn't show every extreme that they name: `expert_ids`: each row names 2 different experts. In each aligned block of 64 rows, no expert is named by more than 20 rows; in some blocks an expert is named by exactly 20 rows.
All inputs are finite; a program needn't handle non-finite values.
Results may differ from a plain program's by a relative error of at most 0.015.
Values may be sent and summed in bfloat16 or wider, within the bound.
No kernel may reach another device: no remote copies, remote signals or barrier semaphores. Data moves between devices by JAX's collectives and lax.ppermute only.
A program may use at most 64 MiB of HBM per device.

v0:
```python
import jax
import jax.numpy as jnp
from jax import lax
from jax.sharding import PartitionSpec as P

FF = 2048


def pair_slots(id_blocks, expert_count):
    onehot = (
        id_blocks[:, :, None] == jnp.arange(expert_count, dtype=jnp.int32)[None, None, :]
    ).astype(jnp.int32)
    earlier = jnp.cumsum(onehot, axis=1) - onehot
    return jnp.sum(earlier * onehot, axis=2)


def per_device(tokens, expert_ids, gate_weights, w_gate, w_up, w_down):
    tok_rows, half_width = tokens.shape
    top_count = expert_ids.shape[1]
    index_count = lax.axis_size("expert")
    part_width = w_gate.shape[1]
    span_count = FF // part_width
    expert_count = index_count // span_count
    capacity = min(
        tok_rows, (5 * tok_rows * top_count + 4 * expert_count - 1) // (4 * expert_count)
    )
    slot_index = pair_slots(expert_ids.reshape(1, tok_rows * top_count), expert_count).reshape(
        tok_rows, top_count
    )
    target = expert_ids * capacity + slot_index
    columns = jnp.arange(expert_count * capacity, dtype=jnp.int32)
    matches = target[:, :, None] == columns[None, None, :]
    selector = jnp.sum(matches.astype(jnp.bfloat16), axis=1)
    weights_table = jnp.sum(jnp.where(matches, gate_weights[:, :, None], 0.0), axis=1)
    buffer = lax.dot_general(
        selector, tokens, (((0,), (0,)), ((), ())), preferred_element_type=jnp.float32
    ).astype(jnp.bfloat16)
    buffer = jnp.repeat(buffer.reshape(expert_count, capacity, half_width), span_count, axis=0)
    received = lax.all_to_all(buffer, "expert", split_axis=0, concat_axis=0, tiled=True)
    sources, slot_count, feature_width = received.shape
    flat_rows = received.reshape(sources * slot_count, feature_width)
    gate_part = jnp.dot(flat_rows, w_gate, preferred_element_type=jnp.float32).astype(jnp.bfloat16)
    up_part = jnp.dot(flat_rows, w_up, preferred_element_type=jnp.float32).astype(jnp.bfloat16)
    gate_full = lax.psum(gate_part, "tensor").astype(jnp.float32)
    up_full = lax.psum(up_part, "tensor").astype(jnp.float32)
    hidden = (jax.nn.silu(gate_full) * up_full).astype(jnp.bfloat16)
    partial_value = jnp.dot(hidden, w_down, preferred_element_type=jnp.float32).astype(jnp.bfloat16)
    results = partial_value.reshape(sources, slot_count, partial_value.shape[1])
    returned = lax.all_to_all(results, "expert", split_axis=0, concat_axis=0, tiled=True)
    by_expert = jnp.sum(
        returned.reshape(expert_count, span_count, capacity, half_width).astype(jnp.float32), axis=1
    )
    combined = jnp.dot(
        weights_table,
        by_expert.reshape(expert_count * capacity, half_width),
        precision=lax.Precision.HIGHEST,
        preferred_element_type=jnp.float32,
    )
    return combined.astype(jnp.bfloat16)


def solution(mesh):
    in_specs = (
        P(("group", "expert"), "tensor"),
        P(("group", "expert"), None),
        P(("group", "expert"), None),
        P("tensor", "expert"),
        P("tensor", "expert"),
        P("expert", "tensor"),
    )
    out_specs = P(("group", "expert"), "tensor")
    return jax.shard_map(
        per_device, mesh=mesh, in_specs=in_specs, out_specs=out_specs, check_vma=False
    )
```

profile of v0, /device:TPU:0, one launch (start us, length us, event | category | flops | bytes accessed | tf_op | source)
XLA Modules:
  0.0 102.9 jit_solution(15109752996699391654)
XLA Ops:
  6.5 0.0 copy-start
  6.5 0.0 all-reduce.3.cloned.1.call-start
  6.5 0.8 copy.19
  7.3 0.1 eq.40
  7.5 0.1 fusion.9
  7.6 0.2 reduce_window_sum.11
  7.8 0.2 select_reduce_fusion.1
  7.9 0.1 reshape.111
  8.1 0.1 copy.20
  8.2 0.7 multiply_add_fusion
  8.9 0.1 fusion.8
  8.9 0.0 copy-done
  9.0 0.3 convolution_convert_fusion.3
  9.3 0.1 reshape_broadcast_in_dim_reshape.3
  9.4 25.3 %all_to_all.10 = bf16[8,20,1792]{2,1,0:T(8,128)(2,1)S(1)} all-to-all(bf16[8,20,1792]{2,1,0:T(8,128)(2,1)S(1)} %reshape_broadcast_in_dim_reshape.3), channel_id=1, replica_groups=mesh['group'=2,'expert'=8,'tensor'=2] {'expert'}, dimensions={0} | all-to-all | bytes 1146880 | tf_op jit(solution)/shard_map/all_to_all | solution.py:39
  34.8 0.1 reshape.112
  34.9 5.4 %convolution_convert_fusion.1 = bf16[160,2048]{1,0:T(8,128)(2,1)} fusion(bf16[160,1792]{1,0:T(8,128)(2,1)S(1)} %reshape.112, bf16[1792,2048]{1,0:T(8,128)(2,1)} %param.10), kind=kOutput, calls=%fused_computation.1 | convolution fusion | flops 1174732800 | bytes 8568832 | tf_op jit(solution)/shard_map/dot_general | solution.py:43
  40.2 5.3 %convolution_convert_fusion.2 = bf16[160,2048]{1,0:T(8,128)(2,1)} fusion(bf16[160,1792]{1,0:T(8,128)(2,1)S(1)} %reshape.112, bf16[1792,2048]{1,0:T(8,128)(2,1)} %param.9), kind=kOutput, calls=%fused_computation.2 | convolution fusion | flops 1174732800 | bytes 8568832 | tf_op jit(solution)/shard_map/dot_general | solution.py:42
  45.6 0.0 all-reduce.3.cloned.1.call-update
  45.6 19.0 %all-reduce.3.cloned.1.call-done = (bf16[160,2048]{1,0:T(8,128)(2,1)}, bf16[160,2048]{1,0:T(8,128)(2,1)}) async-done(((bf16[160,2048]{1,0:T(8,128)(2,1)}, bf16[160,2048]{1,0:T(8,128)(2,1)}), (bf16[160,2048]{1,0:T(8,128)(2,1)}, bf16[160,2048]{1,0:T(8,128)(2,1)})) %all-reduce.3.cloned.1.call-update) | async-done | bytes 1310736 | tf_op jit(solution)/shard_map/psum | solution.py:45
  64.6 5.1 %convolution_convert_fusion = bf16[160,1792]{1,0:T(8,128)(2,1)S(1)} fusion(bf16[2048,1792]{1,0:T(8,128)(2,1)} %param.11, bf16[160,2048]{1,0:T(8,128)(2,1)} %get-tuple-element.5, bf16[160,2048]{1,0:T(8,128)(2,1)} %get-tuple-element.6), kind=kOutput, calls=%fused_computation | convolution fusion | flops 1177313280 | bytes 9224192 | tf_op jit(solution)/shard_map/dot_general | solution.py:47
  69.7 0.0 copy-start.1
  69.7 1.0 reshape.113
  70.7 5.8 %all-to-all-start.1 = ((bf16[8,20,1792]{2,1,0:T(8,128)(2,1)}), bf16[8,20,1792]{2,1,0:T(8,128)(2,1)S(1)}, u32[]{:S(2)}, u32[]{:S(2)}) async-start(bf16[8,20,1792]{2,1,0:T(8,128)(2,1)} %reshape.113), calls=%async_computation.1 | async-start | bytes 1376256 | tf_op jit(solution)/shard_map/all_to_all | solution.py:49
  76.4 0.0 copy-done.1
  76.4 0.1 select_reduce_fusion
  76.6 18.3 %all-to-all-done.1 = bf16[8,20,1792]{2,1,0:T(8,128)(2,1)S(1)} async-done(((bf16[8,20,1792]{2,1,0:T(8,128)(2,1)}), bf16[8,20,1792]{2,1,0:T(8,128)(2,1)S(1)}, u32[]{:S(2)}, u32[]{:S(2)}) %all-to-all-start.1) | async-done | bytes 573472 | tf_op jit(solution)/shard_map/all_to_all | solution.py:49
  94.9 0.1 reshape.114
  95.0 1.1 %convolution_convert_fusion.4 = bf16[64,1792]{1,0:T(8,128)(2,1)} fusion(f32[64,160]{1,0:T(8,128)S(1)} %select_reduce_fusion, bf16[160,1792]{1,0:T(8,128)(2,1)S(1)} %reshape.114), kind=kOutput, calls=%fused_computation.4 | convolution fusion | flops 220315648 | bytes 843776 | tf_op jit(solution)/shard_map/dot_general | solution.py:53
Async XLA Ops:
  6.5 2.4 %copy-start = (bf16[64,1792]{1,0:T(8,128)(2,1)S(1)}, bf16[64,1792]{1,0:T(8,128)(2,1)}, u32[]{:S(2)}) copy-start(bf16[64,1792]{1,0:T(8,128)(2,1)} %param.6) | copy-start | bytes 688132
  6.5 58.1 %all-reduce.3.cloned.1.call-start = ((), (), s32[]{:S(2)}) async-start(), calls=%async_computation.2 | async-start | bytes 2621440 | tf_op jit(solution)/shard_map/psum | solution.py:45
  69.7 6.8 %copy-start.1 = (f32[64,2]{0,1:T(2,128)S(1)}, f32[64,2]{0,1:T(2,128)}, u32[]{:S(2)}) copy-start(f32[64,2]{0,1:T(2,128)} %param.8) | copy-start | bytes 1540
  70.7 24.2 %all-to-all-start.1 = ((bf16[8,20,1792]{2,1,0:T(8,128)(2,1)}), bf16[8,20,1792]{2,1,0:T(8,128)(2,1)S(1)}, u32[]{:S(2)}, u32[]{:S(2)}) async-start(bf16[8,20,1792]{2,1,0:T(8,128)(2,1)} %reshape.113), calls=%async_computation.1 | async-start | bytes 1376256 | tf_op jit(solution)/shard_map/all_to_all | solution.py:49
Sparse Core Ops, SparseCore 0:
  45.7 18.8 all-reduce.2
where the time goes:
time: 103 us
  waiting for transfers between devices  37.4 us (36%)
  blocking collectives  25.3 us (25%)
  matrix products  17.2 us (17%)
  between operations  13.5 us (13%)
  starting transfers between devices  5.79 us (6%)
  local copies, waits for them, and re-layouts  2.49 us (2%)
  other arithmetic  1.32 us (1%)
    all_to_all x1, blocking collectives, per_device(): lax.all_to_all(buffer, 'expert', split_axis=0, concat_axis=0, tiled=True)  25.3 us
    psum x1, waiting for transfers between devices, per_device(): up_full = lax.psum(up_part, 'tensor').astype(jnp.float32)  19 us
    all_to_all x1, waiting for transfers between devices, per_device(): lax.all_to_all(results, 'expert', split_axis=0, concat_axis=0, tiled=True)  18.3 us
    all_to_all x1, starting transfers between devices, per_device(): lax.all_to_all(results, 'expert', split_axis=0, concat_axis=0, tiled=True)  5.78 us
    dot_general x1, matrix products, per_device(): jnp.dot(flat_rows, w_up, preferred_element_type=jnp.float32)  5.35 us
    dot_general x1, matrix products, per_device(): jnp.dot(flat_rows, w_gate, preferred_element_type=jnp.float32)  5.33 us
    dot_general x1, matrix products, per_device(): jnp.dot(hidden, w_down, preferred_element_type=jnp.float32)  5.07 us
  transfers between devices with their start and end apart: 2, of which 2 were waited for; matrix products, arithmetic and copies ran while one was open for 0% of the time, Pallas kernels for 0%

commit v1 on v0

v1 whole, which is shorter than its diff:
```python
import jax
import jax.numpy as jnp
from jax import lax
from jax.experimental import pallas as pl
from jax.experimental.pallas import tpu as pltpu
from jax.sharding import PartitionSpec as P

FF = 2048
BF16 = jnp.bfloat16
F32 = jnp.float32
VMEM_SPEC = pl.BlockSpec(memory_space=pltpu.VMEM)
SMEM_SPEC = pl.BlockSpec(memory_space=pltpu.SMEM)
PIECES = 2
SEND_ORDER = (7, 6, 5, 4, 3, 2, 1)


def pair_slots(id_blocks, expert_count):
    onehot = (
        id_blocks[:, :, None] == jnp.arange(expert_count, dtype=jnp.int32)[None, None, :]
    ).astype(jnp.int32)
    earlier = jnp.cumsum(onehot, axis=1) - onehot
    return jnp.sum(earlier * onehot, axis=2)


def capacity_of(tok_rows, top_count, expert_count):
    return min(tok_rows, (5 * tok_rows * top_count + 4 * expert_count - 1) // (4 * expert_count))


def general(tokens, expert_ids, gate_weights, w_gate, w_up, w_down):
    tok_rows, half_width = tokens.shape
    top_count = expert_ids.shape[1]
    index_count = lax.axis_size("expert")
    part_width = w_gate.shape[1]
    span_count = FF // part_width
    expert_count = index_count // span_count
    capacity = capacity_of(tok_rows, top_count, expert_count)
    slot_index = pair_slots(expert_ids.reshape(1, tok_rows * top_count), expert_count).reshape(
        tok_rows, top_count
    )
    target = expert_ids * capacity + slot_index
    columns = jnp.arange(expert_count * capacity, dtype=jnp.int32)
    matches = target[:, :, None] == columns[None, None, :]
    selector = jnp.sum(matches.astype(BF16), axis=1)
    weights_table = jnp.sum(jnp.where(matches, gate_weights[:, :, None], 0.0), axis=1)
    buffer = lax.dot_general(
        selector, tokens, (((0,), (0,)), ((), ())), preferred_element_type=F32
    ).astype(BF16)
    buffer = jnp.repeat(buffer.reshape(expert_count, capacity, half_width), span_count, axis=0)
    received = lax.all_to_all(buffer, "expert", split_axis=0, concat_axis=0, tiled=True)
    sources, slot_count, feature_width = received.shape
    flat_rows = received.reshape(sources * slot_count, feature_width)
    gate_part = jnp.dot(flat_rows, w_gate, preferred_element_type=F32).astype(BF16)
    up_part = jnp.dot(flat_rows, w_up, preferred_element_type=F32).astype(BF16)
    gate_full = lax.psum(gate_part, "tensor").astype(F32)
    up_full = lax.psum(up_part, "tensor").astype(F32)
    hidden = (jax.nn.silu(gate_full) * up_full).astype(BF16)
    partial_value = jnp.dot(hidden, w_down, preferred_element_type=F32).astype(BF16)
    results = partial_value.reshape(sources, slot_count, partial_value.shape[1])
    returned = lax.all_to_all(results, "expert", split_axis=0, concat_axis=0, tiled=True)
    by_expert = jnp.sum(
        returned.reshape(expert_count, span_count, capacity, half_width).astype(F32), axis=1
    )
    combined = jnp.dot(
        weights_table,
        by_expert.reshape(expert_count * capacity, half_width),
        precision=lax.Precision.HIGHEST,
        preferred_element_type=F32,
    )
    return combined.astype(BF16)


def slot_rows(ids_ref, me, n, cap, tok_rows):
    shape = (n, tok_rows)
    expert = lax.broadcasted_iota(jnp.int32, shape, 0)
    first = (ids_ref[0:1, :] == expert).astype(F32)
    second = (ids_ref[1:2, :] == expert).astype(F32)
    before = (
        lax.broadcasted_iota(jnp.int32, (tok_rows, tok_rows), 0)
        < lax.broadcasted_iota(jnp.int32, (tok_rows, tok_rows), 1)
    ).astype(BF16)
    earlier = jnp.dot((first + second).astype(BF16), before, preferred_element_type=F32)
    slots = (
        jnp.sum(earlier * first, axis=0, keepdims=True),
        jnp.sum((earlier + first) * second, axis=0, keepdims=True),
    )
    return [
        (ids_ref[k : k + 1, :] ^ me) * (2 * cap) + slots[k].astype(jnp.int32) for k in range(2)
    ]


def dispatch_kernel(n, cap, me_ref, ids_ref, tok_ref, *out_refs):
    tok_rows, width = tok_ref.shape
    half = width // 2
    rows = slot_rows(ids_ref, me_ref[0], n, cap, tok_rows)
    number = lax.broadcasted_iota(jnp.int32, (2 * cap * n, tok_rows), 0)
    upper = jnp.where((number == rows[0]) | (number == rows[1]), 1.0, 0.0).astype(BF16)
    lower = jnp.where((number == rows[0] + cap) | (number == rows[1] + cap), 1.0, 0.0).astype(BF16)
    packed = jnp.dot(upper, tok_ref[:, :half], preferred_element_type=F32)
    packed = packed + jnp.dot(lower, tok_ref[:, half:], preferred_element_type=F32)
    for o in range(n):
        out_refs[o][...] = packed[o * 2 * cap : (o + 1) * 2 * cap].astype(BF16)


def gate_up_kernel(n, cap, piece, *refs):
    blocks, (wg_ref, wu_ref, out_ref, x_ref) = refs[:n], refs[n:]
    half = blocks[0].shape[1]
    for o in range(n):
        x_ref[pl.ds(o * cap, cap), :half] = blocks[o][:cap, :]
        x_ref[pl.ds(o * cap, cap), half:] = blocks[o][cap:, :]
    width = out_ref.shape[1] // 2
    tile = 512
    for which, w_ref in enumerate((wg_ref, wu_ref)):
        for j in range(width // tile):
            columns = pl.ds(piece * width + j * tile, tile)
            out_ref[:, pl.ds(which * width + j * tile, tile)] = jnp.dot(
                x_ref[...], w_ref[:, columns], preferred_element_type=F32
            ).astype(BF16)


def hidden_of(own_ref, other_ref):
    width = own_ref.shape[1] // 2
    gate = own_ref[:, :width].astype(F32) + other_ref[:, :width].astype(F32)
    up = own_ref[:, width:].astype(F32) + other_ref[:, width:].astype(F32)
    return (gate / (1.0 + jnp.exp(-gate)) * up).astype(BF16)


def down_first_kernel(own_ref, other_ref, wd_ref, acc_ref):
    hidden = hidden_of(own_ref, other_ref)
    acc_ref[...] = jnp.dot(hidden, wd_ref[: hidden.shape[1], :], preferred_element_type=F32)


def down_last_kernel(n, cap, own_ref, other_ref, wd_ref, acc_ref, *out_refs):
    hidden = hidden_of(own_ref, other_ref)
    depth = hidden.shape[1]
    out = acc_ref[...] + jnp.dot(hidden, wd_ref[depth:, :], preferred_element_type=F32)
    half = out.shape[1] // 2
    for o in range(n):
        out_refs[o][:cap, :] = out[o * cap : (o + 1) * cap, :half].astype(BF16)
        out_refs[o][cap:, :] = out[o * cap : (o + 1) * cap, half:].astype(BF16)


def combine_kernel(n, cap, me_ref, ids_ref, weights_ref, *refs):
    blocks, (out_ref, all_ref) = refs[:n], refs[n:]
    tok_rows, width = out_ref.shape
    half = width // 2
    for o in range(n):
        all_ref[pl.ds(o * 2 * cap, 2 * cap), :] = blocks[o][...]
    rows = slot_rows(ids_ref, me_ref[0], n, cap, tok_rows)
    number = lax.broadcasted_iota(jnp.int32, (2 * cap * n, tok_rows), 0)
    own = lax.broadcasted_iota(jnp.int32, (tok_rows, tok_rows), 0) == lax.broadcasted_iota(
        jnp.int32, (tok_rows, tok_rows), 1
    )
    weights = [
        jnp.sum(jnp.where(own, weights_ref[k : k + 1, :], 0.0), axis=1, keepdims=True)
        for k in range(2)
    ]
    for part in range(2):
        total = None
        for k in range(2):
            pick = jnp.where(number == rows[k] + part * cap, 1.0, 0.0).astype(BF16)
            picked = lax.dot_general(
                pick, all_ref[...], (((0,), (0,)), ((), ())), preferred_element_type=F32
            )
            term = weights[k] * picked
            total = term if total is None else total + term
        out_ref[:, part * half : (part + 1) * half] = total.astype(BF16)


def in_vmem(x):
    return pltpu.with_memory_space_constraint(x, pltpu.VMEM)


def resident(w, limit):
    return pl.pallas_call(
        lambda w_ref, out_ref: None,
        out_shape=pltpu.VMEM(w.shape, w.dtype),
        in_specs=[pl.BlockSpec(memory_space=pl.ANY)],
        out_specs=pl.BlockSpec(memory_space=pl.ANY),
        input_output_aliases={0: 0},
        compiler_params=pltpu.CompilerParams(vmem_limit_bytes=limit),
        name="weights_to_vmem",
    )(in_vmem(w))


def call(kernel, outs, args, smem=0, scratch=(), limit=20 << 20, cost=None, name=None, to_vmem=True):
    many = isinstance(outs, (tuple, list))
    shapes = [
        pltpu.VMEM(o.shape, o.dtype) if to_vmem else o for o in (outs if many else [outs])
    ]
    result = pl.pallas_call(
        kernel,
        out_shape=shapes,
        in_specs=[SMEM_SPEC] * smem + [VMEM_SPEC] * (len(args) - smem),
        out_specs=[VMEM_SPEC] * len(shapes),
        scratch_shapes=scratch,
        compiler_params=pltpu.CompilerParams(vmem_limit_bytes=limit),
        cost_estimate=cost,
        name=name,
    )(*args[:smem], *(in_vmem(a) for a in args[smem:]))
    return result if many else result[0]


def swap(x, axis, distance):
    return lax.ppermute(x, axis, [(i, i ^ distance) for i in range(lax.axis_size(axis))])


def one_expert_each(tokens, expert_ids, gate_weights, w_gate, w_up, w_down):
    tok_rows, width = tokens.shape
    n = lax.axis_size("expert")
    cap = capacity_of(tok_rows, expert_ids.shape[1], n)
    half, hidden_units = width // 2, w_gate.shape[1]
    me = lax.axis_index("expert").astype(jnp.int32).reshape(1)
    ids = expert_ids.T
    block = jax.ShapeDtypeStruct((2 * cap, half), BF16)

    sent = call(
        lambda *refs: dispatch_kernel(n, cap, *refs),
        [block] * n,
        [me, ids, tokens],
        smem=1,
        name="dispatch",
    )
    received = list(sent)
    for o in SEND_ORDER:
        received[o] = swap(sent[o], "expert", o)
    wg, wu, wd = (resident(w, 1 << 20) for w in (w_gate, w_up, w_down))

    piece_width = hidden_units // PIECES
    own, other = [], []
    for piece in range(PIECES):
        own.append(
            call(
                lambda *refs, piece=piece: gate_up_kernel(n, cap, piece, *refs),
                jax.ShapeDtypeStruct((n * cap, 2 * piece_width), BF16),
                [*received, wg, wu],
                scratch=[pltpu.VMEM((n * cap, width), BF16)],
                name="gate_up",
            )
        )
        other.append(swap(own[-1], "tensor", 1))
    acc = call(
        down_first_kernel,
        jax.ShapeDtypeStruct((n * cap, width), F32),
        [own[0], other[0], wd],
        name="down_first",
    )
    results = call(
        lambda *refs: down_last_kernel(n, cap, *refs),
        [block] * n,
        [own[1], other[1], wd, acc],
        name="down_last",
    )
    returned = list(results)
    for o in SEND_ORDER:
        returned[o] = swap(results[o], "expert", o)
    return call(
        lambda *refs: combine_kernel(n, cap, *refs),
        jax.ShapeDtypeStruct((tok_rows, width), BF16),
        [me, ids, gate_weights.T, *returned],
        smem=1,
        scratch=[pltpu.VMEM((2 * cap * n, half), BF16)],
        name="combine",
        to_vmem=False,
    )


def per_device(tokens, expert_ids, gate_weights, w_gate, w_up, w_down):
    args = (tokens, expert_ids, gate_weights, w_gate, w_up, w_down)
    whole = w_gate.shape[1] == FF and lax.axis_size("expert") == 8 and lax.axis_size("tensor") == 2
    if whole and expert_ids.shape[1] == 2:
        return one_expert_each(*args)
    return general(*args)


def solution(mesh):
    in_specs = (
        P(("group", "expert"), "tensor"),
        P(("group", "expert"), None),
        P(("group", "expert"), None),
        P("tensor", "expert"),
        P("tensor", "expert"),
        P("expert", "tensor"),
    )
    out_specs = P(("group", "expert"), "tensor")
    return jax.shard_map(
        per_device, mesh=mesh, in_specs=in_specs, out_specs=out_specs, check_vma=False
    )
```

time: 103 us -> 66.7 us (0.65)
  waiting for transfers between devices: 37.4 us -> 6.95 us
  blocking collectives: 25.3 us -> 0 us
  local copies, waits for them, and re-layouts: 2.49 us -> 27.7 us
  starting transfers between devices: 5.79 us -> 24.7 us
  matrix products: 17.2 us -> 0 us
  between operations: 13.5 us -> 0.13 us
  Pallas kernels: 0 us -> 6.81 us
  other arithmetic: 1.32 us -> 0.01 us
    unnamed x5 -> x25, local copies, waits for them, and re-layouts: 0.82 us -> 27.7 us
    all_to_all x1 -> x0, blocking collectives: 25.3 us -> none  [per_device(): lax.all_to_all(buffer, 'expert', split_axis=0, concat_axis=0, tiled=True)]
    ppermute x0 -> x16, starting transfers between devices: none -> 24.7 us  [swap(): lax.ppermute(x, axis, [(i, i ^ distance) for i in range(lax.axis_size(axi...]
    psum x1 -> x0, waiting for transfers between devices: 19 us -> none  [per_device(): up_full = lax.psum(up_part, 'tensor').astype(jnp.float32)]
    all_to_all x1 -> x0, waiting for transfers between devices: 18.3 us -> none  [per_device(): lax.all_to_all(results, 'expert', split_axis=0, concat_axis=0, tiled=True)]
    dot_general x5 -> x0, matrix products: 17.2 us -> none  [the longest x1 5.35 us: per_device(): jnp.dot(flat_rows, w_up, preferred_element_type=jnp.float32)]
    ppermute x0 -> x16, waiting for transfers between devices: none -> 6.95 us  [swap(): lax.ppermute(x, axis, [(i, i ^ distance) for i in range(lax.axis_size(axi...]
    pallas_call x0 -> x9, Pallas kernels: none -> 6.81 us  [the longest x6 6.81 us: call(): pl.pallas_call(kernel, out_shape=shapes, in_specs=[SMEM_SPEC] * smem + [V...]
  transfers between devices with their start and end apart: 2 -> 16, of which waited for: 2 -> 3; matrix products, arithmetic and copies ran while one was open for 0% -> 0% of each run, Pallas kernels for 0% -> 4%
where the time goes in v1:
time: 66.7 us; the launch traced here: 66.3 us
  local copies, waits for them, and re-layouts  27.7 us (42%)
  starting transfers between devices  24.7 us (37%)
  waiting for transfers between devices  6.95 us (10%)
  Pallas kernels  6.81 us (10%)
    unnamed x25, local copies, waits for them, and re-layouts  27.7 us
    ppermute x16, starting transfers between devices, swap(): lax.ppermute(x, axis, [(i, i ^ distance) for i in range(lax.axis_size(axi...  24.7 us
    ppermute x16, waiting for transfers between devices, swap(): lax.ppermute(x, axis, [(i, i ^ distance) for i in range(lax.axis_size(axi...  6.95 us
    pallas_call x6, Pallas kernels, call(): pl.pallas_call(kernel, out_shape=shapes, in_specs=[SMEM_SPEC] * smem + [V...  6.81 us
  transfers between devices with their start and end apart: 16, of which 3 were waited for; matrix products, arithmetic and copies ran while one was open for 0% of the time, Pallas kernels for 4%

profile of v1, /device:TPU:0, one launch (start us, length us, event | category | flops | bytes accessed | tf_op | source)
XLA Modules:
  0.0 66.3 jit_solution(8314178758348104282)
XLA Ops:
  0.0 0.0 copy-start.6
  0.0 7.6 %copy.16.w_ref = bf16[1792,2048]{1,0:T(8,128)(2,1)} copy(bf16[1792,2048]{1,0:T(8,128)(2,1)} %param.9) | data formatting | bytes 14680064
  7.6 0.0 copy-done.6
  7.6 3.0 %copy.17.w_ref = bf16[1792,2048]{1,0:T(8,128)(2,1)} copy(bf16[1792,2048]{1,0:T(8,128)(2,1)S(1)} %copy-done.6) | data formatting | bytes 14680064
  10.6 0.0 copy-start.3
  10.6 0.0 copy-start.4
  10.6 6.5 %copy.18.w_ref = bf16[2048,1792]{1,0:T(8,128)(2,1)} copy(bf16[2048,1792]{1,0:T(8,128)(2,1)} %param.11) | data formatting | bytes 14680064
  17.1 0.0 copy-done.3
  17.1 0.0 copy-done.4
  17.1 0.6 dispatch.1
  17.7 3.0 %collective-permute-start = (bf16[40,896]{1,0:T(8,128)(2,1)S(1)}, bf16[40,896]{1,0:T(8,128)(2,1)S(1)}, u32[]{:S(2)}, u32[]{:S(2)}) collective-permute-start(bf16[40,896]{1,0:T(8,128)(2,1)S(1)} %get-tuple-element.22), channel_id=1, source_target_pairs={{0,2},{2,0},{4,6},{6,4},{8,10},{10,8},{12,14},{14,12},{1,3},{3,1},... | collective-permute-start | bytes 215048 | tf_op jit(solution)/shard_map/ppermute | solution.py:204
  20.7 1.6 %collective-permute-start.1 = (bf16[40,896]{1,0:T(8,128)(2,1)S(1)}, bf16[40,896]{1,0:T(8,128)(2,1)S(1)}, u32[]{:S(2)}, u32[]{:S(2)}) collective-permute-start(bf16[40,896]{1,0:T(8,128)(2,1)S(1)} %get-tuple-element.23), channel_id=1, source_target_pairs={{0,4},{2,6},{4,0},{6,2},{8,12},{10,14},{12,8},{14,10},{1,5},{3,7},... | collective-permute-start | bytes 215048 | tf_op jit(solution)/shard_map/ppermute | solution.py:204
  22.3 0.0 collective-permute-start.2
  22.3 3.0 %collective-permute-start.3 = (bf16[40,896]{1,0:T(8,128)(2,1)S(1)}, bf16[40,896]{1,0:T(8,128)(2,1)S(1)}, u32[]{:S(2)}, u32[]{:S(2)}) collective-permute-start(bf16[40,896]{1,0:T(8,128)(2,1)S(1)} %get-tuple-element.25), channel_id=1, source_target_pairs={{0,8},{2,10},{4,12},{6,14},{8,0},{10,2},{12,4},{14,6},{1,9},{3,11}... | collective-permute-start | bytes 215048 | tf_op jit(solution)/shard_map/ppermute | solution.py:204
  25.3 1.3 %collective-permute-start.4 = (bf16[40,896]{1,0:T(8,128)(2,1)S(1)}, bf16[40,896]{1,0:T(8,128)(2,1)S(1)}, u32[]{:S(2)}, u32[]{:S(2)}) collective-permute-start(bf16[40,896]{1,0:T(8,128)(2,1)S(1)} %get-tuple-element.26), channel_id=1, source_target_pairs={{0,10},{2,8},{4,14},{6,12},{8,2},{10,0},{12,6},{14,4},{1,11},{3,9}... | collective-permute-start | bytes 215048 | tf_op jit(solution)/shard_map/ppermute | solution.py:204
  26.6 0.0 collective-permute-done.refs_1_
  26.6 3.6 %collective-permute-start.5 = (bf16[40,896]{1,0:T(8,128)(2,1)S(1)}, bf16[40,896]{1,0:T(8,128)(2,1)S(1)}, u32[]{:S(2)}, u32[]{:S(2)}) collective-permute-start(bf16[40,896]{1,0:T(8,128)(2,1)S(1)} %get-tuple-element.27), channel_id=1, source_target_pairs={{0,12},{2,14},{4,8},{6,10},{8,4},{10,6},{12,0},{14,2},{1,13},{3,15... | collective-permute-start | bytes 215048 | tf_op jit(solution)/shard_map/ppermute | solution.py:204
  30.2 0.0 collective-permute-done.1.refs_2_
  30.2 0.0 slice-start
  30.2 0.0 slice-start.1
  30.2 0.1 collective-permute-start.6
  30.2 0.0 copy-start
  30.2 3.2 %copy-done = bf16[1792,2048]{1,0:T(8,128)(2,1)S(1)} copy-done((bf16[1792,2048]{1,0:T(8,128)(2,1)S(1)}, bf16[1792,2048]{1,0:T(8,128)(2,1)}, u32[]{:S(2)}) %copy-start) | copy-done | bytes 7340056
  33.5 0.0 copy-start.1
  33.5 3.6 %copy-done.1 = bf16[1792,2048]{1,0:T(8,128)(2,1)} copy-done((bf16[1792,2048]{1,0:T(8,128)(2,1)}, bf16[1792,2048]{1,0:T(8,128)(2,1)S(1)}, u32[]{:S(2)}) %copy-start.1) | copy-done | bytes 7340056
  37.1 0.0 slice-done
  37.1 0.7 %slice-done.1 = s8[3145728]{0:T(1024)(128)(4,1)S(1)} async-done(((s8[7340032]{0:T(1024)(128)(4,1)}), s8[3145728]{0:T(1024)(128)(4,1)S(1)}, s32[]{:S(2)}) %slice-start.1) | async-done | bytes 3145752
  37.8 0.0 collective-permute-done.2.refs_3_
  37.8 0.0 collective-permute-done.3.refs_4_
  37.8 0.0 collective-permute-done.4.refs_5_
  37.8 0.0 collective-permute-done.5.refs_6_
  37.8 0.0 collective-permute-done.6.refs_7_
  37.8 0.0 copy-start.2
  37.8 3.1 %copy-done.2 = bf16[1792,2048]{1,0:T(8,128)(2,1)S(1)} copy-done((bf16[1792,2048]{1,0:T(8,128)(2,1)S(1)}, bf16[1792,2048]{1,0:T(8,128)(2,1)}, u32[]{:S(2)}) %copy-start.2) | copy-done | bytes 7340056
  40.9 0.0 slice-start.2
  40.9 1.4 %gate_up.3.own_ref = bf16[160,2048]{1,0:T(8,128)(2,1)S(1)} custom-call(bf16[40,896]{1,0:T(8,128)(2,1)S(1)} %get-tuple-element.21.refs_0_, bf16[40,896]{1,0:T(8,128)(2,1)S(1)} %collective-permute-done.refs_1_, bf16[40,896]{1,0:T(8,128)(2,1)S(1)} %collective-permute-done.1.refs_2_, bf16[40,896]{1,0:T(8,128)(2,1)S(1)} %collective-permute-done.2.refs_3_, ...), custom_call_target="tpu_custom_call" | custom-call | tf_op jit(solution)/shard_map/gate_up/pallas_call | solution.py:190
  42.3 0.0 slice-start.3
  42.3 0.1 collective-permute-start.8
  42.4 1.4 %gate_up.2.refs_0_ = bf16[160,2048]{1,0:T(8,128)(2,1)S(1)} custom-call(bf16[40,896]{1,0:T(8,128)(2,1)S(1)} %get-tuple-element.21.refs_0_, bf16[40,896]{1,0:T(8,128)(2,1)S(1)} %collective-permute-done.refs_1_, bf16[40,896]{1,0:T(8,128)(2,1)S(1)} %collective-permute-done.1.refs_2_, bf16[40,896]{1,0:T(8,128)(2,1)S(1)} %collective-permute-done.2.refs_3_, ...), custom_call_target="tpu_custom_call" | custom-call | tf_op jit(solution)/shard_map/gate_up/pallas_call | solution.py:190
  43.8 0.6 collective-permute-start.7
  44.4 0.0 slice-done.2
  44.4 0.0 slice-done.3
  44.4 0.1 collective-permute-done.8.other_ref
  44.5 1.0 %down_first.1.refs_3_ = f32[160,1792]{1,0:T(8,128)S(1)} custom-call(bf16[160,2048]{1,0:T(8,128)(2,1)S(1)} %gate_up.3.own_ref, bf16[160,2048]{1,0:T(8,128)(2,1)S(1)} %collective-permute-done.8.other_ref, bf16[2048,1792]{1,0:T(8,128)(2,1)S(1)} %weights_to_vmem.5.wd_ref.refs_2_), custom_call_target="tpu_custom_call" | custom-call | tf_op jit(solution)/shard_map/down_first/pallas_call | solution.py:190
  45.4 0.0 copy-start.5
  45.5 0.7 collective-permute-done.7.refs_1_
  46.1 1.0 %down_last.1 = (bf16[40,896]{1,0:T(8,128)(2,1)S(1)}, bf16[40,896]{1,0:T(8,128)(2,1)S(1)}, bf16[40,896]{1,0:T(8,128)(2,1)S(1)}, bf16[40,896]{1,0:T(8,128)(2,1)S(1...) custom-call(bf16[160,2048]{1,0:T(8,128)(2,1)S(1)} %gate_up.2.refs_0_, ...), custom_call_target="tpu_custom_call" | custom-call | tf_op jit(solution)/shard_map/down_last/pallas_call | solution.py:190
  47.1 0.8 %collective-permute-start.9 = (bf16[40,896]{1,0:T(8,128)(2,1)S(1)}, bf16[40,896]{1,0:T(8,128)(2,1)S(1)}, u32[]{:S(2)}, u32[]{:S(2)}) collective-permute-start(bf16[40,896]{1,0:T(8,128)(2,1)S(1)} %get-tuple-element.30), channel_id=1, source_target_pairs={{0,2},{2,0},{4,6},{6,4},{8,10},{10,8},{12,14},{14,12},{1,3},{3,1},... | collective-permute-start | bytes 215048 | tf_op jit(solution)/shard_map/ppermute | solution.py:204
  47.9 2.2 %collective-permute-start.10 = (bf16[40,896]{1,0:T(8,128)(2,1)S(1)}, bf16[40,896]{1,0:T(8,128)(2,1)S(1)}, u32[]{:S(2)}, u32[]{:S(2)}) collective-permute-start(bf16[40,896]{1,0:T(8,128)(2,1)S(1)} %get-tuple-element.31), channel_id=1, source_target_pairs={{0,4},{2,6},{4,0},{6,2},{8,12},{10,14},{12,8},{14,10},{1,5},{3,7},... | collective-permute-start | bytes 215048 | tf_op jit(solution)/shard_map/ppermute | solution.py:204
  50.1 0.7 collective-permute-start.11
  50.8 3.1 %collective-permute-start.12 = (bf16[40,896]{1,0:T(8,128)(2,1)S(1)}, bf16[40,896]{1,0:T(8,128)(2,1)S(1)}, u32[]{:S(2)}, u32[]{:S(2)}) collective-permute-start(bf16[40,896]{1,0:T(8,128)(2,1)S(1)} %get-tuple-element.33), channel_id=1, source_target_pairs={{0,8},{2,10},{4,12},{6,14},{8,0},{10,2},{12,4},{14,6},{1,9},{3,11}... | collective-permute-start | bytes 215048 | tf_op jit(solution)/shard_map/ppermute | solution.py:204
  53.9 0.0 collective-permute-start.13
  54.0 0.0 collective-permute-done.9.refs_4_
  54.0 2.9 %collective-permute-start.14 = (bf16[40,896]{1,0:T(8,128)(2,1)S(1)}, bf16[40,896]{1,0:T(8,128)(2,1)S(1)}, u32[]{:S(2)}, u32[]{:S(2)}) collective-permute-start(bf16[40,896]{1,0:T(8,128)(2,1)S(1)} %get-tuple-element.35), channel_id=1, source_target_pairs={{0,12},{2,14},{4,8},{6,10},{8,4},{10,6},{12,0},{14,2},{1,13},{3,15... | collective-permute-start | bytes 215048 | tf_op jit(solution)/shard_map/ppermute | solution.py:204
  56.8 0.0 collective-permute-done.10.refs_5_
  56.8 1.8 %collective-permute-start.15 = (bf16[40,896]{1,0:T(8,128)(2,1)S(1)}, bf16[40,896]{1,0:T(8,128)(2,1)S(1)}, u32[]{:S(2)}, u32[]{:S(2)}) collective-permute-start(bf16[40,896]{1,0:T(8,128)(2,1)S(1)} %get-tuple-element.36), channel_id=1, source_target_pairs={{0,14},{2,12},{4,10},{6,8},{8,6},{10,4},{12,2},{14,0},{1,15},{3,13... | collective-permute-start | bytes 215048 | tf_op jit(solution)/shard_map/ppermute | solution.py:204
  58.7 0.0 collective-permute-done.11.refs_6_
  58.7 0.0 collective-permute-done.12.refs_7_
  58.7 6.2 %collective-permute-done.13.refs_8_ = bf16[40,896]{1,0:T(8,128)(2,1)S(1)} collective-permute-done((bf16[40,896]{1,0:T(8,128)(2,1)S(1)}, bf16[40,896]{1,0:T(8,128)(2,1)S(1)}, u32[]{:S(2)}, u32[]{:S(2)}) %collective-permute-start.13) | collective-permute-done | bytes 71712 | tf_op jit(solution)/shard_map/ppermute | solution.py:204
  64.8 0.0 collective-permute-done.14.refs_9_
  64.8 0.0 collective-permute-done.15.refs_10_
  64.8 0.0 copy-done.5
  64.9 1.4 %combine.1 = bf16[64,1792]{1,0:T(8,128)(2,1)} custom-call(s32[1]{0:T(128)} %bitcast.refs_0_, s32[2,64]{1,0:T(2,128)S(1)} %bitcast.8, f32[2,64]{1,0:T(2,128)S(1)} %bitcast.9, bf16[40,896]{1,0:T(8,128)(2,1)S(1)} %get-tuple-element.29.refs_3_, bf16[40,896]{1,0:T(8,128)(2,1)S(1)} %collective-permute-done.9.refs_4_, ...), custom_call_target="tpu_custom_call" | custom-call | tf_op jit(solution)/shard_map/combine/pallas_call | solution.py:190
  (5 shorter events, 0.0 us)
Async XLA Ops:
  0.0 7.6 %copy-start.6 = (bf16[1792,2048]{1,0:T(8,128)(2,1)S(1)}, bf16[1792,2048]{1,0:T(8,128)(2,1)}, u32[]{:S(2)}) copy-start(bf16[1792,2048]{1,0:T(8,128)(2,1)} %param.10) | copy-start | bytes 22020100
  10.6 6.5 %copy-start.3 = (bf16[64,1792]{1,0:T(8,128)(2,1)S(1)}, bf16[64,1792]{1,0:T(8,128)(2,1)}, u32[]{:S(2)}) copy-start(bf16[64,1792]{1,0:T(8,128)(2,1)} %refs_2_.1) | copy-start | bytes 688132
  10.6 6.5 %copy-start.4 = (s32[64,2]{0,1:T(2,128)S(1)}, s32[64,2]{0,1:T(2,128)}, u32[]{:S(2)}) copy-start(s32[64,2]{0,1:T(2,128)} %param.7) | copy-start | bytes 1540
  17.7 8.9 %collective-permute-start = (bf16[40,896]{1,0:T(8,128)(2,1)S(1)}, bf16[40,896]{1,0:T(8,128)(2,1)S(1)}, u32[]{:S(2)}, u32[]{:S(2)}) collective-permute-start(bf16[40,896]{1,0:T(8,128)(2,1)S(1)} %get-tuple-element.22), channel_id=1, source_target_pairs={{0,2},{2,0},{4,6},{6,4},{8,10},{10,8},{12,14},{14,12},{1,3},{3,1},... | collective-permute-start | bytes 215048 | tf_op jit(solution)/shard_map/ppermute | solution.py:204
  20.7 9.5 %collective-permute-start.1 = (bf16[40,896]{1,0:T(8,128)(2,1)S(1)}, bf16[40,896]{1,0:T(8,128)(2,1)S(1)}, u32[]{:S(2)}, u32[]{:S(2)}) collective-permute-start(bf16[40,896]{1,0:T(8,128)(2,1)S(1)} %get-tuple-element.23), channel_id=1, source_target_pairs={{0,4},{2,6},{4,0},{6,2},{8,12},{10,14},{12,8},{14,10},{1,5},{3,7},... | collective-permute-start | bytes 215048 | tf_op jit(solution)/shard_map/ppermute | solution.py:204
  22.3 15.5 %collective-permute-start.2 = (bf16[40,896]{1,0:T(8,128)(2,1)S(1)}, bf16[40,896]{1,0:T(8,128)(2,1)S(1)}, u32[]{:S(2)}, u32[]{:S(2)}) collective-permute-start(bf16[40,896]{1,0:T(8,128)(2,1)S(1)} %get-tuple-element.24), channel_id=1, source_target_pairs={{0,6},{2,4},{4,2},{6,0},{8,14},{10,12},{12,10},{14,8},{1,7},{3,5},... | collective-permute-start | bytes 215048 | tf_op jit(solution)/shard_map/ppermute | solution.py:204
  22.3 15.5 %collective-permute-start.3 = (bf16[40,896]{1,0:T(8,128)(2,1)S(1)}, bf16[40,896]{1,0:T(8,128)(2,1)S(1)}, u32[]{:S(2)}, u32[]{:S(2)}) collective-permute-start(bf16[40,896]{1,0:T(8,128)(2,1)S(1)} %get-tuple-element.25), channel_id=1, source_target_pairs={{0,8},{2,10},{4,12},{6,14},{8,0},{10,2},{12,4},{14,6},{1,9},{3,11}... | collective-permute-start | bytes 215048 | tf_op jit(solution)/shard_map/ppermute | solution.py:204
  25.3 12.5 %collective-permute-start.4 = (bf16[40,896]{1,0:T(8,128)(2,1)S(1)}, bf16[40,896]{1,0:T(8,128)(2,1)S(1)}, u32[]{:S(2)}, u32[]{:S(2)}) collective-permute-start(bf16[40,896]{1,0:T(8,128)(2,1)S(1)} %get-tuple-element.26), channel_id=1, source_target_pairs={{0,10},{2,8},{4,14},{6,12},{8,2},{10,0},{12,6},{14,4},{1,11},{3,9}... | collective-permute-start | bytes 215048 | tf_op jit(solution)/shard_map/ppermute | solution.py:204
  26.6 11.2 %collective-permute-start.5 = (bf16[40,896]{1,0:T(8,128)(2,1)S(1)}, bf16[40,896]{1,0:T(8,128)(2,1)S(1)}, u32[]{:S(2)}, u32[]{:S(2)}) collective-permute-start(bf16[40,896]{1,0:T(8,128)(2,1)S(1)} %get-tuple-element.27), channel_id=1, source_target_pairs={{0,12},{2,14},{4,8},{6,10},{8,4},{10,6},{12,0},{14,2},{1,13},{3,15... | collective-permute-start | bytes 215048 | tf_op jit(solution)/shard_map/ppermute | solution.py:204
  30.2 6.9 %slice-start = ((s8[7340032]{0:T(1024)(128)(4,1)}), s8[4194304]{0:T(1024)(128)(4,1)S(1)}, s32[]{:S(2)}) async-start(s8[7340032]{0:T(1024)(128)(4,1)} %bitcast.3), calls=%async_computation | async-start | bytes 8388608
  30.2 7.6 %slice-start.1 = ((s8[7340032]{0:T(1024)(128)(4,1)}), s8[3145728]{0:T(1024)(128)(4,1)S(1)}, s32[]{:S(2)}) async-start(s8[7340032]{0:T(1024)(128)(4,1)} %bitcast.3), calls=%async_computation.1 | async-start | bytes 6291456
  30.2 7.6 %collective-permute-start.6 = (bf16[40,896]{1,0:T(8,128)(2,1)S(1)}, bf16[40,896]{1,0:T(8,128)(2,1)S(1)}, u32[]{:S(2)}, u32[]{:S(2)}) collective-permute-start(bf16[40,896]{1,0:T(8,128)(2,1)S(1)} %get-tuple-element.28), channel_id=1, source_target_pairs={{0,14},{2,12},{4,10},{6,8},{8,6},{10,4},{12,2},{14,0},{1,15},{3,13... | collective-permute-start | bytes 215048 | tf_op jit(solution)/shard_map/ppermute | solution.py:204
  30.2 3.2 %copy-start = (bf16[1792,2048]{1,0:T(8,128)(2,1)S(1)}, bf16[1792,2048]{1,0:T(8,128)(2,1)}, u32[]{:S(2)}) copy-start(bf16[1792,2048]{1,0:T(8,128)(2,1)} %copy.16.w_ref) | copy-start | bytes 22020100
  33.5 3.6 %copy-start.1 = (bf16[1792,2048]{1,0:T(8,128)(2,1)}, bf16[1792,2048]{1,0:T(8,128)(2,1)S(1)}, u32[]{:S(2)}) copy-start(bf16[1792,2048]{1,0:T(8,128)(2,1)S(1)} %weights_to_vmem.3.refs_8_) | copy-start | bytes 22020100
  37.8 3.1 %copy-start.2 = (bf16[1792,2048]{1,0:T(8,128)(2,1)S(1)}, bf16[1792,2048]{1,0:T(8,128)(2,1)}, u32[]{:S(2)}) copy-start(bf16[1792,2048]{1,0:T(8,128)(2,1)} %copy-done.1) | copy-start | bytes 22020100
  40.9 3.5 %slice-start.2 = ((s8[7340032]{0:T(1024)(128)(4,1)}), s8[4194304]{0:T(1024)(128)(4,1)S(1)}, s32[]{:S(2)}) async-start(s8[7340032]{0:T(1024)(128)(4,1)} %bitcast.5), calls=%async_computation.2 | async-start | bytes 8388608
  42.3 2.1 %slice-start.3 = ((s8[7340032]{0:T(1024)(128)(4,1)}), s8[3145728]{0:T(1024)(128)(4,1)S(1)}, s32[]{:S(2)}) async-start(s8[7340032]{0:T(1024)(128)(4,1)} %bitcast.5), calls=%async_computation.3 | async-start | bytes 6291456
  42.3 2.2 %collective-permute-start.8 = (bf16[160,2048]{1,0:T(8,128)(2,1)S(1)}, bf16[160,2048]{1,0:T(8,128)(2,1)S(1)}, u32[]{:S(2)}, u32[]{:S(2)}) collective-permute-start(bf16[160,2048]{1,0:T(8,128)(2,1)S(1)} %gate_up.3.own_ref), channel_id=1, source_target_pairs={{0,1},{1,0},{2,3},{3,2},{4,5},{5,4},{6,7},{7,6},{8,9},{9,8},{10,11... | collective-permute-start | bytes 1966088 | tf_op jit(solution)/shard_map/ppermute | solution.py:204
  43.8 2.3 %collective-permute-start.7 = (bf16[160,2048]{1,0:T(8,128)(2,1)S(1)}, bf16[160,2048]{1,0:T(8,128)(2,1)S(1)}, u32[]{:S(2)}, u32[]{:S(2)}) collective-permute-start(bf16[160,2048]{1,0:T(8,128)(2,1)S(1)} %gate_up.2.refs_0_), channel_id=1, source_target_pairs={{0,1},{1,0},{2,3},{3,2},{4,5},{5,4},{6,7},{7,6},{8,9},{9,8},{10,11... | collective-permute-start | bytes 1966088 | tf_op jit(solution)/shard_map/ppermute | solution.py:204
  45.4 19.4 %copy-start.5 = (f32[64,2]{0,1:T(2,128)S(1)}, f32[64,2]{0,1:T(2,128)}, u32[]{:S(2)}) copy-start(f32[64,2]{0,1:T(2,128)} %param.8) | copy-start | bytes 1540
  47.1 6.8 %collective-permute-start.9 = (bf16[40,896]{1,0:T(8,128)(2,1)S(1)}, bf16[40,896]{1,0:T(8,128)(2,1)S(1)}, u32[]{:S(2)}, u32[]{:S(2)}) collective-permute-start(bf16[40,896]{1,0:T(8,128)(2,1)S(1)} %get-tuple-element.30), channel_id=1, source_target_pairs={{0,2},{2,0},{4,6},{6,4},{8,10},{10,8},{12,14},{14,12},{1,3},{3,1},... | collective-permute-start | bytes 215048 | tf_op jit(solution)/shard_map/ppermute | solution.py:204
  47.9 8.9 %collective-permute-start.10 = (bf16[40,896]{1,0:T(8,128)(2,1)S(1)}, bf16[40,896]{1,0:T(8,128)(2,1)S(1)}, u32[]{:S(2)}, u32[]{:S(2)}) collective-permute-start(bf16[40,896]{1,0:T(8,128)(2,1)S(1)} %get-tuple-element.31), channel_id=1, source_target_pairs={{0,4},{2,6},{4,0},{6,2},{8,12},{10,14},{12,8},{14,10},{1,5},{3,7},... | collective-permute-start | bytes 215048 | tf_op jit(solution)/shard_map/ppermute | solution.py:204
  50.1 8.5 %collective-permute-start.11 = (bf16[40,896]{1,0:T(8,128)(2,1)S(1)}, bf16[40,896]{1,0:T(8,128)(2,1)S(1)}, u32[]{:S(2)}, u32[]{:S(2)}) collective-permute-start(bf16[40,896]{1,0:T(8,128)(2,1)S(1)} %get-tuple-element.32), channel_id=1, source_target_pairs={{0,6},{2,4},{4,2},{6,0},{8,14},{10,12},{12,10},{14,8},{1,7},{3,5},... | collective-permute-start | bytes 215048 | tf_op jit(solution)/shard_map/ppermute | solution.py:204
  50.8 7.9 %collective-permute-start.12 = (bf16[40,896]{1,0:T(8,128)(2,1)S(1)}, bf16[40,896]{1,0:T(8,128)(2,1)S(1)}, u32[]{:S(2)}, u32[]{:S(2)}) collective-permute-start(bf16[40,896]{1,0:T(8,128)(2,1)S(1)} %get-tuple-element.33), channel_id=1, source_target_pairs={{0,8},{2,10},{4,12},{6,14},{8,0},{10,2},{12,4},{14,6},{1,9},{3,11}... | collective-permute-start | bytes 215048 | tf_op jit(solution)/shard_map/ppermute | solution.py:204
  53.9 10.9 %collective-permute-start.13 = (bf16[40,896]{1,0:T(8,128)(2,1)S(1)}, bf16[40,896]{1,0:T(8,128)(2,1)S(1)}, u32[]{:S(2)}, u32[]{:S(2)}) collective-permute-start(bf16[40,896]{1,0:T(8,128)(2,1)S(1)} %get-tuple-element.34), channel_id=1, source_target_pairs={{0,10},{2,8},{4,14},{6,12},{8,2},{10,0},{12,6},{14,4},{1,11},{3,9}... | collective-permute-start | bytes 215048 | tf_op jit(solution)/shard_map/ppermute | solution.py:204
  54.0 10.9 %collective-permute-start.14 = (bf16[40,896]{1,0:T(8,128)(2,1)S(1)}, bf16[40,896]{1,0:T(8,128)(2,1)S(1)}, u32[]{:S(2)}, u32[]{:S(2)}) collective-permute-start(bf16[40,896]{1,0:T(8,128)(2,1)S(1)} %get-tuple-element.35), channel_id=1, source_target_pairs={{0,12},{2,14},{4,8},{6,10},{8,4},{10,6},{12,0},{14,2},{1,13},{3,15... | collective-permute-start | bytes 215048 | tf_op jit(solution)/shard_map/ppermute | solution.py:204
  56.8 8.0 %collective-permute-start.15 = (bf16[40,896]{1,0:T(8,128)(2,1)S(1)}, bf16[40,896]{1,0:T(8,128)(2,1)S(1)}, u32[]{:S(2)}, u32[]{:S(2)}) collective-permute-start(bf16[40,896]{1,0:T(8,128)(2,1)S(1)} %get-tuple-element.36), channel_id=1, source_target_pairs={{0,14},{2,12},{4,10},{6,8},{8,6},{10,4},{12,2},{14,0},{1,15},{3,13... | collective-permute-start | bytes 215048 | tf_op jit(solution)/shard_map/ppermute | solution.py:204

commit v2 on v1

--- a/solution.py
+++ b/solution.py
@@ -11,7 +11,7 @@
 VMEM_SPEC = pl.BlockSpec(memory_space=pltpu.VMEM)
 SMEM_SPEC = pl.BlockSpec(memory_space=pltpu.SMEM)
 PIECES = 2
-SEND_ORDER = (7, 6, 5, 4, 3, 2, 1)
+ORDER = (7, 6, 5, 4, 3, 2, 1, 0)
 
 
 def pair_slots(id_blocks, expert_count):
@@ -97,16 +97,16 @@
     lower = jnp.where((number == rows[0] + cap) | (number == rows[1] + cap), 1.0, 0.0).astype(BF16)
     packed = jnp.dot(upper, tok_ref[:, :half], preferred_element_type=F32)
     packed = packed + jnp.dot(lower, tok_ref[:, half:], preferred_element_type=F32)
-    for o in range(n):
-        out_refs[o][...] = packed[o * 2 * cap : (o + 1) * 2 * cap].astype(BF16)
+    for o, out_ref in zip(ORDER, out_refs):
+        out_ref[...] = packed[o * 2 * cap : (o + 1) * 2 * cap].astype(BF16)
 
 
 def gate_up_kernel(n, cap, piece, *refs):
     blocks, (wg_ref, wu_ref, out_ref, x_ref) = refs[:n], refs[n:]
     half = blocks[0].shape[1]
-    for o in range(n):
-        x_ref[pl.ds(o * cap, cap), :half] = blocks[o][:cap, :]
-        x_ref[pl.ds(o * cap, cap), half:] = blocks[o][cap:, :]
+    for o, block in zip(ORDER, blocks):
+        x_ref[pl.ds(o * cap, cap), :half] = block[:cap, :]
+        x_ref[pl.ds(o * cap, cap), half:] = block[cap:, :]
     width = out_ref.shape[1] // 2
     tile = 512
     for which, w_ref in enumerate((wg_ref, wu_ref)):
@@ -134,17 +134,17 @@
     depth = hidden.shape[1]
     out = acc_ref[...] + jnp.dot(hidden, wd_ref[depth:, :], preferred_element_type=F32)
     half = out.shape[1] // 2
-    for o in range(n):
-        out_refs[o][:cap, :] = out[o * cap : (o + 1) * cap, :half].astype(BF16)
-        out_refs[o][cap:, :] = out[o * cap : (o + 1) * cap, half:].astype(BF16)
+    for o, out_ref in zip(ORDER, out_refs):
+        out_ref[:cap, :] = out[o * cap : (o + 1) * cap, :half].astype(BF16)
+        out_ref[cap:, :] = out[o * cap : (o + 1) * cap, half:].astype(BF16)
 
 
 def combine_kernel(n, cap, me_ref, ids_ref, weights_ref, *refs):
     blocks, (out_ref, all_ref) = refs[:n], refs[n:]
     tok_rows, width = out_ref.shape
     half = width // 2
-    for o in range(n):
-        all_ref[pl.ds(o * 2 * cap, 2 * cap), :] = blocks[o][...]
+    for o, block in zip(ORDER, blocks):
+        all_ref[pl.ds(o * 2 * cap, 2 * cap), :] = block[...]
     rows = slot_rows(ids_ref, me_ref[0], n, cap, tok_rows)
     number = lax.broadcasted_iota(jnp.int32, (2 * cap * n, tok_rows), 0)
     own = lax.broadcasted_iota(jnp.int32, (tok_rows, tok_rows), 0) == lax.broadcasted_iota(
@@ -168,18 +168,6 @@
 
 def in_vmem(x):
     return pltpu.with_memory_space_constraint(x, pltpu.VMEM)
-
-
-def resident(w, limit):
-    return pl.pallas_call(
-        lambda w_ref, out_ref: None,
-        out_shape=pltpu.VMEM(w.shape, w.dtype),
-        in_specs=[pl.BlockSpec(memory_space=pl.ANY)],
-        out_specs=pl.BlockSpec(memory_space=pl.ANY),
-        input_output_aliases={0: 0},
-        compiler_params=pltpu.CompilerParams(vmem_limit_bytes=limit),
-        name="weights_to_vmem",
-    )(in_vmem(w))
 
 
 def call(kernel, outs, args, smem=0, scratch=(), limit=20 << 20, cost=None, name=None, to_vmem=True):
@@ -201,6 +189,8 @@
 
 
 def swap(x, axis, distance):
+    if distance == 0:
+        return x
     return lax.ppermute(x, axis, [(i, i ^ distance) for i in range(lax.axis_size(axis))])
 
 
@@ -211,6 +201,7 @@
     half, hidden_units = width // 2, w_gate.shape[1]
     me = lax.axis_index("expert").astype(jnp.int32).reshape(1)
     ids = expert_ids.T
+    loaded = sum(w.size * 2 for w in (w_gate, w_up, w_down))
     block = jax.ShapeDtypeStruct((2 * cap, half), BF16)
 
     sent = call(
@@ -218,12 +209,10 @@
         [block] * n,
         [me, ids, tokens],
         smem=1,
+        cost=pl.CostEstimate(flops=20_000_000_000, bytes_accessed=2 * loaded, transcendentals=0),
         name="dispatch",
     )
-    received = list(sent)
-    for o in SEND_ORDER:
-        received[o] = swap(sent[o], "expert", o)
-    wg, wu, wd = (resident(w, 1 << 20) for w in (w_gate, w_up, w_down))
+    received = [swap(x, "expert", o) for o, x in zip(ORDER, sent)]
 
     piece_width = hidden_units // PIECES
     own, other = [], []
@@ -232,7 +221,7 @@
             call(
                 lambda *refs, piece=piece: gate_up_kernel(n, cap, piece, *refs),
                 jax.ShapeDtypeStruct((n * cap, 2 * piece_width), BF16),
-                [*received, wg, wu],
+                [*received, w_gate, w_up],
                 scratch=[pltpu.VMEM((n * cap, width), BF16)],
                 name="gate_up",
             )
@@ -241,18 +230,16 @@
     acc = call(
         down_first_kernel,
         jax.ShapeDtypeStruct((n * cap, width), F32),
-        [own[0], other[0], wd],
+        [own[0], other[0], w_down],
         name="down_first",
     )
     results = call(
         lambda *refs: down_last_kernel(n, cap, *refs),
         [block] * n,
-        [own[1], other[1], wd, acc],
+        [own[1], other[1], w_down, acc],
         name="down_last",
     )
-    returned = list(results)
-    for o in SEND_ORDER:
-        returned[o] = swap(results[o], "expert", o)
+    returned = [swap(x, "expert", o) for o, x in zip(ORDER, results)]
     return call(
         lambda *refs: combine_kernel(n, cap, *refs),
         jax.ShapeDtypeStruct((tok_rows, width), BF16),

time: 66.7 us -> 48.3 us (0.72)
  local copies, waits for them, and re-layouts: 27.7 us -> 1.65 us
  starting transfers between devices: 24.7 us -> 29 us
  waiting for transfers between devices: 6.95 us -> 10.7 us
    unnamed x25 -> x16, local copies, waits for them, and re-layouts: 27.7 us -> 1.65 us
    ppermute x16, starting transfers between devices: 24.7 us -> 29 us  [swap(): lax.ppermute(x, axis, [(i, i ^ distance) for i in range(lax.axis_size(axi...]
    ppermute x16, waiting for transfers between devices: 6.95 us -> 10.7 us  [swap(): lax.ppermute(x, axis, [(i, i ^ distance) for i in range(lax.axis_size(axi...]
  transfers between devices with their start and end apart: 16 -> 16, of which waited for: 3 -> 6; matrix products, arithmetic and copies ran while one was open for 0% -> 0% of each run, Pallas kernels for 4% -> 5%
where the time goes in v2:
time: 48.3 us; the launch traced here: 48.2 us
  starting transfers between devices  29 us (60%)
  waiting for transfers between devices  10.7 us (22%)
  Pallas kernels  6.65 us (14%)
  local copies, waits for them, and re-layouts  1.65 us (3%)
    ppermute x16, starting transfers between devices, swap(): lax.ppermute(x, axis, [(i, i ^ distance) for i in range(lax.axis_size(axi...  29 us
    ppermute x16, waiting for transfers between devices, swap(): lax.ppermute(x, axis, [(i, i ^ distance) for i in range(lax.axis_size(axi...  10.7 us
    pallas_call x6, Pallas kernels, call(): pl.pallas_call(kernel, out_shape=shapes, in_specs=[SMEM_SPEC] * smem + [V...  6.65 us
    unnamed x16, local copies, waits for them, and re-layouts  1.65 us
  transfers between devices with their start and end apart: 16, of which 6 were waited for; matrix products, arithmetic and copies ran while one was open for 0% of the time, Pallas kernels for 5%

profile of v2, /device:TPU:0, one launch (start us, length us, event | category | flops | bytes accessed | tf_op | source)
XLA Modules:
  0.0 48.2 jit_solution(15965024873813016628)
XLA Ops:
  0.0 0.0 copy-start.2
  0.0 0.7 %copy-done.2 = s32[64,2]{0,1:T(2,128)S(1)} copy-done((s32[64,2]{0,1:T(2,128)S(1)}, s32[64,2]{0,1:T(2,128)}, u32[]{:S(2)}) %copy-start.2) | copy-done | bytes 536
  0.7 0.0 copy-start.5
  0.7 0.9 %copy-done.5 = bf16[64,1792]{1,0:T(8,128)(2,1)S(1)} copy-done((bf16[64,1792]{1,0:T(8,128)(2,1)S(1)}, bf16[64,1792]{1,0:T(8,128)(2,1)}, u32[]{:S(2)}) %copy-start.5) | copy-done | bytes 229400
  1.6 0.0 copy-start
  1.6 0.0 copy-start.1
  1.6 0.6 %dispatch.1 = (bf16[40,896]{1,0:T(8,128)(2,1)S(1)}, bf16[40,896]{1,0:T(8,128)(2,1)S(1)}, bf16[40,896]{1,0:T(8,128)(2,1)S(1)}, bf16[40,896]{1,0:T(8,128)(2,1)S(1)...) custom-call(s32[1]{0:T(128)} %bitcast.refs_0_, ...), custom_call_target="tpu_custom_call" | custom-call | flops 20000000000 | bytes 44040192 | tf_op jit(solution)/shard_map/dispatch/pallas_call | solution.py:178
  2.2 6.0 %collective-permute-start = (bf16[40,896]{1,0:T(8,128)(2,1)S(1)}, bf16[40,896]{1,0:T(8,128)(2,1)S(1)}, u32[]{:S(2)}, u32[]{:S(2)}) collective-permute-start(bf16[40,896]{1,0:T(8,128)(2,1)S(1)} %get-tuple-element.21), channel_id=1, source_target_pairs={{0,14},{2,12},{4,10},{6,8},{8,6},{10,4},{12,2},{14,0},{1,15},{3,13... | collective-permute-start | bytes 215048 | tf_op jit(solution)/shard_map/ppermute | solution.py:194
  8.3 0.2 collective-permute-start.1
  8.5 0.8 %collective-permute-start.2 = (bf16[40,896]{1,0:T(8,128)(2,1)S(1)}, bf16[40,896]{1,0:T(8,128)(2,1)S(1)}, u32[]{:S(2)}, u32[]{:S(2)}) collective-permute-start(bf16[40,896]{1,0:T(8,128)(2,1)S(1)} %get-tuple-element.23), channel_id=1, source_target_pairs={{0,10},{2,8},{4,14},{6,12},{8,2},{10,0},{12,6},{14,4},{1,11},{3,9}... | collective-permute-start | bytes 215048 | tf_op jit(solution)/shard_map/ppermute | solution.py:194
  9.3 2.0 %collective-permute-start.3 = (bf16[40,896]{1,0:T(8,128)(2,1)S(1)}, bf16[40,896]{1,0:T(8,128)(2,1)S(1)}, u32[]{:S(2)}, u32[]{:S(2)}) collective-permute-start(bf16[40,896]{1,0:T(8,128)(2,1)S(1)} %get-tuple-element.24), channel_id=1, source_target_pairs={{0,8},{2,10},{4,12},{6,14},{8,0},{10,2},{12,4},{14,6},{1,9},{3,11}... | collective-permute-start | bytes 215048 | tf_op jit(solution)/shard_map/ppermute | solution.py:194
  11.3 2.3 %collective-permute-start.4 = (bf16[40,896]{1,0:T(8,128)(2,1)S(1)}, bf16[40,896]{1,0:T(8,128)(2,1)S(1)}, u32[]{:S(2)}, u32[]{:S(2)}) collective-permute-start(bf16[40,896]{1,0:T(8,128)(2,1)S(1)} %get-tuple-element.25), channel_id=1, source_target_pairs={{0,6},{2,4},{4,2},{6,0},{8,14},{10,12},{12,10},{14,8},{1,7},{3,5},... | collective-permute-start | bytes 215048 | tf_op jit(solution)/shard_map/ppermute | solution.py:194
  13.6 0.0 collective-permute-done.refs_0_
  13.6 1.8 %collective-permute-start.5 = (bf16[40,896]{1,0:T(8,128)(2,1)S(1)}, bf16[40,896]{1,0:T(8,128)(2,1)S(1)}, u32[]{:S(2)}, u32[]{:S(2)}) collective-permute-start(bf16[40,896]{1,0:T(8,128)(2,1)S(1)} %get-tuple-element.26), channel_id=1, source_target_pairs={{0,4},{2,6},{4,0},{6,2},{8,12},{10,14},{12,8},{14,10},{1,5},{3,7},... | collective-permute-start | bytes 215048 | tf_op jit(solution)/shard_map/ppermute | solution.py:194
  15.4 0.0 collective-permute-done.1.refs_1_
  15.4 0.5 %collective-permute-start.6 = (bf16[40,896]{1,0:T(8,128)(2,1)S(1)}, bf16[40,896]{1,0:T(8,128)(2,1)S(1)}, u32[]{:S(2)}, u32[]{:S(2)}) collective-permute-start(bf16[40,896]{1,0:T(8,128)(2,1)S(1)} %get-tuple-element.27), channel_id=1, source_target_pairs={{0,2},{2,0},{4,6},{6,4},{8,10},{10,8},{12,14},{14,12},{1,3},{3,1},... | collective-permute-start | bytes 215048 | tf_op jit(solution)/shard_map/ppermute | solution.py:194
  16.0 3.6 %collective-permute-done.2.refs_2_ = bf16[40,896]{1,0:T(8,128)(2,1)S(1)} collective-permute-done((bf16[40,896]{1,0:T(8,128)(2,1)S(1)}, bf16[40,896]{1,0:T(8,128)(2,1)S(1)}, u32[]{:S(2)}, u32[]{:S(2)}) %collective-permute-start.2) | collective-permute-done | bytes 71712 | tf_op jit(solution)/shard_map/ppermute | solution.py:194
  19.6 0.9 %collective-permute-done.3.refs_3_ = bf16[40,896]{1,0:T(8,128)(2,1)S(1)} collective-permute-done((bf16[40,896]{1,0:T(8,128)(2,1)S(1)}, bf16[40,896]{1,0:T(8,128)(2,1)S(1)}, u32[]{:S(2)}, u32[]{:S(2)}) %collective-permute-start.3) | collective-permute-done | bytes 71712 | tf_op jit(solution)/shard_map/ppermute | solution.py:194
  20.5 0.0 collective-permute-done.4.refs_4_
  20.5 0.0 collective-permute-done.5.refs_5_
  20.5 0.0 collective-permute-done.6.refs_6_
  20.5 0.0 copy-done
  20.5 0.0 copy-done.1
  20.5 0.0 slice-start
  20.5 1.4 %gate_up.3.own_ref = bf16[160,2048]{1,0:T(8,128)(2,1)S(1)} custom-call(bf16[40,896]{1,0:T(8,128)(2,1)S(1)} %collective-permute-done.refs_0_, bf16[40,896]{1,0:T(8,128)(2,1)S(1)} %collective-permute-done.1.refs_1_, bf16[40,896]{1,0:T(8,128)(2,1)S(1)} %collective-permute-done.2.refs_2_, bf16[40,896]{1,0:T(8,128)(2,1)S(1)} %collective-permute-done.3.refs_3_, ...), custom_call_target="tpu_custom_call" | custom-call | tf_op jit(solution)/shard_map/gate_up/pallas_call | solution.py:178
  21.9 0.0 slice-start.1
  21.9 0.1 collective-permute-start.8
  22.0 1.4 %gate_up.2.refs_0_ = bf16[160,2048]{1,0:T(8,128)(2,1)S(1)} custom-call(bf16[40,896]{1,0:T(8,128)(2,1)S(1)} %collective-permute-done.refs_0_, bf16[40,896]{1,0:T(8,128)(2,1)S(1)} %collective-permute-done.1.refs_1_, bf16[40,896]{1,0:T(8,128)(2,1)S(1)} %collective-permute-done.2.refs_2_, bf16[40,896]{1,0:T(8,128)(2,1)S(1)} %collective-permute-done.3.refs_3_, ...), custom_call_target="tpu_custom_call" | custom-call | tf_op jit(solution)/shard_map/gate_up/pallas_call | solution.py:178
  23.3 0.6 %collective-permute-start.7 = (bf16[160,2048]{1,0:T(8,128)(2,1)S(1)}, bf16[160,2048]{1,0:T(8,128)(2,1)S(1)}, u32[]{:S(2)}, u32[]{:S(2)}) collective-permute-start(bf16[160,2048]{1,0:T(8,128)(2,1)S(1)} %gate_up.2.refs_0_), channel_id=1, source_target_pairs={{0,1},{1,0},{2,3},{3,2},{4,5},{5,4},{6,7},{7,6},{8,9},{9,8},{10,11... | collective-permute-start | bytes 1966088 | tf_op jit(solution)/shard_map/ppermute | solution.py:194
  23.9 0.2 collective-permute-done.8.other_ref
  24.0 0.0 slice-done
  24.0 0.0 slice-done.1
  24.1 0.9 %down_first.1.refs_3_ = f32[160,1792]{1,0:T(8,128)S(1)} custom-call(bf16[160,2048]{1,0:T(8,128)(2,1)S(1)} %gate_up.3.own_ref, bf16[160,2048]{1,0:T(8,128)(2,1)S(1)} %collective-permute-done.8.other_ref, bf16[2048,1792]{1,0:T(8,128)(2,1)S(1)} %bitcast.4), custom_call_target="tpu_custom_call" | custom-call | tf_op jit(solution)/shard_map/down_first/pallas_call | solution.py:178
  25.0 0.0 copy-start.3
  25.0 0.0 copy-start.4
  25.0 0.6 %collective-permute-done.7.refs_1_ = bf16[160,2048]{1,0:T(8,128)(2,1)S(1)} collective-permute-done((bf16[160,2048]{1,0:T(8,128)(2,1)S(1)}, bf16[160,2048]{1,0:T(8,128)(2,1)S(1)}, u32[]{:S(2)}, u32[]{:S(2)}) %collective-permute-start.7) | collective-permute-done | bytes 655392 | tf_op jit(solution)/shard_map/ppermute | solution.py:194
  25.6 1.0 %down_last.1 = (bf16[40,896]{1,0:T(8,128)(2,1)S(1)}, bf16[40,896]{1,0:T(8,128)(2,1)S(1)}, bf16[40,896]{1,0:T(8,128)(2,1)S(1)}, bf16[40,896]{1,0:T(8,128)(2,1)S(1...) custom-call(bf16[160,2048]{1,0:T(8,128)(2,1)S(1)} %gate_up.2.refs_0_, ...), custom_call_target="tpu_custom_call" | custom-call | tf_op jit(solution)/shard_map/down_last/pallas_call | solution.py:178
  26.6 3.6 %collective-permute-start.10 = (bf16[40,896]{1,0:T(8,128)(2,1)S(1)}, bf16[40,896]{1,0:T(8,128)(2,1)S(1)}, u32[]{:S(2)}, u32[]{:S(2)}) collective-permute-start(bf16[40,896]{1,0:T(8,128)(2,1)S(1)} %get-tuple-element.30), channel_id=1, source_target_pairs={{0,12},{2,14},{4,8},{6,10},{8,4},{10,6},{12,0},{14,2},{1,13},{3,15... | collective-permute-start | bytes 215048 | tf_op jit(solution)/shard_map/ppermute | solution.py:194
  30.2 0.3 collective-permute-start.11
  30.5 3.5 %collective-permute-start.12 = (bf16[40,896]{1,0:T(8,128)(2,1)S(1)}, bf16[40,896]{1,0:T(8,128)(2,1)S(1)}, u32[]{:S(2)}, u32[]{:S(2)}) collective-permute-start(bf16[40,896]{1,0:T(8,128)(2,1)S(1)} %get-tuple-element.32), channel_id=1, source_target_pairs={{0,8},{2,10},{4,12},{6,14},{8,0},{10,2},{12,4},{14,6},{1,9},{3,11}... | collective-permute-start | bytes 215048 | tf_op jit(solution)/shard_map/ppermute | solution.py:194
  34.0 0.8 %collective-permute-start.13 = (bf16[40,896]{1,0:T(8,128)(2,1)S(1)}, bf16[40,896]{1,0:T(8,128)(2,1)S(1)}, u32[]{:S(2)}, u32[]{:S(2)}) collective-permute-start(bf16[40,896]{1,0:T(8,128)(2,1)S(1)} %get-tuple-element.33), channel_id=1, source_target_pairs={{0,6},{2,4},{4,2},{6,0},{8,14},{10,12},{12,10},{14,8},{1,7},{3,5},... | collective-permute-start | bytes 215048 | tf_op jit(solution)/shard_map/ppermute | solution.py:194
  34.8 1.2 %collective-permute-start.14 = (bf16[40,896]{1,0:T(8,128)(2,1)S(1)}, bf16[40,896]{1,0:T(8,128)(2,1)S(1)}, u32[]{:S(2)}, u32[]{:S(2)}) collective-permute-start(bf16[40,896]{1,0:T(8,128)(2,1)S(1)} %get-tuple-element.34), channel_id=1, source_target_pairs={{0,4},{2,6},{4,0},{6,2},{8,12},{10,14},{12,8},{14,10},{1,5},{3,7},... | collective-permute-start | bytes 215048 | tf_op jit(solution)/shard_map/ppermute | solution.py:194
  36.0 0.0 collective-permute-done.10.refs_4_
  36.0 1.5 %collective-permute-start.15 = (bf16[40,896]{1,0:T(8,128)(2,1)S(1)}, bf16[40,896]{1,0:T(8,128)(2,1)S(1)}, u32[]{:S(2)}, u32[]{:S(2)}) collective-permute-start(bf16[40,896]{1,0:T(8,128)(2,1)S(1)} %get-tuple-element.35), channel_id=1, source_target_pairs={{0,2},{2,0},{4,6},{6,4},{8,10},{10,8},{12,14},{14,12},{1,3},{3,1},... | collective-permute-start | bytes 215048 | tf_op jit(solution)/shard_map/ppermute | solution.py:194
  37.5 2.2 %collective-permute-done.11.refs_5_ = bf16[40,896]{1,0:T(8,128)(2,1)S(1)} collective-permute-done((bf16[40,896]{1,0:T(8,128)(2,1)S(1)}, bf16[40,896]{1,0:T(8,128)(2,1)S(1)}, u32[]{:S(2)}, u32[]{:S(2)}) %collective-permute-start.11) | collective-permute-done | bytes 71712 | tf_op jit(solution)/shard_map/ppermute | solution.py:194
  39.7 3.7 %collective-permute-start.9 = (bf16[40,896]{1,0:T(8,128)(2,1)S(1)}, bf16[40,896]{1,0:T(8,128)(2,1)S(1)}, u32[]{:S(2)}, u32[]{:S(2)}) collective-permute-start(bf16[40,896]{1,0:T(8,128)(2,1)S(1)} %get-tuple-element.29), channel_id=1, source_target_pairs={{0,14},{2,12},{4,10},{6,8},{8,6},{10,4},{12,2},{14,0},{1,15},{3,13... | collective-permute-start | bytes 215048 | tf_op jit(solution)/shard_map/ppermute | solution.py:194
  43.4 0.0 collective-permute-done.12.refs_6_
  43.4 0.0 collective-permute-done.13.refs_7_
  43.4 0.0 collective-permute-done.14.refs_8_
  43.4 0.0 collective-permute-done.15.refs_9_
  43.4 3.3 %collective-permute-done.9.refs_3_ = bf16[40,896]{1,0:T(8,128)(2,1)S(1)} collective-permute-done((bf16[40,896]{1,0:T(8,128)(2,1)S(1)}, bf16[40,896]{1,0:T(8,128)(2,1)S(1)}, u32[]{:S(2)}, u32[]{:S(2)}) %collective-permute-start.9) | collective-permute-done | bytes 71712 | tf_op jit(solution)/shard_map/ppermute | solution.py:194
  46.7 0.0 copy-done.3
  46.7 0.0 copy-done.4
  46.7 1.4 %combine.1 = bf16[64,1792]{1,0:T(8,128)(2,1)} custom-call(s32[1]{0:T(128)} %bitcast.refs_0_, s32[2,64]{1,0:T(2,128)S(1)} %bitcast.6, f32[2,64]{1,0:T(2,128)S(1)} %bitcast.7, bf16[40,896]{1,0:T(8,128)(2,1)S(1)} %collective-permute-done.9.refs_3_, bf16[40,896]{1,0:T(8,128)(2,1)S(1)} %collective-permute-done.10.refs_4_, ...), custom_call_target="tpu_custom_call" | custom-call | tf_op jit(solution)/shard_map/combine/pallas_call | solution.py:178
  (1 shorter events, 0.0 us)
Async XLA Ops:
  0.0 0.7 %copy-start.2 = (s32[64,2]{0,1:T(2,128)S(1)}, s32[64,2]{0,1:T(2,128)}, u32[]{:S(2)}) copy-start(s32[64,2]{0,1:T(2,128)} %param.7) | copy-start | bytes 1540
  0.7 0.9 %copy-start.5 = (bf16[64,1792]{1,0:T(8,128)(2,1)S(1)}, bf16[64,1792]{1,0:T(8,128)(2,1)}, u32[]{:S(2)}) copy-start(bf16[64,1792]{1,0:T(8,128)(2,1)} %refs_2_.2) | copy-start | bytes 688132
  1.6 18.8 %copy-start = (bf16[1792,2048]{1,0:T(8,128)(2,1)S(1)}, bf16[1792,2048]{1,0:T(8,128)(2,1)}, u32[]{:S(2)}) copy-start(bf16[1792,2048]{1,0:T(8,128)(2,1)} %refs_8_.3) | copy-start | bytes 22020100
  1.6 18.9 %copy-start.1 = (bf16[1792,2048]{1,0:T(8,128)(2,1)S(1)}, bf16[1792,2048]{1,0:T(8,128)(2,1)}, u32[]{:S(2)}) copy-start(bf16[1792,2048]{1,0:T(8,128)(2,1)} %refs_9_.3) | copy-start | bytes 22020100
  2.2 11.3 %collective-permute-start = (bf16[40,896]{1,0:T(8,128)(2,1)S(1)}, bf16[40,896]{1,0:T(8,128)(2,1)S(1)}, u32[]{:S(2)}, u32[]{:S(2)}) collective-permute-start(bf16[40,896]{1,0:T(8,128)(2,1)S(1)} %get-tuple-element.21), channel_id=1, source_target_pairs={{0,14},{2,12},{4,10},{6,8},{8,6},{10,4},{12,2},{14,0},{1,15},{3,13... | collective-permute-start | bytes 215048 | tf_op jit(solution)/shard_map/ppermute | solution.py:194
  8.3 7.1 %collective-permute-start.1 = (bf16[40,896]{1,0:T(8,128)(2,1)S(1)}, bf16[40,896]{1,0:T(8,128)(2,1)S(1)}, u32[]{:S(2)}, u32[]{:S(2)}) collective-permute-start(bf16[40,896]{1,0:T(8,128)(2,1)S(1)} %get-tuple-element.22), channel_id=1, source_target_pairs={{0,12},{2,14},{4,8},{6,10},{8,4},{10,6},{12,0},{14,2},{1,13},{3,15... | collective-permute-start | bytes 215048 | tf_op jit(solution)/shard_map/ppermute | solution.py:194
  8.5 11.1 %collective-permute-start.2 = (bf16[40,896]{1,0:T(8,128)(2,1)S(1)}, bf16[40,896]{1,0:T(8,128)(2,1)S(1)}, u32[]{:S(2)}, u32[]{:S(2)}) collective-permute-start(bf16[40,896]{1,0:T(8,128)(2,1)S(1)} %get-tuple-element.23), channel_id=1, source_target_pairs={{0,10},{2,8},{4,14},{6,12},{8,2},{10,0},{12,6},{14,4},{1,11},{3,9}... | collective-permute-start | bytes 215048 | tf_op jit(solution)/shard_map/ppermute | solution.py:194
  9.3 11.2 %collective-permute-start.3 = (bf16[40,896]{1,0:T(8,128)(2,1)S(1)}, bf16[40,896]{1,0:T(8,128)(2,1)S(1)}, u32[]{:S(2)}, u32[]{:S(2)}) collective-permute-start(bf16[40,896]{1,0:T(8,128)(2,1)S(1)} %get-tuple-element.24), channel_id=1, source_target_pairs={{0,8},{2,10},{4,12},{6,14},{8,0},{10,2},{12,4},{14,6},{1,9},{3,11}... | collective-permute-start | bytes 215048 | tf_op jit(solution)/shard_map/ppermute | solution.py:194
  11.3 9.2 %collective-permute-start.4 = (bf16[40,896]{1,0:T(8,128)(2,1)S(1)}, bf16[40,896]{1,0:T(8,128)(2,1)S(1)}, u32[]{:S(2)}, u32[]{:S(2)}) collective-permute-start(bf16[40,896]{1,0:T(8,128)(2,1)S(1)} %get-tuple-element.25), channel_id=1, source_target_pairs={{0,6},{2,4},{4,2},{6,0},{8,14},{10,12},{12,10},{14,8},{1,7},{3,5},... | collective-permute-start | bytes 215048 | tf_op jit(solution)/shard_map/ppermute | solution.py:194
  13.6 6.9 %collective-permute-start.5 = (bf16[40,896]{1,0:T(8,128)(2,1)S(1)}, bf16[40,896]{1,0:T(8,128)(2,1)S(1)}, u32[]{:S(2)}, u32[]{:S(2)}) collective-permute-start(bf16[40,896]{1,0:T(8,128)(2,1)S(1)} %get-tuple-element.26), channel_id=1, source_target_pairs={{0,4},{2,6},{4,0},{6,2},{8,12},{10,14},{12,8},{14,10},{1,5},{3,7},... | collective-permute-start | bytes 215048 | tf_op jit(solution)/shard_map/ppermute | solution.py:194
  15.4 5.0 %collective-permute-start.6 = (bf16[40,896]{1,0:T(8,128)(2,1)S(1)}, bf16[40,896]{1,0:T(8,128)(2,1)S(1)}, u32[]{:S(2)}, u32[]{:S(2)}) collective-permute-start(bf16[40,896]{1,0:T(8,128)(2,1)S(1)} %get-tuple-element.27), channel_id=1, source_target_pairs={{0,2},{2,0},{4,6},{6,4},{8,10},{10,8},{12,14},{14,12},{1,3},{3,1},... | collective-permute-start | bytes 215048 | tf_op jit(solution)/shard_map/ppermute | solution.py:194
  20.5 3.6 %slice-start = ((s8[7340032]{0:T(1024)(128)(4,1)}), s8[4194304]{0:T(1024)(128)(4,1)S(1)}, s32[]{:S(2)}) async-start(s8[7340032]{0:T(1024)(128)(4,1)} %bitcast.3), calls=%async_computation | async-start | bytes 8388608
  21.9 2.2 %slice-start.1 = ((s8[7340032]{0:T(1024)(128)(4,1)}), s8[3145728]{0:T(1024)(128)(4,1)S(1)}, s32[]{:S(2)}) async-start(s8[7340032]{0:T(1024)(128)(4,1)} %bitcast.3), calls=%async_computation.1 | async-start | bytes 6291456
  21.9 2.2 %collective-permute-start.8 = (bf16[160,2048]{1,0:T(8,128)(2,1)S(1)}, bf16[160,2048]{1,0:T(8,128)(2,1)S(1)}, u32[]{:S(2)}, u32[]{:S(2)}) collective-permute-start(bf16[160,2048]{1,0:T(8,128)(2,1)S(1)} %gate_up.3.own_ref), channel_id=1, source_target_pairs={{0,1},{1,0},{2,3},{3,2},{4,5},{5,4},{6,7},{7,6},{8,9},{9,8},{10,11... | collective-permute-start | bytes 1966088 | tf_op jit(solution)/shard_map/ppermute | solution.py:194
  23.3 2.3 %collective-permute-start.7 = (bf16[160,2048]{1,0:T(8,128)(2,1)S(1)}, bf16[160,2048]{1,0:T(8,128)(2,1)S(1)}, u32[]{:S(2)}, u32[]{:S(2)}) collective-permute-start(bf16[160,2048]{1,0:T(8,128)(2,1)S(1)} %gate_up.2.refs_0_), channel_id=1, source_target_pairs={{0,1},{1,0},{2,3},{3,2},{4,5},{5,4},{6,7},{7,6},{8,9},{9,8},{10,11... | collective-permute-start | bytes 1966088 | tf_op jit(solution)/shard_map/ppermute | solution.py:194
  25.0 21.7 %copy-start.3 = (s32[64,2]{0,1:T(2,128)S(1)}, s32[64,2]{0,1:T(2,128)}, u32[]{:S(2)}) copy-start(s32[64,2]{0,1:T(2,128)} %param.7) | copy-start | bytes 1540
  25.0 21.7 %copy-start.4 = (f32[64,2]{0,1:T(2,128)S(1)}, f32[64,2]{0,1:T(2,128)}, u32[]{:S(2)}) copy-start(f32[64,2]{0,1:T(2,128)} %param.8) | copy-start | bytes 1540
  26.6 9.4 %collective-permute-start.10 = (bf16[40,896]{1,0:T(8,128)(2,1)S(1)}, bf16[40,896]{1,0:T(8,128)(2,1)S(1)}, u32[]{:S(2)}, u32[]{:S(2)}) collective-permute-start(bf16[40,896]{1,0:T(8,128)(2,1)S(1)} %get-tuple-element.30), channel_id=1, source_target_pairs={{0,12},{2,14},{4,8},{6,10},{8,4},{10,6},{12,0},{14,2},{1,13},{3,15... | collective-permute-start | bytes 215048 | tf_op jit(solution)/shard_map/ppermute | solution.py:194
  30.2 9.5 %collective-permute-start.11 = (bf16[40,896]{1,0:T(8,128)(2,1)S(1)}, bf16[40,896]{1,0:T(8,128)(2,1)S(1)}, u32[]{:S(2)}, u32[]{:S(2)}) collective-permute-start(bf16[40,896]{1,0:T(8,128)(2,1)S(1)} %get-tuple-element.31), channel_id=1, source_target_pairs={{0,10},{2,8},{4,14},{6,12},{8,2},{10,0},{12,6},{14,4},{1,11},{3,9}... | collective-permute-start | bytes 215048 | tf_op jit(solution)/shard_map/ppermute | solution.py:194
  30.5 12.9 %collective-permute-start.12 = (bf16[40,896]{1,0:T(8,128)(2,1)S(1)}, bf16[40,896]{1,0:T(8,128)(2,1)S(1)}, u32[]{:S(2)}, u32[]{:S(2)}) collective-permute-start(bf16[40,896]{1,0:T(8,128)(2,1)S(1)} %get-tuple-element.32), channel_id=1, source_target_pairs={{0,8},{2,10},{4,12},{6,14},{8,0},{10,2},{12,4},{14,6},{1,9},{3,11}... | collective-permute-start | bytes 215048 | tf_op jit(solution)/shard_map/ppermute | solution.py:194
  34.0 9.4 %collective-permute-start.13 = (bf16[40,896]{1,0:T(8,128)(2,1)S(1)}, bf16[40,896]{1,0:T(8,128)(2,1)S(1)}, u32[]{:S(2)}, u32[]{:S(2)}) collective-permute-start(bf16[40,896]{1,0:T(8,128)(2,1)S(1)} %get-tuple-element.33), channel_id=1, source_target_pairs={{0,6},{2,4},{4,2},{6,0},{8,14},{10,12},{12,10},{14,8},{1,7},{3,5},... | collective-permute-start | bytes 215048 | tf_op jit(solution)/shard_map/ppermute | solution.py:194
  34.8 8.6 %collective-permute-start.14 = (bf16[40,896]{1,0:T(8,128)(2,1)S(1)}, bf16[40,896]{1,0:T(8,128)(2,1)S(1)}, u32[]{:S(2)}, u32[]{:S(2)}) collective-permute-start(bf16[40,896]{1,0:T(8,128)(2,1)S(1)} %get-tuple-element.34), channel_id=1, source_target_pairs={{0,4},{2,6},{4,0},{6,2},{8,12},{10,14},{12,8},{14,10},{1,5},{3,7},... | collective-permute-start | bytes 215048 | tf_op jit(solution)/shard_map/ppermute | solution.py:194
  36.0 7.4 %collective-permute-start.15 = (bf16[40,896]{1,0:T(8,128)(2,1)S(1)}, bf16[40,896]{1,0:T(8,128)(2,1)S(1)}, u32[]{:S(2)}, u32[]{:S(2)}) collective-permute-start(bf16[40,896]{1,0:T(8,128)(2,1)S(1)} %get-tuple-element.35), channel_id=1, source_target_pairs={{0,2},{2,0},{4,6},{6,4},{8,10},{10,8},{12,14},{14,12},{1,3},{3,1},... | collective-permute-start | bytes 215048 | tf_op jit(solution)/shard_map/ppermute | solution.py:194
  39.7 7.0 %collective-permute-start.9 = (bf16[40,896]{1,0:T(8,128)(2,1)S(1)}, bf16[40,896]{1,0:T(8,128)(2,1)S(1)}, u32[]{:S(2)}, u32[]{:S(2)}) collective-permute-start(bf16[40,896]{1,0:T(8,128)(2,1)S(1)} %get-tuple-element.29), channel_id=1, source_target_pairs={{0,14},{2,12},{4,10},{6,8},{8,6},{10,4},{12,2},{14,0},{1,15},{3,13... | collective-permute-start | bytes 215048 | tf_op jit(solution)/shard_map/ppermute | solution.py:194

commit v3 on v2

--- a/solution.py
+++ b/solution.py
@@ -10,8 +10,9 @@
 F32 = jnp.float32
 VMEM_SPEC = pl.BlockSpec(memory_space=pltpu.VMEM)
 SMEM_SPEC = pl.BlockSpec(memory_space=pltpu.SMEM)
-PIECES = 2
-ORDER = (7, 6, 5, 4, 3, 2, 1, 0)
+PIECES = (2,)
+BATCHES = ((6, 1, 4, 3, 5, 7, 2, 0),)
+STARTS = (6, 1, 4, 3, 5, 7, 2, 0)
 
 
 def pair_slots(id_blocks, expert_count):
@@ -88,27 +89,34 @@
     ]
 
 
-def dispatch_kernel(n, cap, me_ref, ids_ref, tok_ref, *out_refs):
+def dispatch_kernel(n, cap, me_ref, ids_hbm, tok_hbm, *refs):
+    out_refs, (ids_ref, tok_ref, sems) = refs[:n], refs[n:]
+    ids_copy = pltpu.make_async_copy(ids_hbm, ids_ref, sems.at[0])
+    tok_copy = pltpu.make_async_copy(tok_hbm, tok_ref, sems.at[1])
+    ids_copy.start()
+    tok_copy.start()
     tok_rows, width = tok_ref.shape
     half = width // 2
+    ids_copy.wait()
     rows = slot_rows(ids_ref, me_ref[0], n, cap, tok_rows)
     number = lax.broadcasted_iota(jnp.int32, (2 * cap * n, tok_rows), 0)
     upper = jnp.where((number == rows[0]) | (number == rows[1]), 1.0, 0.0).astype(BF16)
     lower = jnp.where((number == rows[0] + cap) | (number == rows[1] + cap), 1.0, 0.0).astype(BF16)
+    tok_copy.wait()
     packed = jnp.dot(upper, tok_ref[:, :half], preferred_element_type=F32)
     packed = packed + jnp.dot(lower, tok_ref[:, half:], preferred_element_type=F32)
-    for o, out_ref in zip(ORDER, out_refs):
+    for o, out_ref in zip(STARTS, out_refs):
         out_ref[...] = packed[o * 2 * cap : (o + 1) * 2 * cap].astype(BF16)
 
 
-def gate_up_kernel(n, cap, piece, *refs):
-    blocks, (wg_ref, wu_ref, out_ref, x_ref) = refs[:n], refs[n:]
+def gate_up_kernel(cap, piece, *refs):
+    blocks, (wg_ref, wu_ref, out_ref, x_ref) = refs[:-4], refs[-4:]
     half = blocks[0].shape[1]
-    for o, block in zip(ORDER, blocks):
-        x_ref[pl.ds(o * cap, cap), :half] = block[:cap, :]
-        x_ref[pl.ds(o * cap, cap), half:] = block[cap:, :]
+    for i, block in enumerate(blocks):
+        x_ref[pl.ds(i * cap, cap), :half] = block[:cap, :]
+        x_ref[pl.ds(i * cap, cap), half:] = block[cap:, :]
     width = out_ref.shape[1] // 2
-    tile = 512
+    tile = min(512, width)
     for which, w_ref in enumerate((wg_ref, wu_ref)):
         for j in range(width // tile):
             columns = pl.ds(piece * width + j * tile, tile)
@@ -124,67 +132,95 @@
     return (gate / (1.0 + jnp.exp(-gate)) * up).astype(BF16)
 
 
-def down_first_kernel(own_ref, other_ref, wd_ref, acc_ref):
+def down_first_kernel(count, *refs):
+    own, other, (wd_ref, acc_ref) = refs[:count], refs[count : 2 * count], refs[2 * count :]
+    total = None
+    for i in range(count):
+        hidden = hidden_of(own[i], other[i])
+        depth = hidden.shape[1]
+        term = jnp.dot(hidden, wd_ref[pl.ds(i * depth, depth), :], preferred_element_type=F32)
+        total = term if total is None else total + term
+    acc_ref[...] = total
+
+
+def down_last_kernel(cap, own_ref, other_ref, wd_ref, acc_ref, *out_refs):
     hidden = hidden_of(own_ref, other_ref)
-    acc_ref[...] = jnp.dot(hidden, wd_ref[: hidden.shape[1], :], preferred_element_type=F32)
-
-
-def down_last_kernel(n, cap, own_ref, other_ref, wd_ref, acc_ref, *out_refs):
-    hidden = hidden_of(own_ref, other_ref)
-    depth = hidden.shape[1]
-    out = acc_ref[...] + jnp.dot(hidden, wd_ref[depth:, :], preferred_element_type=F32)
+    out = acc_ref[...] + jnp.dot(
+        hidden, wd_ref[wd_ref.shape[0] - hidden.shape[1] :, :], preferred_element_type=F32
+    )
     half = out.shape[1] // 2
-    for o, out_ref in zip(ORDER, out_refs):
-        out_ref[:cap, :] = out[o * cap : (o + 1) * cap, :half].astype(BF16)
-        out_ref[cap:, :] = out[o * cap : (o + 1) * cap, half:].astype(BF16)
-
-
-def combine_kernel(n, cap, me_ref, ids_ref, weights_ref, *refs):
-    blocks, (out_ref, all_ref) = refs[:n], refs[n:]
+    for i, out_ref in enumerate(out_refs):
+        out_ref[:cap, :] = out[i * cap : (i + 1) * cap, :half].astype(BF16)
+        out_ref[cap:, :] = out[i * cap : (i + 1) * cap, half:].astype(BF16)
+
+
+def plan_kernel(n, cap, me_ref, ids_ref, weights_ref, pick_ref, scale_ref):
+    tok_rows = ids_ref.shape[1]
+    rows = slot_rows(ids_ref, me_ref[0], n, cap, tok_rows)
+    own = lax.broadcasted_iota(jnp.int32, (tok_rows, tok_rows), 0) == lax.broadcasted_iota(
+        jnp.int32, (tok_rows, tok_rows), 1
+    )
+    number = lax.broadcasted_iota(jnp.int32, (tok_rows, 2 * cap * n), 1)
+    for k in range(2):
+        weight = jnp.sum(jnp.where(own, weights_ref[k : k + 1, :], 0.0), axis=1, keepdims=True)
+        scale_ref[pl.ds(k * tok_rows, tok_rows), :] = jnp.broadcast_to(weight, (tok_rows, 128))
+        row = jnp.sum(jnp.where(own, rows[k].astype(F32), 0.0), axis=1, keepdims=True)
+        row = row.astype(jnp.int32)
+        for part in range(2):
+            pick = jnp.where(number == row + part * cap, 1.0, 0.0).astype(BF16)
+            pick_ref[pl.ds((2 * part + k) * tok_rows, tok_rows), :] = pick
+
+
+def combine_kernel(cap, places, pick_ref, scale_ref, *refs):
+    n = len(places)
+    blocks, (out_hbm, all_ref, out_ref, sems) = refs[:n], refs[n:]
     tok_rows, width = out_ref.shape
     half = width // 2
-    for o, block in zip(ORDER, blocks):
+    for o, block in zip(places, blocks):
         all_ref[pl.ds(o * 2 * cap, 2 * cap), :] = block[...]
-    rows = slot_rows(ids_ref, me_ref[0], n, cap, tok_rows)
-    number = lax.broadcasted_iota(jnp.int32, (2 * cap * n, tok_rows), 0)
-    own = lax.broadcasted_iota(jnp.int32, (tok_rows, tok_rows), 0) == lax.broadcasted_iota(
-        jnp.int32, (tok_rows, tok_rows), 1
-    )
-    weights = [
-        jnp.sum(jnp.where(own, weights_ref[k : k + 1, :], 0.0), axis=1, keepdims=True)
-        for k in range(2)
-    ]
+    weights = [scale_ref[pl.ds(k * tok_rows, tok_rows), 0:1] for k in range(2)]
+    copies = []
     for part in range(2):
-        total = None
-        for k in range(2):
-            pick = jnp.where(number == rows[k] + part * cap, 1.0, 0.0).astype(BF16)
-            picked = lax.dot_general(
-                pick, all_ref[...], (((0,), (0,)), ((), ())), preferred_element_type=F32
+        picked = jnp.dot(
+            pick_ref[pl.ds(2 * part * tok_rows, 2 * tok_rows), :],
+            all_ref[...],
+            preferred_element_type=F32,
+        )
+        total = weights[0] * picked[:tok_rows] + weights[1] * picked[tok_rows:]
+        columns = pl.ds(part * half, half)
+        out_ref[:, columns] = total.astype(BF16)
+        copies.append(
+            pltpu.make_async_copy(
+                out_ref.at[:, columns], out_hbm.at[:, columns], sems.at[part]
             )
-            term = weights[k] * picked
-            total = term if total is None else total + term
-        out_ref[:, part * half : (part + 1) * half] = total.astype(BF16)
+        )
+        copies[-1].start()
+    for copy in copies:
+        copy.wait()
 
 
 def in_vmem(x):
     return pltpu.with_memory_space_constraint(x, pltpu.VMEM)
 
 
-def call(kernel, outs, args, smem=0, scratch=(), limit=20 << 20, cost=None, name=None, to_vmem=True):
+def in_hbm(x):
+    return pltpu.with_memory_space_constraint(x, pltpu.HBM)
+
+
+def call(kernel, outs, args, smem=0, hbm=0, scratch=(), limit=20 << 20, cost=None, name=None):
     many = isinstance(outs, (tuple, list))
-    shapes = [
-        pltpu.VMEM(o.shape, o.dtype) if to_vmem else o for o in (outs if many else [outs])
-    ]
     result = pl.pallas_call(
         kernel,
-        out_shape=shapes,
-        in_specs=[SMEM_SPEC] * smem + [VMEM_SPEC] * (len(args) - smem),
-        out_specs=[VMEM_SPEC] * len(shapes),
+        out_shape=[pltpu.VMEM(o.shape, o.dtype) for o in (outs if many else [outs])],
+        in_specs=[SMEM_SPEC] * smem
+        + [pl.BlockSpec(memory_space=pltpu.HBM)] * hbm
+        + [VMEM_SPEC] * (len(args) - smem - hbm),
+        out_specs=[VMEM_SPEC] * (len(outs) if many else 1),
         scratch_shapes=scratch,
         compiler_params=pltpu.CompilerParams(vmem_limit_bytes=limit),
         cost_estimate=cost,
         name=name,
-    )(*args[:smem], *(in_vmem(a) for a in args[smem:]))
+    )(*args[: smem + hbm], *(in_vmem(a) for a in args[smem + hbm :]))
     return result if many else result[0]
 
 
@@ -194,61 +230,101 @@
     return lax.ppermute(x, axis, [(i, i ^ distance) for i in range(lax.axis_size(axis))])
 
 
-def one_expert_each(tokens, expert_ids, gate_weights, w_gate, w_up, w_down):
-    tok_rows, width = tokens.shape
-    n = lax.axis_size("expert")
-    cap = capacity_of(tok_rows, expert_ids.shape[1], n)
-    half, hidden_units = width // 2, w_gate.shape[1]
-    me = lax.axis_index("expert").astype(jnp.int32).reshape(1)
-    ids = expert_ids.T
-    loaded = sum(w.size * 2 for w in (w_gate, w_up, w_down))
-    block = jax.ShapeDtypeStruct((2 * cap, half), BF16)
-
-    sent = call(
-        lambda *refs: dispatch_kernel(n, cap, *refs),
-        [block] * n,
-        [me, ids, tokens],
-        smem=1,
-        cost=pl.CostEstimate(flops=20_000_000_000, bytes_accessed=2 * loaded, transcendentals=0),
-        name="dispatch",
-    )
-    received = [swap(x, "expert", o) for o, x in zip(ORDER, sent)]
-
-    piece_width = hidden_units // PIECES
+def experts(blocks, after, pieces, cap, w_gate, w_up, w_down):
+    rows, width, hidden_units = len(blocks) * cap, 2 * blocks[0].shape[1], w_gate.shape[1]
+    piece_width = hidden_units // pieces
     own, other = [], []
-    for piece in range(PIECES):
+    for piece in range(pieces):
         own.append(
             call(
-                lambda *refs, piece=piece: gate_up_kernel(n, cap, piece, *refs),
-                jax.ShapeDtypeStruct((n * cap, 2 * piece_width), BF16),
-                [*received, w_gate, w_up],
-                scratch=[pltpu.VMEM((n * cap, width), BF16)],
+                lambda *refs, piece=piece: gate_up_kernel(cap, piece, *refs[len(after) :]),
+                jax.ShapeDtypeStruct((rows, 2 * piece_width), BF16),
+                [*after, *blocks, w_gate, w_up],
+                scratch=[pltpu.VMEM((rows, width), BF16)],
+                cost=estimate(),
                 name="gate_up",
             )
         )
         other.append(swap(own[-1], "tensor", 1))
     acc = call(
-        down_first_kernel,
-        jax.ShapeDtypeStruct((n * cap, width), F32),
-        [own[0], other[0], w_down],
+        lambda *refs: down_first_kernel(pieces - 1, *refs),
+        jax.ShapeDtypeStruct((rows, width), F32),
+        [*own[:-1], *other[:-1], w_down],
+        cost=estimate(),
         name="down_first",
     )
     results = call(
-        lambda *refs: down_last_kernel(n, cap, *refs),
+        lambda *refs: down_last_kernel(cap, *refs),
+        [jax.ShapeDtypeStruct(b.shape, b.dtype) for b in blocks],
+        [own[-1], other[-1], w_down, acc],
+        cost=estimate(),
+        name="down_last",
+    )
+    return results, own
+
+
+def estimate():
+    return pl.CostEstimate(flops=1, bytes_accessed=0, transcendentals=0)
+
+
+def one_expert_each(tokens, expert_ids, gate_weights, w_gate, w_up, w_down):
+    tok_rows, width = tokens.shape
+    n = lax.axis_size("expert")
+    cap = capacity_of(tok_rows, expert_ids.shape[1], n)
+    half = width // 2
+    me = lax.axis_index("expert").astype(jnp.int32).reshape(1)
+    ids = expert_ids.T
+    loaded = sum(w.size * 2 for w in (w_gate, w_up, w_down))
+    block = jax.ShapeDtypeStruct((2 * cap, half), BF16)
+
+    sent = call(
+        lambda *refs: dispatch_kernel(n, cap, *refs),
         [block] * n,
-        [own[1], other[1], w_down, acc],
-        name="down_last",
-    )
-    returned = [swap(x, "expert", o) for o, x in zip(ORDER, results)]
-    return call(
-        lambda *refs: combine_kernel(n, cap, *refs),
-        jax.ShapeDtypeStruct((tok_rows, width), BF16),
-        [me, ids, gate_weights.T, *returned],
+        [me, in_hbm(ids), in_hbm(tokens)],
         smem=1,
-        scratch=[pltpu.VMEM((2 * cap * n, half), BF16)],
+        hbm=2,
+        scratch=[
+            pltpu.VMEM(ids.shape, ids.dtype),
+            pltpu.VMEM(tokens.shape, tokens.dtype),
+            pltpu.SemaphoreType.DMA((2,)),
+        ],
+        cost=pl.CostEstimate(flops=20_000_000_000, bytes_accessed=2 * loaded, transcendentals=0),
+        name="dispatch",
+    )
+    received = {o: swap(x, "expert", o) for o, x in zip(STARTS, sent)}
+    returned = {}
+    after = []
+    for batch, pieces in zip(BATCHES, PIECES):
+        results, after = experts(
+            [received[o] for o in batch], after, pieces, cap, w_gate, w_up, w_down
+        )
+        for o, x in zip(batch, results):
+            returned[o] = swap(x, "expert", o)
+    pick, scale = call(
+        lambda *refs: plan_kernel(n, cap, *refs),
+        [
+            jax.ShapeDtypeStruct((4 * tok_rows, 2 * cap * n), BF16),
+            jax.ShapeDtypeStruct((2 * tok_rows, 128), F32),
+        ],
+        [me, ids, gate_weights.T],
+        smem=1,
+        cost=estimate(),
+        name="plan",
+    )
+    places = [o for batch in BATCHES for o in batch]
+    return pl.pallas_call(
+        lambda *refs: combine_kernel(cap, places, *refs),
+        out_shape=jax.ShapeDtypeStruct((tok_rows, width), BF16),
+        in_specs=[VMEM_SPEC] * (2 + n),
+        out_specs=pl.BlockSpec(memory_space=pl.ANY),
+        scratch_shapes=[
+            pltpu.VMEM((2 * cap * n, half), BF16),
+            pltpu.VMEM((tok_rows, width), BF16),
+            pltpu.SemaphoreType.DMA((2,)),
+        ],
+        compiler_params=pltpu.CompilerParams(vmem_limit_bytes=20 << 20),
         name="combine",
-        to_vmem=False,
-    )
+    )(*(in_vmem(x) for x in (pick, scale, *(returned[o] for o in places))))
 
 
 def per_device(tokens, expert_ids, gate_weights, w_gate, w_up, w_down):

time: 48.3 us -> 42.2 us (0.87)
  starting transfers between devices: 29 us -> 24.2 us
  local copies, waits for them, and re-layouts: 1.65 us -> 0.03 us
  Pallas kernels: 6.65 us -> 7.54 us
  waiting for transfers between devices: 10.7 us -> 10.1 us
    ppermute x16, starting transfers between devices: 29 us -> 24.2 us  [swap(): lax.ppermute(x, axis, [(i, i ^ distance) for i in range(lax.axis_size(axi...]
    unnamed x16 -> x12, local copies, waits for them, and re-layouts: 1.65 us -> 0.03 us
    pallas_call x6 -> x7, Pallas kernels: 6.65 us -> 7.54 us  [the longest x6 6.46 us: call(): pl.pallas_call(kernel, out_shape=[pltpu.VMEM(o.shape, o.dtype) for o in (...]
    ppermute x16, waiting for transfers between devices: 10.7 us -> 10.1 us  [swap(): lax.ppermute(x, axis, [(i, i ^ distance) for i in range(lax.axis_size(axi...]
  transfers between devices with their start and end apart: 16 -> 16, of which waited for: 6 -> 8; matrix products, arithmetic and copies ran while one was open for 0% -> 0% of each run, Pallas kernels for 5% -> 6%
where the time goes in v3:
time: 42.2 us; the launch traced here: 42 us
  starting transfers between devices  24.2 us (57%)
  waiting for transfers between devices  10.1 us (24%)
  Pallas kernels  7.54 us (18%)
    ppermute x16, starting transfers between devices, swap(): lax.ppermute(x, axis, [(i, i ^ distance) for i in range(lax.axis_size(axi...  24.2 us
    ppermute x16, waiting for transfers between devices, swap(): lax.ppermute(x, axis, [(i, i ^ distance) for i in range(lax.axis_size(axi...  10.1 us
    pallas_call x6, Pallas kernels, call(): pl.pallas_call(kernel, out_shape=[pltpu.VMEM(o.shape, o.dtype) for o in (...  6.46 us
    pallas_call x1, Pallas kernels, one_expert_each(): pl.pallas_call(lambda *refs: combine_kernel(cap, places, *refs), out_shap...  1.08 us
  transfers between devices with their start and end apart: 16, of which 8 were waited for; matrix products, arithmetic and copies ran while one was open for 0% of the time, Pallas kernels for 6%

profile of v3, /device:TPU:0, one launch (start us, length us, event | category | flops | bytes accessed | tf_op | source)
XLA Modules:
  0.0 42.0 jit_solution(17772163325732508814)
XLA Ops:
  0.0 0.0 copy-start
  0.0 0.0 copy-start.1
  0.0 1.6 %dispatch.1 = (bf16[40,896]{1,0:T(8,128)(2,1)S(1)}, bf16[40,896]{1,0:T(8,128)(2,1)S(1)}, bf16[40,896]{1,0:T(8,128)(2,1)S(1)}, bf16[40,896]{1,0:T(8,128)(2,1)S(1)...) custom-call(s32[1]{0:T(128)} %bitcast.refs_0_, ...), custom_call_target="tpu_custom_call" | custom-call | flops 20000000000 | bytes 44040192 | tf_op jit(solution)/shard_map/dispatch/pallas_call | solution.py:212
  1.6 5.1 %collective-permute-start = (bf16[40,896]{1,0:T(8,128)(2,1)S(1)}, bf16[40,896]{1,0:T(8,128)(2,1)S(1)}, u32[]{:S(2)}, u32[]{:S(2)}) collective-permute-start(bf16[40,896]{1,0:T(8,128)(2,1)S(1)} %get-tuple-element.25), channel_id=1, source_target_pairs={{0,12},{2,14},{4,8},{6,10},{8,4},{10,6},{12,0},{14,2},{1,13},{3,15... | collective-permute-start | bytes 215048 | tf_op jit(solution)/shard_map/ppermute | solution.py:230
  6.7 1.5 %collective-permute-start.1 = (bf16[40,896]{1,0:T(8,128)(2,1)S(1)}, bf16[40,896]{1,0:T(8,128)(2,1)S(1)}, u32[]{:S(2)}, u32[]{:S(2)}) collective-permute-start(bf16[40,896]{1,0:T(8,128)(2,1)S(1)} %get-tuple-element.26), channel_id=1, source_target_pairs={{0,2},{2,0},{4,6},{6,4},{8,10},{10,8},{12,14},{14,12},{1,3},{3,1},... | collective-permute-start | bytes 215048 | tf_op jit(solution)/shard_map/ppermute | solution.py:230
  8.2 0.0 collective-permute-start.2
  8.2 0.6 %collective-permute-start.3 = (bf16[40,896]{1,0:T(8,128)(2,1)S(1)}, bf16[40,896]{1,0:T(8,128)(2,1)S(1)}, u32[]{:S(2)}, u32[]{:S(2)}) collective-permute-start(bf16[40,896]{1,0:T(8,128)(2,1)S(1)} %get-tuple-element.28), channel_id=1, source_target_pairs={{0,6},{2,4},{4,2},{6,0},{8,14},{10,12},{12,10},{14,8},{1,7},{3,5},... | collective-permute-start | bytes 215048 | tf_op jit(solution)/shard_map/ppermute | solution.py:230
  8.8 2.8 %collective-permute-start.4 = (bf16[40,896]{1,0:T(8,128)(2,1)S(1)}, bf16[40,896]{1,0:T(8,128)(2,1)S(1)}, u32[]{:S(2)}, u32[]{:S(2)}) collective-permute-start(bf16[40,896]{1,0:T(8,128)(2,1)S(1)} %get-tuple-element.29), channel_id=1, source_target_pairs={{0,10},{2,8},{4,14},{6,12},{8,2},{10,0},{12,6},{14,4},{1,11},{3,9}... | collective-permute-start | bytes 215048 | tf_op jit(solution)/shard_map/ppermute | solution.py:230
  11.6 0.0 collective-permute-done.refs_0_
  11.6 3.0 %collective-permute-start.5 = (bf16[40,896]{1,0:T(8,128)(2,1)S(1)}, bf16[40,896]{1,0:T(8,128)(2,1)S(1)}, u32[]{:S(2)}, u32[]{:S(2)}) collective-permute-start(bf16[40,896]{1,0:T(8,128)(2,1)S(1)} %get-tuple-element.30), channel_id=1, source_target_pairs={{0,14},{2,12},{4,10},{6,8},{8,6},{10,4},{12,2},{14,0},{1,15},{3,13... | collective-permute-start | bytes 215048 | tf_op jit(solution)/shard_map/ppermute | solution.py:230
  14.5 0.0 collective-permute-done.1.refs_1_
  14.5 0.0 collective-permute-start.6
  14.6 0.5 %collective-permute-done.2.refs_2_ = bf16[40,896]{1,0:T(8,128)(2,1)S(1)} collective-permute-done((bf16[40,896]{1,0:T(8,128)(2,1)S(1)}, bf16[40,896]{1,0:T(8,128)(2,1)S(1)}, u32[]{:S(2)}, u32[]{:S(2)}) %collective-permute-start.2) | collective-permute-done | bytes 71712 | tf_op jit(solution)/shard_map/ppermute | solution.py:230
  15.0 0.0 collective-permute-done.3.refs_3_
  15.0 3.2 %collective-permute-done.4.refs_4_ = bf16[40,896]{1,0:T(8,128)(2,1)S(1)} collective-permute-done((bf16[40,896]{1,0:T(8,128)(2,1)S(1)}, bf16[40,896]{1,0:T(8,128)(2,1)S(1)}, u32[]{:S(2)}, u32[]{:S(2)}) %collective-permute-start.4) | collective-permute-done | bytes 71712 | tf_op jit(solution)/shard_map/ppermute | solution.py:230
  18.2 0.7 %collective-permute-done.5.refs_5_ = bf16[40,896]{1,0:T(8,128)(2,1)S(1)} collective-permute-done((bf16[40,896]{1,0:T(8,128)(2,1)S(1)}, bf16[40,896]{1,0:T(8,128)(2,1)S(1)}, u32[]{:S(2)}, u32[]{:S(2)}) %collective-permute-start.5) | collective-permute-done | bytes 71712 | tf_op jit(solution)/shard_map/ppermute | solution.py:230
  18.9 0.4 collective-permute-done.6.refs_6_
  19.3 0.0 copy-done
  19.3 0.0 copy-done.1
  19.3 0.0 slice-start
  19.3 1.4 %gate_up.3.refs_0_ = bf16[160,2048]{1,0:T(8,128)(2,1)S(1)} custom-call(bf16[40,896]{1,0:T(8,128)(2,1)S(1)} %collective-permute-done.refs_0_, bf16[40,896]{1,0:T(8,128)(2,1)S(1)} %collective-permute-done.1.refs_1_, bf16[40,896]{1,0:T(8,128)(2,1)S(1)} %collective-permute-done.2.refs_2_, bf16[40,896]{1,0:T(8,128)(2,1)S(1)} %collective-permute-done.3.refs_3_, ...), custom_call_target="tpu_custom_call" | custom-call | flops 1 | tf_op jit(solution)/shard_map/gate_up/pallas_call | solution.py:212
  20.7 0.0 slice-start.1
  20.7 0.1 collective-permute-start.8
  20.8 1.4 %gate_up.2.refs_0_ = bf16[160,2048]{1,0:T(8,128)(2,1)S(1)} custom-call(bf16[40,896]{1,0:T(8,128)(2,1)S(1)} %collective-permute-done.refs_0_, bf16[40,896]{1,0:T(8,128)(2,1)S(1)} %collective-permute-done.1.refs_1_, bf16[40,896]{1,0:T(8,128)(2,1)S(1)} %collective-permute-done.2.refs_2_, bf16[40,896]{1,0:T(8,128)(2,1)S(1)} %collective-permute-done.3.refs_3_, ...), custom_call_target="tpu_custom_call" | custom-call | flops 1 | tf_op jit(solution)/shard_map/gate_up/pallas_call | solution.py:212
  22.2 0.6 %collective-permute-start.7 = (bf16[160,2048]{1,0:T(8,128)(2,1)S(1)}, bf16[160,2048]{1,0:T(8,128)(2,1)S(1)}, u32[]{:S(2)}, u32[]{:S(2)}) collective-permute-start(bf16[160,2048]{1,0:T(8,128)(2,1)S(1)} %gate_up.2.refs_0_), channel_id=1, source_target_pairs={{0,1},{1,0},{2,3},{3,2},{4,5},{5,4},{6,7},{7,6},{8,9},{9,8},{10,11... | collective-permute-start | bytes 1966088 | tf_op jit(solution)/shard_map/ppermute | solution.py:230
  22.7 0.1 collective-permute-done.8.refs_1_
  22.9 0.0 slice-done
  22.9 0.0 slice-done.1
  22.9 0.9 %down_first.1.refs_3_ = f32[160,1792]{1,0:T(8,128)S(1)} custom-call(bf16[160,2048]{1,0:T(8,128)(2,1)S(1)} %gate_up.3.refs_0_, bf16[160,2048]{1,0:T(8,128)(2,1)S(1)} %collective-permute-done.8.refs_1_, bf16[2048,1792]{1,0:T(8,128)(2,1)S(1)} %bitcast.4), custom_call_target="tpu_custom_call" | custom-call | flops 1 | tf_op jit(solution)/shard_map/down_first/pallas_call | solution.py:212
  23.8 0.0 copy-start.2
  23.9 0.0 copy-start.3
  23.9 0.6 %collective-permute-done.7.refs_1_ = bf16[160,2048]{1,0:T(8,128)(2,1)S(1)} collective-permute-done((bf16[160,2048]{1,0:T(8,128)(2,1)S(1)}, bf16[160,2048]{1,0:T(8,128)(2,1)S(1)}, u32[]{:S(2)}, u32[]{:S(2)}) %collective-permute-start.7) | collective-permute-done | bytes 655392 | tf_op jit(solution)/shard_map/ppermute | solution.py:230
  24.5 1.0 %down_last.1 = (bf16[40,896]{1,0:T(8,128)(2,1)S(1)}, bf16[40,896]{1,0:T(8,128)(2,1)S(1)}, bf16[40,896]{1,0:T(8,128)(2,1)S(1)}, bf16[40,896]{1,0:T(8,128)(2,1)S(1...) custom-call(bf16[160,2048]{1,0:T(8,128)(2,1)S(1)} %gate_up.2.refs_0_, ...), custom_call_target="tpu_custom_call" | custom-call | flops 1 | tf_op jit(solution)/shard_map/down_last/pallas_call | solution.py:212
  25.4 0.9 %collective-permute-start.10 = (bf16[40,896]{1,0:T(8,128)(2,1)S(1)}, bf16[40,896]{1,0:T(8,128)(2,1)S(1)}, u32[]{:S(2)}, u32[]{:S(2)}) collective-permute-start(bf16[40,896]{1,0:T(8,128)(2,1)S(1)} %get-tuple-element.34), channel_id=1, source_target_pairs={{0,2},{2,0},{4,6},{6,4},{8,10},{10,8},{12,14},{14,12},{1,3},{3,1},... | collective-permute-start | bytes 215048 | tf_op jit(solution)/shard_map/ppermute | solution.py:230
  26.3 2.1 %collective-permute-start.11 = (bf16[40,896]{1,0:T(8,128)(2,1)S(1)}, bf16[40,896]{1,0:T(8,128)(2,1)S(1)}, u32[]{:S(2)}, u32[]{:S(2)}) collective-permute-start(bf16[40,896]{1,0:T(8,128)(2,1)S(1)} %get-tuple-element.35), channel_id=1, source_target_pairs={{0,8},{2,10},{4,12},{6,14},{8,0},{10,2},{12,4},{14,6},{1,9},{3,11}... | collective-permute-start | bytes 215048 | tf_op jit(solution)/shard_map/ppermute | solution.py:230
  28.4 1.4 %collective-permute-start.12 = (bf16[40,896]{1,0:T(8,128)(2,1)S(1)}, bf16[40,896]{1,0:T(8,128)(2,1)S(1)}, u32[]{:S(2)}, u32[]{:S(2)}) collective-permute-start(bf16[40,896]{1,0:T(8,128)(2,1)S(1)} %get-tuple-element.36), channel_id=1, source_target_pairs={{0,6},{2,4},{4,2},{6,0},{8,14},{10,12},{12,10},{14,8},{1,7},{3,5},... | collective-permute-start | bytes 215048 | tf_op jit(solution)/shard_map/ppermute | solution.py:230
  29.9 1.6 %collective-permute-start.13 = (bf16[40,896]{1,0:T(8,128)(2,1)S(1)}, bf16[40,896]{1,0:T(8,128)(2,1)S(1)}, u32[]{:S(2)}, u32[]{:S(2)}) collective-permute-start(bf16[40,896]{1,0:T(8,128)(2,1)S(1)} %get-tuple-element.37), channel_id=1, source_target_pairs={{0,10},{2,8},{4,14},{6,12},{8,2},{10,0},{12,6},{14,4},{1,11},{3,9}... | collective-permute-start | bytes 215048 | tf_op jit(solution)/shard_map/ppermute | solution.py:230
  31.5 3.2 %collective-permute-start.14 = (bf16[40,896]{1,0:T(8,128)(2,1)S(1)}, bf16[40,896]{1,0:T(8,128)(2,1)S(1)}, u32[]{:S(2)}, u32[]{:S(2)}) collective-permute-start(bf16[40,896]{1,0:T(8,128)(2,1)S(1)} %get-tuple-element.38), channel_id=1, source_target_pairs={{0,14},{2,12},{4,10},{6,8},{8,6},{10,4},{12,2},{14,0},{1,15},{3,13... | collective-permute-start | bytes 215048 | tf_op jit(solution)/shard_map/ppermute | solution.py:230
  34.7 0.0 collective-permute-done.10.refs_3_
  34.7 0.0 collective-permute-start.15
  34.7 0.0 collective-permute-done.11.refs_4_
  34.7 1.4 %collective-permute-start.9 = (bf16[40,896]{1,0:T(8,128)(2,1)S(1)}, bf16[40,896]{1,0:T(8,128)(2,1)S(1)}, u32[]{:S(2)}, u32[]{:S(2)}) collective-permute-start(bf16[40,896]{1,0:T(8,128)(2,1)S(1)} %get-tuple-element.33), channel_id=1, source_target_pairs={{0,12},{2,14},{4,8},{6,10},{8,4},{10,6},{12,0},{14,2},{1,13},{3,15... | collective-permute-start | bytes 215048 | tf_op jit(solution)/shard_map/ppermute | solution.py:230
  36.1 0.0 copy-done.2
  36.1 0.0 copy-done.3
  36.1 0.3 plan.1
  36.3 0.0 collective-permute-done.12.refs_5_
  36.3 3.9 %collective-permute-done.13.refs_6_ = bf16[40,896]{1,0:T(8,128)(2,1)S(1)} collective-permute-done((bf16[40,896]{1,0:T(8,128)(2,1)S(1)}, bf16[40,896]{1,0:T(8,128)(2,1)S(1)}, u32[]{:S(2)}, u32[]{:S(2)}) %collective-permute-start.13) | collective-permute-done | bytes 71712 | tf_op jit(solution)/shard_map/ppermute | solution.py:230
  40.2 0.0 collective-permute-done.14.refs_7_
  40.2 0.0 collective-permute-done.15.refs_8_
  40.2 0.7 %collective-permute-done.9.refs_2_ = bf16[40,896]{1,0:T(8,128)(2,1)S(1)} collective-permute-done((bf16[40,896]{1,0:T(8,128)(2,1)S(1)}, bf16[40,896]{1,0:T(8,128)(2,1)S(1)}, u32[]{:S(2)}, u32[]{:S(2)}) %collective-permute-start.9) | collective-permute-done | bytes 71712 | tf_op jit(solution)/shard_map/ppermute | solution.py:230
  41.0 1.1 %combine.1 = bf16[64,1792]{1,0:T(8,128)(2,1)} custom-call(bf16[256,320]{1,0:T(8,128)(2,1)S(1)} %get-tuple-element.23.refs_0_, f32[128,128]{1,0:T(8,128)S(1)} %get-tuple-element.24.refs_1_, bf16[40,896]{1,0:T(8,128)(2,1)S(1)} %collective-permute-done.9.refs_2_, bf16[40,896]{1,0:T(8,128)(2,1)S(1)} %collective-permute-done.10.refs_3_, ...), custom_call_target="tpu_custom_call" | custom-call | tf_op jit(solution)/shard_map/combine/pallas_call | solution.py:315
  (1 shorter events, 0.0 us)
Async XLA Ops:
  0.0 19.3 %copy-start = (bf16[1792,2048]{1,0:T(8,128)(2,1)S(1)}, bf16[1792,2048]{1,0:T(8,128)(2,1)}, u32[]{:S(2)}) copy-start(bf16[1792,2048]{1,0:T(8,128)(2,1)} %refs_8_.3) | copy-start | bytes 22020100
  0.0 19.3 %copy-start.1 = (bf16[1792,2048]{1,0:T(8,128)(2,1)S(1)}, bf16[1792,2048]{1,0:T(8,128)(2,1)}, u32[]{:S(2)}) copy-start(bf16[1792,2048]{1,0:T(8,128)(2,1)} %refs_9_.3) | copy-start | bytes 22020100
  1.6 10.0 %collective-permute-start = (bf16[40,896]{1,0:T(8,128)(2,1)S(1)}, bf16[40,896]{1,0:T(8,128)(2,1)S(1)}, u32[]{:S(2)}, u32[]{:S(2)}) collective-permute-start(bf16[40,896]{1,0:T(8,128)(2,1)S(1)} %get-tuple-element.25), channel_id=1, source_target_pairs={{0,12},{2,14},{4,8},{6,10},{8,4},{10,6},{12,0},{14,2},{1,13},{3,15... | collective-permute-start | bytes 215048 | tf_op jit(solution)/shard_map/ppermute | solution.py:230
  6.7 7.8 %collective-permute-start.1 = (bf16[40,896]{1,0:T(8,128)(2,1)S(1)}, bf16[40,896]{1,0:T(8,128)(2,1)S(1)}, u32[]{:S(2)}, u32[]{:S(2)}) collective-permute-start(bf16[40,896]{1,0:T(8,128)(2,1)S(1)} %get-tuple-element.26), channel_id=1, source_target_pairs={{0,2},{2,0},{4,6},{6,4},{8,10},{10,8},{12,14},{14,12},{1,3},{3,1},... | collective-permute-start | bytes 215048 | tf_op jit(solution)/shard_map/ppermute | solution.py:230
  8.2 6.8 %collective-permute-start.2 = (bf16[40,896]{1,0:T(8,128)(2,1)S(1)}, bf16[40,896]{1,0:T(8,128)(2,1)S(1)}, u32[]{:S(2)}, u32[]{:S(2)}) collective-permute-start(bf16[40,896]{1,0:T(8,128)(2,1)S(1)} %get-tuple-element.27), channel_id=1, source_target_pairs={{0,8},{2,10},{4,12},{6,14},{8,0},{10,2},{12,4},{14,6},{1,9},{3,11}... | collective-permute-start | bytes 215048 | tf_op jit(solution)/shard_map/ppermute | solution.py:230
  8.2 6.8 %collective-permute-start.3 = (bf16[40,896]{1,0:T(8,128)(2,1)S(1)}, bf16[40,896]{1,0:T(8,128)(2,1)S(1)}, u32[]{:S(2)}, u32[]{:S(2)}) collective-permute-start(bf16[40,896]{1,0:T(8,128)(2,1)S(1)} %get-tuple-element.28), channel_id=1, source_target_pairs={{0,6},{2,4},{4,2},{6,0},{8,14},{10,12},{12,10},{14,8},{1,7},{3,5},... | collective-permute-start | bytes 215048 | tf_op jit(solution)/shard_map/ppermute | solution.py:230
  8.8 9.4 %collective-permute-start.4 = (bf16[40,896]{1,0:T(8,128)(2,1)S(1)}, bf16[40,896]{1,0:T(8,128)(2,1)S(1)}, u32[]{:S(2)}, u32[]{:S(2)}) collective-permute-start(bf16[40,896]{1,0:T(8,128)(2,1)S(1)} %get-tuple-element.29), channel_id=1, source_target_pairs={{0,10},{2,8},{4,14},{6,12},{8,2},{10,0},{12,6},{14,4},{1,11},{3,9}... | collective-permute-start | bytes 215048 | tf_op jit(solution)/shard_map/ppermute | solution.py:230
  11.6 7.3 %collective-permute-start.5 = (bf16[40,896]{1,0:T(8,128)(2,1)S(1)}, bf16[40,896]{1,0:T(8,128)(2,1)S(1)}, u32[]{:S(2)}, u32[]{:S(2)}) collective-permute-start(bf16[40,896]{1,0:T(8,128)(2,1)S(1)} %get-tuple-element.30), channel_id=1, source_target_pairs={{0,14},{2,12},{4,10},{6,8},{8,6},{10,4},{12,2},{14,0},{1,15},{3,13... | collective-permute-start | bytes 215048 | tf_op jit(solution)/shard_map/ppermute | solution.py:230
  14.5 4.8 %collective-permute-start.6 = (bf16[40,896]{1,0:T(8,128)(2,1)S(1)}, bf16[40,896]{1,0:T(8,128)(2,1)S(1)}, u32[]{:S(2)}, u32[]{:S(2)}) collective-permute-start(bf16[40,896]{1,0:T(8,128)(2,1)S(1)} %get-tuple-element.31), channel_id=1, source_target_pairs={{0,4},{2,6},{4,0},{6,2},{8,12},{10,14},{12,8},{14,10},{1,5},{3,7},... | collective-permute-start | bytes 215048 | tf_op jit(solution)/shard_map/ppermute | solution.py:230
  19.3 3.6 %slice-start = ((s8[7340032]{0:T(1024)(128)(4,1)}), s8[4194304]{0:T(1024)(128)(4,1)S(1)}, s32[]{:S(2)}) async-start(s8[7340032]{0:T(1024)(128)(4,1)} %bitcast.3), calls=%async_computation | async-start | bytes 8388608
  20.7 2.2 %slice-start.1 = ((s8[7340032]{0:T(1024)(128)(4,1)}), s8[3145728]{0:T(1024)(128)(4,1)S(1)}, s32[]{:S(2)}) async-start(s8[7340032]{0:T(1024)(128)(4,1)} %bitcast.3), calls=%async_computation.1 | async-start | bytes 6291456
  20.7 2.2 %collective-permute-start.8 = (bf16[160,2048]{1,0:T(8,128)(2,1)S(1)}, bf16[160,2048]{1,0:T(8,128)(2,1)S(1)}, u32[]{:S(2)}, u32[]{:S(2)}) collective-permute-start(bf16[160,2048]{1,0:T(8,128)(2,1)S(1)} %gate_up.3.refs_0_), channel_id=1, source_target_pairs={{0,1},{1,0},{2,3},{3,2},{4,5},{5,4},{6,7},{7,6},{8,9},{9,8},{10,11... | collective-permute-start | bytes 1966088 | tf_op jit(solution)/shard_map/ppermute | solution.py:230
  22.2 2.3 %collective-permute-start.7 = (bf16[160,2048]{1,0:T(8,128)(2,1)S(1)}, bf16[160,2048]{1,0:T(8,128)(2,1)S(1)}, u32[]{:S(2)}, u32[]{:S(2)}) collective-permute-start(bf16[160,2048]{1,0:T(8,128)(2,1)S(1)} %gate_up.2.refs_0_), channel_id=1, source_target_pairs={{0,1},{1,0},{2,3},{3,2},{4,5},{5,4},{6,7},{7,6},{8,9},{9,8},{10,11... | collective-permute-start | bytes 1966088 | tf_op jit(solution)/shard_map/ppermute | solution.py:230
  23.8 12.2 %copy-start.2 = (s32[64,2]{0,1:T(2,128)S(1)}, s32[64,2]{0,1:T(2,128)}, u32[]{:S(2)}) copy-start(s32[64,2]{0,1:T(2,128)} %param.7) | copy-start | bytes 1540
  23.9 12.2 %copy-start.3 = (f32[64,2]{0,1:T(2,128)S(1)}, f32[64,2]{0,1:T(2,128)}, u32[]{:S(2)}) copy-start(f32[64,2]{0,1:T(2,128)} %param.8) | copy-start | bytes 1540
  25.4 9.2 %collective-permute-start.10 = (bf16[40,896]{1,0:T(8,128)(2,1)S(1)}, bf16[40,896]{1,0:T(8,128)(2,1)S(1)}, u32[]{:S(2)}, u32[]{:S(2)}) collective-permute-start(bf16[40,896]{1,0:T(8,128)(2,1)S(1)} %get-tuple-element.34), channel_id=1, source_target_pairs={{0,2},{2,0},{4,6},{6,4},{8,10},{10,8},{12,14},{14,12},{1,3},{3,1},... | collective-permute-start | bytes 215048 | tf_op jit(solution)/shard_map/ppermute | solution.py:230
  26.3 8.3 %collective-permute-start.11 = (bf16[40,896]{1,0:T(8,128)(2,1)S(1)}, bf16[40,896]{1,0:T(8,128)(2,1)S(1)}, u32[]{:S(2)}, u32[]{:S(2)}) collective-permute-start(bf16[40,896]{1,0:T(8,128)(2,1)S(1)} %get-tuple-element.35), channel_id=1, source_target_pairs={{0,8},{2,10},{4,12},{6,14},{8,0},{10,2},{12,4},{14,6},{1,9},{3,11}... | collective-permute-start | bytes 215048 | tf_op jit(solution)/shard_map/ppermute | solution.py:230
  28.4 7.9 %collective-permute-start.12 = (bf16[40,896]{1,0:T(8,128)(2,1)S(1)}, bf16[40,896]{1,0:T(8,128)(2,1)S(1)}, u32[]{:S(2)}, u32[]{:S(2)}) collective-permute-start(bf16[40,896]{1,0:T(8,128)(2,1)S(1)} %get-tuple-element.36), channel_id=1, source_target_pairs={{0,6},{2,4},{4,2},{6,0},{8,14},{10,12},{12,10},{14,8},{1,7},{3,5},... | collective-permute-start | bytes 215048 | tf_op jit(solution)/shard_map/ppermute | solution.py:230
  29.9 10.3 %collective-permute-start.13 = (bf16[40,896]{1,0:T(8,128)(2,1)S(1)}, bf16[40,896]{1,0:T(8,128)(2,1)S(1)}, u32[]{:S(2)}, u32[]{:S(2)}) collective-permute-start(bf16[40,896]{1,0:T(8,128)(2,1)S(1)} %get-tuple-element.37), channel_id=1, source_target_pairs={{0,10},{2,8},{4,14},{6,12},{8,2},{10,0},{12,6},{14,4},{1,11},{3,9}... | collective-permute-start | bytes 215048 | tf_op jit(solution)/shard_map/ppermute | solution.py:230
  31.5 8.8 %collective-permute-start.14 = (bf16[40,896]{1,0:T(8,128)(2,1)S(1)}, bf16[40,896]{1,0:T(8,128)(2,1)S(1)}, u32[]{:S(2)}, u32[]{:S(2)}) collective-permute-start(bf16[40,896]{1,0:T(8,128)(2,1)S(1)} %get-tuple-element.38), channel_id=1, source_target_pairs={{0,14},{2,12},{4,10},{6,8},{8,6},{10,4},{12,2},{14,0},{1,15},{3,13... | collective-permute-start | bytes 215048 | tf_op jit(solution)/shard_map/ppermute | solution.py:230
  34.7 5.6 %collective-permute-start.15 = (bf16[40,896]{1,0:T(8,128)(2,1)S(1)}, bf16[40,896]{1,0:T(8,128)(2,1)S(1)}, u32[]{:S(2)}, u32[]{:S(2)}) collective-permute-start(bf16[40,896]{1,0:T(8,128)(2,1)S(1)} %get-tuple-element.39), channel_id=1, source_target_pairs={{0,4},{2,6},{4,0},{6,2},{8,12},{10,14},{12,8},{14,10},{1,5},{3,7},... | collective-permute-start | bytes 215048 | tf_op jit(solution)/shard_map/ppermute | solution.py:230
  34.7 6.3 %collective-permute-start.9 = (bf16[40,896]{1,0:T(8,128)(2,1)S(1)}, bf16[40,896]{1,0:T(8,128)(2,1)S(1)}, u32[]{:S(2)}, u32[]{:S(2)}) collective-permute-start(bf16[40,896]{1,0:T(8,128)(2,1)S(1)} %get-tuple-element.33), channel_id=1, source_target_pairs={{0,12},{2,14},{4,8},{6,10},{8,4},{10,6},{12,0},{14,2},{1,13},{3,15... | collective-permute-start | bytes 215048 | tf_op jit(solution)/shard_map/ppermute | solution.py:230

commit v4 on v3

--- a/solution.py
+++ b/solution.py
@@ -11,8 +11,11 @@
 VMEM_SPEC = pl.BlockSpec(memory_space=pltpu.VMEM)
 SMEM_SPEC = pl.BlockSpec(memory_space=pltpu.SMEM)
 PIECES = (2,)
-BATCHES = ((6, 1, 4, 3, 5, 7, 2, 0),)
+PIECES = (1024, 512, 512)
 STARTS = (6, 1, 4, 3, 5, 7, 2, 0)
+ROWS = (6, 1, 4, 3, 5, 7, 2, 0)
+RETURNS = (6, 1, 4, 3, 5, 7, 2, 0)
+PLACES = (6, 1, 4, 3, 5, 7, 2, 0)
 
 
 def pair_slots(id_blocks, expert_count):
@@ -109,47 +112,59 @@
         out_ref[...] = packed[o * 2 * cap : (o + 1) * 2 * cap].astype(BF16)
 
 
-def gate_up_kernel(cap, piece, *refs):
-    blocks, (wg_ref, wu_ref, out_ref, x_ref) = refs[:-4], refs[-4:]
+def gate_up(x_ref, wg_ref, wu_ref, out_ref, start):
+    width = out_ref.shape[1] // 2
+    tile = 256
+    for which, w_ref in enumerate((wg_ref, wu_ref)):
+        for j in range(width // tile):
+            columns = pl.ds(start + j * tile, tile)
+            out_ref[:, pl.ds(which * width + j * tile, tile)] = jnp.dot(
+                x_ref[...], w_ref[:, columns], preferred_element_type=F32
+            ).astype(BF16)
+
+
+def gate_up_first_kernel(cap, *refs):
+    blocks, (wg_ref, wu_ref, _, out_ref, x_ref) = refs[:-5], refs[-5:]
     half = blocks[0].shape[1]
     for i, block in enumerate(blocks):
         x_ref[pl.ds(i * cap, cap), :half] = block[:cap, :]
         x_ref[pl.ds(i * cap, cap), half:] = block[cap:, :]
-    width = out_ref.shape[1] // 2
-    tile = min(512, width)
-    for which, w_ref in enumerate((wg_ref, wu_ref)):
-        for j in range(width // tile):
-            columns = pl.ds(piece * width + j * tile, tile)
-            out_ref[:, pl.ds(which * width + j * tile, tile)] = jnp.dot(
-                x_ref[...], w_ref[:, columns], preferred_element_type=F32
-            ).astype(BF16)
-
-
-def hidden_of(own_ref, other_ref):
+    gate_up(x_ref, wg_ref, wu_ref, out_ref, 0)
+
+
+def gate_up_next_kernel(start, x_ref, wg_ref, wu_ref, out_ref):
+    gate_up(x_ref, wg_ref, wu_ref, out_ref, start)
+
+
+def hidden_of(own_ref, other_ref, low, count):
     width = own_ref.shape[1] // 2
-    gate = own_ref[:, :width].astype(F32) + other_ref[:, :width].astype(F32)
-    up = own_ref[:, width:].astype(F32) + other_ref[:, width:].astype(F32)
+    gates, ups = pl.ds(low, count), pl.ds(width + low, count)
+    gate = own_ref[:, gates].astype(F32) + other_ref[:, gates].astype(F32)
+    up = own_ref[:, ups].astype(F32) + other_ref[:, ups].astype(F32)
     return (gate / (1.0 + jnp.exp(-gate)) * up).astype(BF16)
 
 
 def down_first_kernel(count, *refs):
     own, other, (wd_ref, acc_ref) = refs[:count], refs[count : 2 * count], refs[2 * count :]
-    total = None
+    total, start = None, 0
     for i in range(count):
-        hidden = hidden_of(own[i], other[i])
-        depth = hidden.shape[1]
-        term = jnp.dot(hidden, wd_ref[pl.ds(i * depth, depth), :], preferred_element_type=F32)
-        total = term if total is None else total + term
+        width = own[i].shape[1] // 2
+        for low in range(0, width, 512):
+            hidden = hidden_of(own[i], other[i], low, 512)
+            term = jnp.dot(hidden, wd_ref[pl.ds(start, 512), :], preferred_element_type=F32)
+            total = term if total is None else total + term
+            start += 512
     acc_ref[...] = total
 
 
 def down_last_kernel(cap, own_ref, other_ref, wd_ref, acc_ref, *out_refs):
-    hidden = hidden_of(own_ref, other_ref)
+    hidden = hidden_of(own_ref, other_ref, 0, own_ref.shape[1] // 2)
     out = acc_ref[...] + jnp.dot(
         hidden, wd_ref[wd_ref.shape[0] - hidden.shape[1] :, :], preferred_element_type=F32
     )
     half = out.shape[1] // 2
-    for i, out_ref in enumerate(out_refs):
+    for o, out_ref in zip(RETURNS, out_refs):
+        i = ROWS.index(o)
         out_ref[:cap, :] = out[i * cap : (i + 1) * cap, :half].astype(BF16)
         out_ref[cap:, :] = out[i * cap : (i + 1) * cap, half:].astype(BF16)
 
@@ -230,37 +245,44 @@
     return lax.ppermute(x, axis, [(i, i ^ distance) for i in range(lax.axis_size(axis))])
 
 
-def experts(blocks, after, pieces, cap, w_gate, w_up, w_down):
-    rows, width, hidden_units = len(blocks) * cap, 2 * blocks[0].shape[1], w_gate.shape[1]
-    piece_width = hidden_units // pieces
-    own, other = [], []
-    for piece in range(pieces):
-        own.append(
-            call(
-                lambda *refs, piece=piece: gate_up_kernel(cap, piece, *refs[len(after) :]),
-                jax.ShapeDtypeStruct((rows, 2 * piece_width), BF16),
-                [*after, *blocks, w_gate, w_up],
-                scratch=[pltpu.VMEM((rows, width), BF16)],
+def experts(blocks, cap, w_gate, w_up, w_down):
+    rows, width = len(blocks) * cap, 2 * blocks[0].shape[1]
+    own, other, start = [], [], 0
+    for piece in PIECES:
+        out = jax.ShapeDtypeStruct((rows, 2 * piece), BF16)
+        if start == 0:
+            part, x = call(
+                lambda *refs: gate_up_first_kernel(cap, *refs),
+                [out, jax.ShapeDtypeStruct((rows, width), BF16)],
+                [*blocks, w_gate, w_up, w_down],
                 cost=estimate(),
-                name="gate_up",
+                name="gate_up_first",
             )
-        )
-        other.append(swap(own[-1], "tensor", 1))
+        else:
+            part = call(
+                lambda *refs, start=start: gate_up_next_kernel(start, *refs),
+                out,
+                [x, w_gate, w_up],
+                cost=estimate(),
+                name="gate_up_next",
+            )
+        own.append(part)
+        other.append(swap(part, "tensor", 1))
+        start += piece
     acc = call(
-        lambda *refs: down_first_kernel(pieces - 1, *refs),
+        lambda *refs: down_first_kernel(len(PIECES) - 1, *refs),
         jax.ShapeDtypeStruct((rows, width), F32),
         [*own[:-1], *other[:-1], w_down],
         cost=estimate(),
         name="down_first",
     )
-    results = call(
+    return call(
         lambda *refs: down_last_kernel(cap, *refs),
         [jax.ShapeDtypeStruct(b.shape, b.dtype) for b in blocks],
         [own[-1], other[-1], w_down, acc],
         cost=estimate(),
         name="down_last",
     )
-    return results, own
 
 
 def estimate():
@@ -292,14 +314,8 @@
         name="dispatch",
     )
     received = {o: swap(x, "expert", o) for o, x in zip(STARTS, sent)}
-    returned = {}
-    after = []
-    for batch, pieces in zip(BATCHES, PIECES):
-        results, after = experts(
-            [received[o] for o in batch], after, pieces, cap, w_gate, w_up, w_down
-        )
-        for o, x in zip(batch, results):
-            returned[o] = swap(x, "expert", o)
+    results = experts([received[o] for o in ROWS], cap, w_gate, w_up, w_down)
+    returned = {o: swap(x, "expert", o) for o, x in zip(RETURNS, results)}
     pick, scale = call(
         lambda *refs: plan_kernel(n, cap, *refs),
         [
@@ -311,9 +327,8 @@
         cost=estimate(),
         name="plan",
     )
-    places = [o for batch in BATCHES for o in batch]
     return pl.pallas_call(
-        lambda *refs: combine_kernel(cap, places, *refs),
+        lambda *refs: combine_kernel(cap, PLACES, *refs),
         out_shape=jax.ShapeDtypeStruct((tok_rows, width), BF16),
         in_specs=[VMEM_SPEC] * (2 + n),
         out_specs=pl.BlockSpec(memory_space=pl.ANY),
@@ -324,7 +339,7 @@
         ],
         compiler_params=pltpu.CompilerParams(vmem_limit_bytes=20 << 20),
         name="combine",
-    )(*(in_vmem(x) for x in (pick, scale, *(returned[o] for o in places))))
+    )(*(in_vmem(x) for x in (pick, scale, *(returned[o] for o in PLACES))))
 
 
 def per_device(tokens, expert_ids, gate_weights, w_gate, w_up, w_down):

time: 42.2 us -> 41.7 us (0.988)
  waiting for transfers between devices: 10.1 us -> 9.43 us
    ppermute x16 -> x17, waiting for transfers between devices: 10.1 us -> 9.43 us  [swap(): lax.ppermute(x, axis, [(i, i ^ distance) for i in range(lax.axis_size(axi...]
    ppermute x16 -> x17, starting transfers between devices: 24.2 us -> 24.5 us  [swap(): lax.ppermute(x, axis, [(i, i ^ distance) for i in range(lax.axis_size(axi...]
    pallas_call x6 -> x7, Pallas kernels: 6.46 us -> 6.42 us  [call(): pl.pallas_call(kernel, out_shape=[pltpu.VMEM(o.shape, o.dtype) for o in (...]
  transfers between devices with their start and end apart: 16 -> 17, of which waited for: 8 -> 8; matrix products, arithmetic and copies ran while one was open for 0% -> 0% of each run, Pallas kernels for 6% -> 7%
where the time goes in v4:
time: 41.7 us; the launch traced here: 41.5 us
  starting transfers between devices  24.5 us (59%)
  waiting for transfers between devices  9.43 us (23%)
  Pallas kernels  7.5 us (18%)
    ppermute x17, starting transfers between devices, swap(): lax.ppermute(x, axis, [(i, i ^ distance) for i in range(lax.axis_size(axi...  24.5 us
    ppermute x17, waiting for transfers between devices, swap(): lax.ppermute(x, axis, [(i, i ^ distance) for i in range(lax.axis_size(axi...  9.43 us
    pallas_call x7, Pallas kernels, call(): pl.pallas_call(kernel, out_shape=[pltpu.VMEM(o.shape, o.dtype) for o in (...  6.42 us
    pallas_call x1, Pallas kernels, one_expert_each(): pl.pallas_call(lambda *refs: combine_kernel(cap, PLACES, *refs), out_shap...  1.08 us
  transfers between devices with their start and end apart: 17, of which 8 were waited for; matrix products, arithmetic and copies ran while one was open for 0% of the time, Pallas kernels for 7%

profile of v4, /device:TPU:0, one launch (start us, length us, event | category | flops | bytes accessed | tf_op | source)
XLA Modules:
  0.0 41.5 jit_solution(4449091345086051123)
XLA Ops:
  0.0 0.0 copy-start
  0.0 0.0 copy-start.1
  0.0 0.0 copy-start.2
  0.0 1.6 %dispatch.1 = (bf16[40,896]{1,0:T(8,128)(2,1)S(1)}, bf16[40,896]{1,0:T(8,128)(2,1)S(1)}, bf16[40,896]{1,0:T(8,128)(2,1)S(1)}, bf16[40,896]{1,0:T(8,128)(2,1)S(1)...) custom-call(s32[1]{0:T(128)} %bitcast.refs_0_, ...), custom_call_target="tpu_custom_call" | custom-call | flops 20000000000 | bytes 44040192 | tf_op jit(solution)/shard_map/dispatch/pallas_call | solution.py:227
  1.6 5.1 %collective-permute-start = (bf16[40,896]{1,0:T(8,128)(2,1)S(1)}, bf16[40,896]{1,0:T(8,128)(2,1)S(1)}, u32[]{:S(2)}, u32[]{:S(2)}) collective-permute-start(bf16[40,896]{1,0:T(8,128)(2,1)S(1)} %get-tuple-element.27), channel_id=1, source_target_pairs={{0,12},{2,14},{4,8},{6,10},{8,4},{10,6},{12,0},{14,2},{1,13},{3,15... | collective-permute-start | bytes 215048 | tf_op jit(solution)/shard_map/ppermute | solution.py:245
  6.7 1.5 %collective-permute-start.1 = (bf16[40,896]{1,0:T(8,128)(2,1)S(1)}, bf16[40,896]{1,0:T(8,128)(2,1)S(1)}, u32[]{:S(2)}, u32[]{:S(2)}) collective-permute-start(bf16[40,896]{1,0:T(8,128)(2,1)S(1)} %get-tuple-element.28), channel_id=1, source_target_pairs={{0,2},{2,0},{4,6},{6,4},{8,10},{10,8},{12,14},{14,12},{1,3},{3,1},... | collective-permute-start | bytes 215048 | tf_op jit(solution)/shard_map/ppermute | solution.py:245
  8.2 0.0 collective-permute-start.2
  8.2 0.6 %collective-permute-start.3 = (bf16[40,896]{1,0:T(8,128)(2,1)S(1)}, bf16[40,896]{1,0:T(8,128)(2,1)S(1)}, u32[]{:S(2)}, u32[]{:S(2)}) collective-permute-start(bf16[40,896]{1,0:T(8,128)(2,1)S(1)} %get-tuple-element.30), channel_id=1, source_target_pairs={{0,6},{2,4},{4,2},{6,0},{8,14},{10,12},{12,10},{14,8},{1,7},{3,5},... | collective-permute-start | bytes 215048 | tf_op jit(solution)/shard_map/ppermute | solution.py:245
  8.8 2.8 %collective-permute-start.4 = (bf16[40,896]{1,0:T(8,128)(2,1)S(1)}, bf16[40,896]{1,0:T(8,128)(2,1)S(1)}, u32[]{:S(2)}, u32[]{:S(2)}) collective-permute-start(bf16[40,896]{1,0:T(8,128)(2,1)S(1)} %get-tuple-element.31), channel_id=1, source_target_pairs={{0,10},{2,8},{4,14},{6,12},{8,2},{10,0},{12,6},{14,4},{1,11},{3,9}... | collective-permute-start | bytes 215048 | tf_op jit(solution)/shard_map/ppermute | solution.py:245
  11.6 0.0 collective-permute-done.refs_0_
  11.6 3.0 %collective-permute-start.5 = (bf16[40,896]{1,0:T(8,128)(2,1)S(1)}, bf16[40,896]{1,0:T(8,128)(2,1)S(1)}, u32[]{:S(2)}, u32[]{:S(2)}) collective-permute-start(bf16[40,896]{1,0:T(8,128)(2,1)S(1)} %get-tuple-element.32), channel_id=1, source_target_pairs={{0,14},{2,12},{4,10},{6,8},{8,6},{10,4},{12,2},{14,0},{1,15},{3,13... | collective-permute-start | bytes 215048 | tf_op jit(solution)/shard_map/ppermute | solution.py:245
  14.5 0.0 collective-permute-done.1.refs_1_
  14.5 0.0 collective-permute-start.6
  14.5 0.5 %collective-permute-done.2.refs_2_ = bf16[40,896]{1,0:T(8,128)(2,1)S(1)} collective-permute-done((bf16[40,896]{1,0:T(8,128)(2,1)S(1)}, bf16[40,896]{1,0:T(8,128)(2,1)S(1)}, u32[]{:S(2)}, u32[]{:S(2)}) %collective-permute-start.2) | collective-permute-done | bytes 71712 | tf_op jit(solution)/shard_map/ppermute | solution.py:245
  15.0 0.0 collective-permute-done.3.refs_3_
  15.0 3.2 %collective-permute-done.4.refs_4_ = bf16[40,896]{1,0:T(8,128)(2,1)S(1)} collective-permute-done((bf16[40,896]{1,0:T(8,128)(2,1)S(1)}, bf16[40,896]{1,0:T(8,128)(2,1)S(1)}, u32[]{:S(2)}, u32[]{:S(2)}) %collective-permute-start.4) | collective-permute-done | bytes 71712 | tf_op jit(solution)/shard_map/ppermute | solution.py:245
  18.2 0.7 %collective-permute-done.5.refs_5_ = bf16[40,896]{1,0:T(8,128)(2,1)S(1)} collective-permute-done((bf16[40,896]{1,0:T(8,128)(2,1)S(1)}, bf16[40,896]{1,0:T(8,128)(2,1)S(1)}, u32[]{:S(2)}, u32[]{:S(2)}) %collective-permute-start.5) | collective-permute-done | bytes 71712 | tf_op jit(solution)/shard_map/ppermute | solution.py:245
  18.9 0.4 collective-permute-done.6.refs_6_
  19.3 0.0 copy-done
  19.3 0.0 copy-done.1
  19.3 0.0 copy-done.2
  19.3 1.4 %gate_up_first.1 = (bf16[160,2048]{1,0:T(8,128)(2,1)S(1)}, bf16[160,1792]{1,0:T(8,128)(2,1)S(1)}) custom-call(bf16[40,896]{1,0:T(8,128)(2,1)S(1)} %collective-permute-done.refs_0_, bf16[40,896]{1,0:T(8,128)(2,1)S(1)} %collective-permute-done.1.refs_1_, bf16[40,896]{1,0:T(8,128)(2,1)S(1)} %collective-permute-done.2.refs_2_, ...), custom_call_target="tpu_custom_call" | custom-call | flops 1 | tf_op jit(solution)/shard_map/gate_up_first/pallas_call | solution.py:227
  20.7 0.1 collective-permute-start.8
  20.8 0.8 %gate_up_next.3.refs_1_ = bf16[160,1024]{1,0:T(8,128)(2,1)S(1)} custom-call(bf16[160,1792]{1,0:T(8,128)(2,1)S(1)} %get-tuple-element.35.refs_0_, bf16[1792,2048]{1,0:T(8,128)(2,1)S(1)} %copy-done, bf16[1792,2048]{1,0:T(8,128)(2,1)S(1)} %copy-done.1), custom_call_target="tpu_custom_call" | custom-call | flops 1 | tf_op jit(solution)/shard_map/gate_up_next/pallas_call | solution.py:227
  21.6 0.6 %collective-permute-start.9 = (bf16[160,1024]{1,0:T(8,128)(2,1)S(1)}, bf16[160,1024]{1,0:T(8,128)(2,1)S(1)}, u32[]{:S(2)}, u32[]{:S(2)}) collective-permute-start(bf16[160,1024]{1,0:T(8,128)(2,1)S(1)} %gate_up_next.3.refs_1_), channel_id=1, source_target_pairs={{0,1},{1,0},{2,3},{3,2},{4,5},{5,4},{6,7},{7,6},{8,9},{9,8},{10,11... | collective-permute-start | bytes 983048 | tf_op jit(solution)/shard_map/ppermute | solution.py:245
  22.1 0.8 %gate_up_next.2.refs_0_ = bf16[160,1024]{1,0:T(8,128)(2,1)S(1)} custom-call(bf16[160,1792]{1,0:T(8,128)(2,1)S(1)} %get-tuple-element.35.refs_0_, bf16[1792,2048]{1,0:T(8,128)(2,1)S(1)} %copy-done, bf16[1792,2048]{1,0:T(8,128)(2,1)S(1)} %copy-done.1), custom_call_target="tpu_custom_call" | custom-call | flops 1 | tf_op jit(solution)/shard_map/gate_up_next/pallas_call | solution.py:227
  22.9 0.0 copy-start.3
  22.9 0.0 copy-start.4
  22.9 0.1 collective-permute-start.7
  23.0 0.4 collective-permute-done.9.refs_3_
  23.4 0.0 collective-permute-done.8.refs_2_
  23.4 1.1 %down_first.1.refs_3_ = f32[160,1792]{1,0:T(8,128)S(1)} custom-call(bf16[160,2048]{1,0:T(8,128)(2,1)S(1)} %get-tuple-element.36.refs_0_, bf16[160,1024]{1,0:T(8,128)(2,1)S(1)} %gate_up_next.3.refs_1_, bf16[160,2048]{1,0:T(8,128)(2,1)S(1)} %collective-permute-done.8.refs_2_, bf16[160,1024]{1,0:T(8,128)(2,1)S(1)} %collective-permute-done.9.refs_3_, ...), custom_call_target="tpu_custom_call" | custom-call | flops 1 | tf_op jit(solution)/shard_map/down_first/pallas_call | solution.py:227
  24.5 0.1 collective-permute-done.7.refs_1_
  24.6 0.6 %down_last.1 = (bf16[40,896]{1,0:T(8,128)(2,1)S(1)}, bf16[40,896]{1,0:T(8,128)(2,1)S(1)}, bf16[40,896]{1,0:T(8,128)(2,1)S(1)}, bf16[40,896]{1,0:T(8,128)(2,1)S(1...) custom-call(bf16[160,1024]{1,0:T(8,128)(2,1)S(1)} %gate_up_next.2.re, ...), custom_call_target="tpu_custom_call" | custom-call | flops 1 | tf_op jit(solution)/shard_map/down_last/pallas_call | solution.py:227
  25.2 2.4 %collective-permute-start.10 = (bf16[40,896]{1,0:T(8,128)(2,1)S(1)}, bf16[40,896]{1,0:T(8,128)(2,1)S(1)}, u32[]{:S(2)}, u32[]{:S(2)}) collective-permute-start(bf16[40,896]{1,0:T(8,128)(2,1)S(1)} %get-tuple-element.37), channel_id=1, source_target_pairs={{0,12},{2,14},{4,8},{6,10},{8,4},{10,6},{12,0},{14,2},{1,13},{3,15... | collective-permute-start | bytes 215048 | tf_op jit(solution)/shard_map/ppermute | solution.py:245
  27.6 0.8 %collective-permute-start.11 = (bf16[40,896]{1,0:T(8,128)(2,1)S(1)}, bf16[40,896]{1,0:T(8,128)(2,1)S(1)}, u32[]{:S(2)}, u32[]{:S(2)}) collective-permute-start(bf16[40,896]{1,0:T(8,128)(2,1)S(1)} %get-tuple-element.38), channel_id=1, source_target_pairs={{0,2},{2,0},{4,6},{6,4},{8,10},{10,8},{12,14},{14,12},{1,3},{3,1},... | collective-permute-start | bytes 215048 | tf_op jit(solution)/shard_map/ppermute | solution.py:245
  28.4 0.5 %collective-permute-start.12 = (bf16[40,896]{1,0:T(8,128)(2,1)S(1)}, bf16[40,896]{1,0:T(8,128)(2,1)S(1)}, u32[]{:S(2)}, u32[]{:S(2)}) collective-permute-start(bf16[40,896]{1,0:T(8,128)(2,1)S(1)} %get-tuple-element.39), channel_id=1, source_target_pairs={{0,8},{2,10},{4,12},{6,14},{8,0},{10,2},{12,4},{14,6},{1,9},{3,11}... | collective-permute-start | bytes 215048 | tf_op jit(solution)/shard_map/ppermute | solution.py:245
  28.8 2.3 %collective-permute-start.13 = (bf16[40,896]{1,0:T(8,128)(2,1)S(1)}, bf16[40,896]{1,0:T(8,128)(2,1)S(1)}, u32[]{:S(2)}, u32[]{:S(2)}) collective-permute-start(bf16[40,896]{1,0:T(8,128)(2,1)S(1)} %get-tuple-element.40), channel_id=1, source_target_pairs={{0,6},{2,4},{4,2},{6,0},{8,14},{10,12},{12,10},{14,8},{1,7},{3,5},... | collective-permute-start | bytes 215048 | tf_op jit(solution)/shard_map/ppermute | solution.py:245
  31.1 1.5 %collective-permute-start.14 = (bf16[40,896]{1,0:T(8,128)(2,1)S(1)}, bf16[40,896]{1,0:T(8,128)(2,1)S(1)}, u32[]{:S(2)}, u32[]{:S(2)}) collective-permute-start(bf16[40,896]{1,0:T(8,128)(2,1)S(1)} %get-tuple-element.41), channel_id=1, source_target_pairs={{0,10},{2,8},{4,14},{6,12},{8,2},{10,0},{12,6},{14,4},{1,11},{3,9}... | collective-permute-start | bytes 215048 | tf_op jit(solution)/shard_map/ppermute | solution.py:245
  32.6 0.0 collective-permute-done.10.refs_2_
  32.6 2.1 %collective-permute-start.15 = (bf16[40,896]{1,0:T(8,128)(2,1)S(1)}, bf16[40,896]{1,0:T(8,128)(2,1)S(1)}, u32[]{:S(2)}, u32[]{:S(2)}) collective-permute-start(bf16[40,896]{1,0:T(8,128)(2,1)S(1)} %get-tuple-element.42), channel_id=1, source_target_pairs={{0,14},{2,12},{4,10},{6,8},{8,6},{10,4},{12,2},{14,0},{1,15},{3,13... | collective-permute-start | bytes 215048 | tf_op jit(solution)/shard_map/ppermute | solution.py:245
  34.6 0.0 collective-permute-done.11.refs_3_
  34.6 1.4 %collective-permute-start.16 = (bf16[40,896]{1,0:T(8,128)(2,1)S(1)}, bf16[40,896]{1,0:T(8,128)(2,1)S(1)}, u32[]{:S(2)}, u32[]{:S(2)}) collective-permute-start(bf16[40,896]{1,0:T(8,128)(2,1)S(1)} %get-tuple-element.43), channel_id=1, source_target_pairs={{0,4},{2,6},{4,0},{6,2},{8,12},{10,14},{12,8},{14,10},{1,5},{3,7},... | collective-permute-start | bytes 215048 | tf_op jit(solution)/shard_map/ppermute | solution.py:245
  36.0 0.0 copy-done.3
  36.0 0.0 copy-done.4
  36.0 0.3 plan.1
  36.3 0.5 %collective-permute-done.12.refs_4_ = bf16[40,896]{1,0:T(8,128)(2,1)S(1)} collective-permute-done((bf16[40,896]{1,0:T(8,128)(2,1)S(1)}, bf16[40,896]{1,0:T(8,128)(2,1)S(1)}, u32[]{:S(2)}, u32[]{:S(2)}) %collective-permute-start.12) | collective-permute-done | bytes 71712 | tf_op jit(solution)/shard_map/ppermute | solution.py:245
  36.8 0.0 collective-permute-done.13.refs_5_
  36.8 3.6 %collective-permute-done.14.refs_6_ = bf16[40,896]{1,0:T(8,128)(2,1)S(1)} collective-permute-done((bf16[40,896]{1,0:T(8,128)(2,1)S(1)}, bf16[40,896]{1,0:T(8,128)(2,1)S(1)}, u32[]{:S(2)}, u32[]{:S(2)}) %collective-permute-start.14) | collective-permute-done | bytes 71712 | tf_op jit(solution)/shard_map/ppermute | solution.py:245
  40.4 0.0 collective-permute-done.15.refs_7_
  40.4 0.0 collective-permute-done.16.refs_8_
  40.4 1.1 %combine.1 = bf16[64,1792]{1,0:T(8,128)(2,1)} custom-call(bf16[256,320]{1,0:T(8,128)(2,1)S(1)} %get-tuple-element.25.refs_0_, f32[128,128]{1,0:T(8,128)S(1)} %get-tuple-element.26.refs_1_, bf16[40,896]{1,0:T(8,128)(2,1)S(1)} %collective-permute-done.10.refs_2_, bf16[40,896]{1,0:T(8,128)(2,1)S(1)} %collective-permute-done.11.refs_3_, ...), custom_call_target="tpu_custom_call" | custom-call | tf_op jit(solution)/shard_map/combine/pallas_call | solution.py:330
Async XLA Ops:
  0.0 19.3 %copy-start = (bf16[1792,2048]{1,0:T(8,128)(2,1)S(1)}, bf16[1792,2048]{1,0:T(8,128)(2,1)}, u32[]{:S(2)}) copy-start(bf16[1792,2048]{1,0:T(8,128)(2,1)} %refs_1_.3) | copy-start | bytes 22020100
  0.0 19.3 %copy-start.1 = (bf16[1792,2048]{1,0:T(8,128)(2,1)S(1)}, bf16[1792,2048]{1,0:T(8,128)(2,1)}, u32[]{:S(2)}) copy-start(bf16[1792,2048]{1,0:T(8,128)(2,1)} %refs_2_.6) | copy-start | bytes 22020100
  0.0 19.3 %copy-start.2 = (bf16[2048,1792]{1,0:T(8,128)(2,1)S(1)}, bf16[2048,1792]{1,0:T(8,128)(2,1)}, u32[]{:S(2)}) copy-start(bf16[2048,1792]{1,0:T(8,128)(2,1)} %refs_2_.7) | copy-start | bytes 22020100
  1.6 10.0 %collective-permute-start = (bf16[40,896]{1,0:T(8,128)(2,1)S(1)}, bf16[40,896]{1,0:T(8,128)(2,1)S(1)}, u32[]{:S(2)}, u32[]{:S(2)}) collective-permute-start(bf16[40,896]{1,0:T(8,128)(2,1)S(1)} %get-tuple-element.27), channel_id=1, source_target_pairs={{0,12},{2,14},{4,8},{6,10},{8,4},{10,6},{12,0},{14,2},{1,13},{3,15... | collective-permute-start | bytes 215048 | tf_op jit(solution)/shard_map/ppermute | solution.py:245
  6.7 7.8 %collective-permute-start.1 = (bf16[40,896]{1,0:T(8,128)(2,1)S(1)}, bf16[40,896]{1,0:T(8,128)(2,1)S(1)}, u32[]{:S(2)}, u32[]{:S(2)}) collective-permute-start(bf16[40,896]{1,0:T(8,128)(2,1)S(1)} %get-tuple-element.28), channel_id=1, source_target_pairs={{0,2},{2,0},{4,6},{6,4},{8,10},{10,8},{12,14},{14,12},{1,3},{3,1},... | collective-permute-start | bytes 215048 | tf_op jit(solution)/shard_map/ppermute | solution.py:245
  8.2 6.8 %collective-permute-start.2 = (bf16[40,896]{1,0:T(8,128)(2,1)S(1)}, bf16[40,896]{1,0:T(8,128)(2,1)S(1)}, u32[]{:S(2)}, u32[]{:S(2)}) collective-permute-start(bf16[40,896]{1,0:T(8,128)(2,1)S(1)} %get-tuple-element.29), channel_id=1, source_target_pairs={{0,8},{2,10},{4,12},{6,14},{8,0},{10,2},{12,4},{14,6},{1,9},{3,11}... | collective-permute-start | bytes 215048 | tf_op jit(solution)/shard_map/ppermute | solution.py:245
  8.2 6.8 %collective-permute-start.3 = (bf16[40,896]{1,0:T(8,128)(2,1)S(1)}, bf16[40,896]{1,0:T(8,128)(2,1)S(1)}, u32[]{:S(2)}, u32[]{:S(2)}) collective-permute-start(bf16[40,896]{1,0:T(8,128)(2,1)S(1)} %get-tuple-element.30), channel_id=1, source_target_pairs={{0,6},{2,4},{4,2},{6,0},{8,14},{10,12},{12,10},{14,8},{1,7},{3,5},... | collective-permute-start | bytes 215048 | tf_op jit(solution)/shard_map/ppermute | solution.py:245
  8.8 9.4 %collective-permute-start.4 = (bf16[40,896]{1,0:T(8,128)(2,1)S(1)}, bf16[40,896]{1,0:T(8,128)(2,1)S(1)}, u32[]{:S(2)}, u32[]{:S(2)}) collective-permute-start(bf16[40,896]{1,0:T(8,128)(2,1)S(1)} %get-tuple-element.31), channel_id=1, source_target_pairs={{0,10},{2,8},{4,14},{6,12},{8,2},{10,0},{12,6},{14,4},{1,11},{3,9}... | collective-permute-start | bytes 215048 | tf_op jit(solution)/shard_map/ppermute | solution.py:245
  11.6 7.3 %collective-permute-start.5 = (bf16[40,896]{1,0:T(8,128)(2,1)S(1)}, bf16[40,896]{1,0:T(8,128)(2,1)S(1)}, u32[]{:S(2)}, u32[]{:S(2)}) collective-permute-start(bf16[40,896]{1,0:T(8,128)(2,1)S(1)} %get-tuple-element.32), channel_id=1, source_target_pairs={{0,14},{2,12},{4,10},{6,8},{8,6},{10,4},{12,2},{14,0},{1,15},{3,13... | collective-permute-start | bytes 215048 | tf_op jit(solution)/shard_map/ppermute | solution.py:245
  14.5 4.8 %collective-permute-start.6 = (bf16[40,896]{1,0:T(8,128)(2,1)S(1)}, bf16[40,896]{1,0:T(8,128)(2,1)S(1)}, u32[]{:S(2)}, u32[]{:S(2)}) collective-permute-start(bf16[40,896]{1,0:T(8,128)(2,1)S(1)} %get-tuple-element.33), channel_id=1, source_target_pairs={{0,4},{2,6},{4,0},{6,2},{8,12},{10,14},{12,8},{14,10},{1,5},{3,7},... | collective-permute-start | bytes 215048 | tf_op jit(solution)/shard_map/ppermute | solution.py:245
  20.7 2.7 %collective-permute-start.8 = (bf16[160,2048]{1,0:T(8,128)(2,1)S(1)}, bf16[160,2048]{1,0:T(8,128)(2,1)S(1)}, u32[]{:S(2)}, u32[]{:S(2)}) collective-permute-start(bf16[160,2048]{1,0:T(8,128)(2,1)S(1)} %get-tuple-element.36.refs_0_), channel_id=1, source_target_pairs={{0,1},{1,0},{2,3},{3,2},{4,5},{5,4},{6,7},{7,6},{8,9},{9,8},{10,11... | collective-permute-start | bytes 1966088 | tf_op jit(solution)/shard_map/ppermute | solution.py:245
  21.6 1.8 %collective-permute-start.9 = (bf16[160,1024]{1,0:T(8,128)(2,1)S(1)}, bf16[160,1024]{1,0:T(8,128)(2,1)S(1)}, u32[]{:S(2)}, u32[]{:S(2)}) collective-permute-start(bf16[160,1024]{1,0:T(8,128)(2,1)S(1)} %gate_up_next.3.refs_1_), channel_id=1, source_target_pairs={{0,1},{1,0},{2,3},{3,2},{4,5},{5,4},{6,7},{7,6},{8,9},{9,8},{10,11... | collective-permute-start | bytes 983048 | tf_op jit(solution)/shard_map/ppermute | solution.py:245
  22.9 13.1 %copy-start.3 = (s32[64,2]{0,1:T(2,128)S(1)}, s32[64,2]{0,1:T(2,128)}, u32[]{:S(2)}) copy-start(s32[64,2]{0,1:T(2,128)} %param.7) | copy-start | bytes 1540
  22.9 13.1 %copy-start.4 = (f32[64,2]{0,1:T(2,128)S(1)}, f32[64,2]{0,1:T(2,128)}, u32[]{:S(2)}) copy-start(f32[64,2]{0,1:T(2,128)} %param.8) | copy-start | bytes 1540
  22.9 1.7 %collective-permute-start.7 = (bf16[160,1024]{1,0:T(8,128)(2,1)S(1)}, bf16[160,1024]{1,0:T(8,128)(2,1)S(1)}, u32[]{:S(2)}, u32[]{:S(2)}) collective-permute-start(bf16[160,1024]{1,0:T(8,128)(2,1)S(1)} %gate_up_next.2.refs_0_), channel_id=1, source_target_pairs={{0,1},{1,0},{2,3},{3,2},{4,5},{5,4},{6,7},{7,6},{8,9},{9,8},{10,11... | collective-permute-start | bytes 983048 | tf_op jit(solution)/shard_map/ppermute | solution.py:245
  25.2 7.4 %collective-permute-start.10 = (bf16[40,896]{1,0:T(8,128)(2,1)S(1)}, bf16[40,896]{1,0:T(8,128)(2,1)S(1)}, u32[]{:S(2)}, u32[]{:S(2)}) collective-permute-start(bf16[40,896]{1,0:T(8,128)(2,1)S(1)} %get-tuple-element.37), channel_id=1, source_target_pairs={{0,12},{2,14},{4,8},{6,10},{8,4},{10,6},{12,0},{14,2},{1,13},{3,15... | collective-permute-start | bytes 215048 | tf_op jit(solution)/shard_map/ppermute | solution.py:245
  27.6 7.1 %collective-permute-start.11 = (bf16[40,896]{1,0:T(8,128)(2,1)S(1)}, bf16[40,896]{1,0:T(8,128)(2,1)S(1)}, u32[]{:S(2)}, u32[]{:S(2)}) collective-permute-start(bf16[40,896]{1,0:T(8,128)(2,1)S(1)} %get-tuple-element.38), channel_id=1, source_target_pairs={{0,2},{2,0},{4,6},{6,4},{8,10},{10,8},{12,14},{14,12},{1,3},{3,1},... | collective-permute-start | bytes 215048 | tf_op jit(solution)/shard_map/ppermute | solution.py:245
  28.4 8.4 %collective-permute-start.12 = (bf16[40,896]{1,0:T(8,128)(2,1)S(1)}, bf16[40,896]{1,0:T(8,128)(2,1)S(1)}, u32[]{:S(2)}, u32[]{:S(2)}) collective-permute-start(bf16[40,896]{1,0:T(8,128)(2,1)S(1)} %get-tuple-element.39), channel_id=1, source_target_pairs={{0,8},{2,10},{4,12},{6,14},{8,0},{10,2},{12,4},{14,6},{1,9},{3,11}... | collective-permute-start | bytes 215048 | tf_op jit(solution)/shard_map/ppermute | solution.py:245
  28.8 8.0 %collective-permute-start.13 = (bf16[40,896]{1,0:T(8,128)(2,1)S(1)}, bf16[40,896]{1,0:T(8,128)(2,1)S(1)}, u32[]{:S(2)}, u32[]{:S(2)}) collective-permute-start(bf16[40,896]{1,0:T(8,128)(2,1)S(1)} %get-tuple-element.40), channel_id=1, source_target_pairs={{0,6},{2,4},{4,2},{6,0},{8,14},{10,12},{12,10},{14,8},{1,7},{3,5},... | collective-permute-start | bytes 215048 | tf_op jit(solution)/shard_map/ppermute | solution.py:245
  31.1 9.3 %collective-permute-start.14 = (bf16[40,896]{1,0:T(8,128)(2,1)S(1)}, bf16[40,896]{1,0:T(8,128)(2,1)S(1)}, u32[]{:S(2)}, u32[]{:S(2)}) collective-permute-start(bf16[40,896]{1,0:T(8,128)(2,1)S(1)} %get-tuple-element.41), channel_id=1, source_target_pairs={{0,10},{2,8},{4,14},{6,12},{8,2},{10,0},{12,6},{14,4},{1,11},{3,9}... | collective-permute-start | bytes 215048 | tf_op jit(solution)/shard_map/ppermute | solution.py:245
  32.6 7.8 %collective-permute-start.15 = (bf16[40,896]{1,0:T(8,128)(2,1)S(1)}, bf16[40,896]{1,0:T(8,128)(2,1)S(1)}, u32[]{:S(2)}, u32[]{:S(2)}) collective-permute-start(bf16[40,896]{1,0:T(8,128)(2,1)S(1)} %get-tuple-element.42), channel_id=1, source_target_pairs={{0,14},{2,12},{4,10},{6,8},{8,6},{10,4},{12,2},{14,0},{1,15},{3,13... | collective-permute-start | bytes 215048 | tf_op jit(solution)/shard_map/ppermute | solution.py:245
  34.6 5.8 %collective-permute-start.16 = (bf16[40,896]{1,0:T(8,128)(2,1)S(1)}, bf16[40,896]{1,0:T(8,128)(2,1)S(1)}, u32[]{:S(2)}, u32[]{:S(2)}) collective-permute-start(bf16[40,896]{1,0:T(8,128)(2,1)S(1)} %get-tuple-element.43), channel_id=1, source_target_pairs={{0,4},{2,6},{4,0},{6,2},{8,12},{10,14},{12,8},{14,10},{1,5},{3,7},... | collective-permute-start | bytes 215048 | tf_op jit(solution)/shard_map/ppermute | solution.py:245

commit v5 on v4

--- a/solution.py
+++ b/solution.py
@@ -94,20 +94,27 @@
 
 def dispatch_kernel(n, cap, me_ref, ids_hbm, tok_hbm, *refs):
     out_refs, (ids_ref, tok_ref, sems) = refs[:n], refs[n:]
+    tok_rows, half = tok_ref.shape[0] // 2, tok_ref.shape[1]
     ids_copy = pltpu.make_async_copy(ids_hbm, ids_ref, sems.at[0])
-    tok_copy = pltpu.make_async_copy(tok_hbm, tok_ref, sems.at[1])
+    tok_copies = [
+        pltpu.make_async_copy(
+            tok_hbm.at[:, pl.ds(part * half, half)],
+            tok_ref.at[pl.ds(part * tok_rows, tok_rows), :],
+            sems.at[1 + part],
+        )
+        for part in range(2)
+    ]
     ids_copy.start()
-    tok_copy.start()
-    tok_rows, width = tok_ref.shape
-    half = width // 2
+    for copy in tok_copies:
+        copy.start()
     ids_copy.wait()
     rows = slot_rows(ids_ref, me_ref[0], n, cap, tok_rows)
-    number = lax.broadcasted_iota(jnp.int32, (2 * cap * n, tok_rows), 0)
-    upper = jnp.where((number == rows[0]) | (number == rows[1]), 1.0, 0.0).astype(BF16)
-    lower = jnp.where((number == rows[0] + cap) | (number == rows[1] + cap), 1.0, 0.0).astype(BF16)
-    tok_copy.wait()
-    packed = jnp.dot(upper, tok_ref[:, :half], preferred_element_type=F32)
-    packed = packed + jnp.dot(lower, tok_ref[:, half:], preferred_element_type=F32)
+    rows = [jnp.concatenate([row, row + cap], axis=1) for row in rows]
+    number = lax.broadcasted_iota(jnp.int32, (2 * cap * n, 2 * tok_rows), 0)
+    pick = jnp.where((number == rows[0]) | (number == rows[1]), 1.0, 0.0).astype(BF16)
+    for copy in tok_copies:
+        copy.wait()
+    packed = jnp.dot(pick, tok_ref[...], preferred_element_type=F32)
     for o, out_ref in zip(STARTS, out_refs):
         out_ref[...] = packed[o * 2 * cap : (o + 1) * 2 * cap].astype(BF16)
 
@@ -307,8 +314,8 @@
         hbm=2,
         scratch=[
             pltpu.VMEM(ids.shape, ids.dtype),
-            pltpu.VMEM(tokens.shape, tokens.dtype),
-            pltpu.SemaphoreType.DMA((2,)),
+            pltpu.VMEM((2 * tok_rows, half), tokens.dtype),
+            pltpu.SemaphoreType.DMA((3,)),
         ],
         cost=pl.CostEstimate(flops=20_000_000_000, bytes_accessed=2 * loaded, transcendentals=0),
         name="dispatch",

time: 41.7 us -> 41.6 us (level)
  no operation moved by 1% of the time
where the time goes in v5:
time: 41.6 us; the launch traced here: 41.4 us
  starting transfers between devices  24.4 us (59%)
  waiting for transfers between devices  9.46 us (23%)
  Pallas kernels  7.4 us (18%)
    ppermute x17, starting transfers between devices, swap(): lax.ppermute(x, axis, [(i, i ^ distance) for i in range(lax.axis_size(axi...  24.4 us
    ppermute x17, waiting for transfers between devices, swap(): lax.ppermute(x, axis, [(i, i ^ distance) for i in range(lax.axis_size(axi...  9.46 us
    pallas_call x7, Pallas kernels, call(): pl.pallas_call(kernel, out_shape=[pltpu.VMEM(o.shape, o.dtype) for o in (...  6.31 us
    pallas_call x1, Pallas kernels, one_expert_each(): pl.pallas_call(lambda *refs: combine_kernel(cap, PLACES, *refs), out_shap...  1.08 us
  transfers between devices with their start and end apart: 17, of which 8 were waited for; matrix products, arithmetic and copies ran while one was open for 0% of the time, Pallas kernels for 7%

profile of v5, /device:TPU:0, one launch (start us, length us, event | category | flops | bytes accessed | tf_op | source)
XLA Modules:
  0.0 41.4 jit_solution(9239273752391308891)
XLA Ops:
  0.0 0.0 copy-start
  0.0 0.0 copy-start.1
  0.0 0.0 copy-start.2
  0.0 1.4 %dispatch.1 = (bf16[40,896]{1,0:T(8,128)(2,1)S(1)}, bf16[40,896]{1,0:T(8,128)(2,1)S(1)}, bf16[40,896]{1,0:T(8,128)(2,1)S(1)}, bf16[40,896]{1,0:T(8,128)(2,1)S(1)...) custom-call(s32[1]{0:T(128)} %bitcast.refs_0_, ...), custom_call_target="tpu_custom_call" | custom-call | flops 20000000000 | bytes 44040192 | tf_op jit(solution)/shard_map/dispatch/pallas_call | solution.py:234
  1.5 5.1 %collective-permute-start = (bf16[40,896]{1,0:T(8,128)(2,1)S(1)}, bf16[40,896]{1,0:T(8,128)(2,1)S(1)}, u32[]{:S(2)}, u32[]{:S(2)}) collective-permute-start(bf16[40,896]{1,0:T(8,128)(2,1)S(1)} %get-tuple-element.27), channel_id=1, source_target_pairs={{0,12},{2,14},{4,8},{6,10},{8,4},{10,6},{12,0},{14,2},{1,13},{3,15... | collective-permute-start | bytes 215048 | tf_op jit(solution)/shard_map/ppermute | solution.py:252
  6.6 1.5 %collective-permute-start.1 = (bf16[40,896]{1,0:T(8,128)(2,1)S(1)}, bf16[40,896]{1,0:T(8,128)(2,1)S(1)}, u32[]{:S(2)}, u32[]{:S(2)}) collective-permute-start(bf16[40,896]{1,0:T(8,128)(2,1)S(1)} %get-tuple-element.28), channel_id=1, source_target_pairs={{0,2},{2,0},{4,6},{6,4},{8,10},{10,8},{12,14},{14,12},{1,3},{3,1},... | collective-permute-start | bytes 215048 | tf_op jit(solution)/shard_map/ppermute | solution.py:252
  8.1 0.0 collective-permute-start.2
  8.1 0.6 %collective-permute-start.3 = (bf16[40,896]{1,0:T(8,128)(2,1)S(1)}, bf16[40,896]{1,0:T(8,128)(2,1)S(1)}, u32[]{:S(2)}, u32[]{:S(2)}) collective-permute-start(bf16[40,896]{1,0:T(8,128)(2,1)S(1)} %get-tuple-element.30), channel_id=1, source_target_pairs={{0,6},{2,4},{4,2},{6,0},{8,14},{10,12},{12,10},{14,8},{1,7},{3,5},... | collective-permute-start | bytes 215048 | tf_op jit(solution)/shard_map/ppermute | solution.py:252
  8.7 2.8 %collective-permute-start.4 = (bf16[40,896]{1,0:T(8,128)(2,1)S(1)}, bf16[40,896]{1,0:T(8,128)(2,1)S(1)}, u32[]{:S(2)}, u32[]{:S(2)}) collective-permute-start(bf16[40,896]{1,0:T(8,128)(2,1)S(1)} %get-tuple-element.31), channel_id=1, source_target_pairs={{0,10},{2,8},{4,14},{6,12},{8,2},{10,0},{12,6},{14,4},{1,11},{3,9}... | collective-permute-start | bytes 215048 | tf_op jit(solution)/shard_map/ppermute | solution.py:252
  11.5 0.0 collective-permute-done.refs_0_
  11.5 3.0 %collective-permute-start.5 = (bf16[40,896]{1,0:T(8,128)(2,1)S(1)}, bf16[40,896]{1,0:T(8,128)(2,1)S(1)}, u32[]{:S(2)}, u32[]{:S(2)}) collective-permute-start(bf16[40,896]{1,0:T(8,128)(2,1)S(1)} %get-tuple-element.32), channel_id=1, source_target_pairs={{0,14},{2,12},{4,10},{6,8},{8,6},{10,4},{12,2},{14,0},{1,15},{3,13... | collective-permute-start | bytes 215048 | tf_op jit(solution)/shard_map/ppermute | solution.py:252
  14.4 0.0 collective-permute-done.1.refs_1_
  14.4 0.0 collective-permute-start.6
  14.4 0.5 %collective-permute-done.2.refs_2_ = bf16[40,896]{1,0:T(8,128)(2,1)S(1)} collective-permute-done((bf16[40,896]{1,0:T(8,128)(2,1)S(1)}, bf16[40,896]{1,0:T(8,128)(2,1)S(1)}, u32[]{:S(2)}, u32[]{:S(2)}) %collective-permute-start.2) | collective-permute-done | bytes 71712 | tf_op jit(solution)/shard_map/ppermute | solution.py:252
  14.9 0.0 collective-permute-done.3.refs_3_
  14.9 3.2 %collective-permute-done.4.refs_4_ = bf16[40,896]{1,0:T(8,128)(2,1)S(1)} collective-permute-done((bf16[40,896]{1,0:T(8,128)(2,1)S(1)}, bf16[40,896]{1,0:T(8,128)(2,1)S(1)}, u32[]{:S(2)}, u32[]{:S(2)}) %collective-permute-start.4) | collective-permute-done | bytes 71712 | tf_op jit(solution)/shard_map/ppermute | solution.py:252
  18.1 0.7 %collective-permute-done.5.refs_5_ = bf16[40,896]{1,0:T(8,128)(2,1)S(1)} collective-permute-done((bf16[40,896]{1,0:T(8,128)(2,1)S(1)}, bf16[40,896]{1,0:T(8,128)(2,1)S(1)}, u32[]{:S(2)}, u32[]{:S(2)}) %collective-permute-start.5) | collective-permute-done | bytes 71712 | tf_op jit(solution)/shard_map/ppermute | solution.py:252
  18.8 0.4 collective-permute-done.6.refs_6_
  19.2 0.0 copy-done
  19.2 0.0 copy-done.1
  19.2 0.0 copy-done.2
  19.2 1.4 %gate_up_first.1 = (bf16[160,2048]{1,0:T(8,128)(2,1)S(1)}, bf16[160,1792]{1,0:T(8,128)(2,1)S(1)}) custom-call(bf16[40,896]{1,0:T(8,128)(2,1)S(1)} %collective-permute-done.refs_0_, bf16[40,896]{1,0:T(8,128)(2,1)S(1)} %collective-permute-done.1.refs_1_, bf16[40,896]{1,0:T(8,128)(2,1)S(1)} %collective-permute-done.2.refs_2_, ...), custom_call_target="tpu_custom_call" | custom-call | flops 1 | tf_op jit(solution)/shard_map/gate_up_first/pallas_call | solution.py:234
  20.6 0.1 collective-permute-start.8
  20.7 0.8 %gate_up_next.3.refs_1_ = bf16[160,1024]{1,0:T(8,128)(2,1)S(1)} custom-call(bf16[160,1792]{1,0:T(8,128)(2,1)S(1)} %get-tuple-element.35.refs_0_, bf16[1792,2048]{1,0:T(8,128)(2,1)S(1)} %copy-done, bf16[1792,2048]{1,0:T(8,128)(2,1)S(1)} %copy-done.1), custom_call_target="tpu_custom_call" | custom-call | flops 1 | tf_op jit(solution)/shard_map/gate_up_next/pallas_call | solution.py:234
  21.5 0.6 %collective-permute-start.9 = (bf16[160,1024]{1,0:T(8,128)(2,1)S(1)}, bf16[160,1024]{1,0:T(8,128)(2,1)S(1)}, u32[]{:S(2)}, u32[]{:S(2)}) collective-permute-start(bf16[160,1024]{1,0:T(8,128)(2,1)S(1)} %gate_up_next.3.refs_1_), channel_id=1, source_target_pairs={{0,1},{1,0},{2,3},{3,2},{4,5},{5,4},{6,7},{7,6},{8,9},{9,8},{10,11... | collective-permute-start | bytes 983048 | tf_op jit(solution)/shard_map/ppermute | solution.py:252
  22.0 0.8 %gate_up_next.2.refs_0_ = bf16[160,1024]{1,0:T(8,128)(2,1)S(1)} custom-call(bf16[160,1792]{1,0:T(8,128)(2,1)S(1)} %get-tuple-element.35.refs_0_, bf16[1792,2048]{1,0:T(8,128)(2,1)S(1)} %copy-done, bf16[1792,2048]{1,0:T(8,128)(2,1)S(1)} %copy-done.1), custom_call_target="tpu_custom_call" | custom-call | flops 1 | tf_op jit(solution)/shard_map/gate_up_next/pallas_call | solution.py:234
  22.8 0.0 copy-start.3
  22.8 0.0 copy-start.4
  22.8 0.1 collective-permute-start.7
  22.9 0.4 collective-permute-done.9.refs_3_
  23.3 0.0 collective-permute-done.8.refs_2_
  23.3 1.1 %down_first.1.refs_3_ = f32[160,1792]{1,0:T(8,128)S(1)} custom-call(bf16[160,2048]{1,0:T(8,128)(2,1)S(1)} %get-tuple-element.36.refs_0_, bf16[160,1024]{1,0:T(8,128)(2,1)S(1)} %gate_up_next.3.refs_1_, bf16[160,2048]{1,0:T(8,128)(2,1)S(1)} %collective-permute-done.8.refs_2_, bf16[160,1024]{1,0:T(8,128)(2,1)S(1)} %collective-permute-done.9.refs_3_, ...), custom_call_target="tpu_custom_call" | custom-call | flops 1 | tf_op jit(solution)/shard_map/down_first/pallas_call | solution.py:234
  24.4 0.1 collective-permute-done.7.refs_1_
  24.5 0.6 %down_last.1 = (bf16[40,896]{1,0:T(8,128)(2,1)S(1)}, bf16[40,896]{1,0:T(8,128)(2,1)S(1)}, bf16[40,896]{1,0:T(8,128)(2,1)S(1)}, bf16[40,896]{1,0:T(8,128)(2,1)S(1...) custom-call(bf16[160,1024]{1,0:T(8,128)(2,1)S(1)} %gate_up_next.2.re, ...), custom_call_target="tpu_custom_call" | custom-call | flops 1 | tf_op jit(solution)/shard_map/down_last/pallas_call | solution.py:234
  25.1 2.4 %collective-permute-start.10 = (bf16[40,896]{1,0:T(8,128)(2,1)S(1)}, bf16[40,896]{1,0:T(8,128)(2,1)S(1)}, u32[]{:S(2)}, u32[]{:S(2)}) collective-permute-start(bf16[40,896]{1,0:T(8,128)(2,1)S(1)} %get-tuple-element.37), channel_id=1, source_target_pairs={{0,12},{2,14},{4,8},{6,10},{8,4},{10,6},{12,0},{14,2},{1,13},{3,15... | collective-permute-start | bytes 215048 | tf_op jit(solution)/shard_map/ppermute | solution.py:252
  27.5 0.8 %collective-permute-start.11 = (bf16[40,896]{1,0:T(8,128)(2,1)S(1)}, bf16[40,896]{1,0:T(8,128)(2,1)S(1)}, u32[]{:S(2)}, u32[]{:S(2)}) collective-permute-start(bf16[40,896]{1,0:T(8,128)(2,1)S(1)} %get-tuple-element.38), channel_id=1, source_target_pairs={{0,2},{2,0},{4,6},{6,4},{8,10},{10,8},{12,14},{14,12},{1,3},{3,1},... | collective-permute-start | bytes 215048 | tf_op jit(solution)/shard_map/ppermute | solution.py:252
  28.3 0.5 %collective-permute-start.12 = (bf16[40,896]{1,0:T(8,128)(2,1)S(1)}, bf16[40,896]{1,0:T(8,128)(2,1)S(1)}, u32[]{:S(2)}, u32[]{:S(2)}) collective-permute-start(bf16[40,896]{1,0:T(8,128)(2,1)S(1)} %get-tuple-element.39), channel_id=1, source_target_pairs={{0,8},{2,10},{4,12},{6,14},{8,0},{10,2},{12,4},{14,6},{1,9},{3,11}... | collective-permute-start | bytes 215048 | tf_op jit(solution)/shard_map/ppermute | solution.py:252
  28.7 2.3 %collective-permute-start.13 = (bf16[40,896]{1,0:T(8,128)(2,1)S(1)}, bf16[40,896]{1,0:T(8,128)(2,1)S(1)}, u32[]{:S(2)}, u32[]{:S(2)}) collective-permute-start(bf16[40,896]{1,0:T(8,128)(2,1)S(1)} %get-tuple-element.40), channel_id=1, source_target_pairs={{0,6},{2,4},{4,2},{6,0},{8,14},{10,12},{12,10},{14,8},{1,7},{3,5},... | collective-permute-start | bytes 215048 | tf_op jit(solution)/shard_map/ppermute | solution.py:252
  31.0 1.5 %collective-permute-start.14 = (bf16[40,896]{1,0:T(8,128)(2,1)S(1)}, bf16[40,896]{1,0:T(8,128)(2,1)S(1)}, u32[]{:S(2)}, u32[]{:S(2)}) collective-permute-start(bf16[40,896]{1,0:T(8,128)(2,1)S(1)} %get-tuple-element.41), channel_id=1, source_target_pairs={{0,10},{2,8},{4,14},{6,12},{8,2},{10,0},{12,6},{14,4},{1,11},{3,9}... | collective-permute-start | bytes 215048 | tf_op jit(solution)/shard_map/ppermute | solution.py:252
  32.5 0.0 collective-permute-done.10.refs_2_
  32.5 2.1 %collective-permute-start.15 = (bf16[40,896]{1,0:T(8,128)(2,1)S(1)}, bf16[40,896]{1,0:T(8,128)(2,1)S(1)}, u32[]{:S(2)}, u32[]{:S(2)}) collective-permute-start(bf16[40,896]{1,0:T(8,128)(2,1)S(1)} %get-tuple-element.42), channel_id=1, source_target_pairs={{0,14},{2,12},{4,10},{6,8},{8,6},{10,4},{12,2},{14,0},{1,15},{3,13... | collective-permute-start | bytes 215048 | tf_op jit(solution)/shard_map/ppermute | solution.py:252
  34.5 0.0 collective-permute-done.11.refs_3_
  34.5 1.3 %collective-permute-start.16 = (bf16[40,896]{1,0:T(8,128)(2,1)S(1)}, bf16[40,896]{1,0:T(8,128)(2,1)S(1)}, u32[]{:S(2)}, u32[]{:S(2)}) collective-permute-start(bf16[40,896]{1,0:T(8,128)(2,1)S(1)} %get-tuple-element.43), channel_id=1, source_target_pairs={{0,4},{2,6},{4,0},{6,2},{8,12},{10,14},{12,8},{14,10},{1,5},{3,7},... | collective-permute-start | bytes 215048 | tf_op jit(solution)/shard_map/ppermute | solution.py:252
  35.8 0.0 copy-done.3
  35.8 0.0 copy-done.4
  35.8 0.3 plan.1
  36.1 0.6 %collective-permute-done.12.refs_4_ = bf16[40,896]{1,0:T(8,128)(2,1)S(1)} collective-permute-done((bf16[40,896]{1,0:T(8,128)(2,1)S(1)}, bf16[40,896]{1,0:T(8,128)(2,1)S(1)}, u32[]{:S(2)}, u32[]{:S(2)}) %collective-permute-start.12) | collective-permute-done | bytes 71712 | tf_op jit(solution)/shard_map/ppermute | solution.py:252
  36.7 0.0 collective-permute-done.13.refs_5_
  36.7 3.6 %collective-permute-done.14.refs_6_ = bf16[40,896]{1,0:T(8,128)(2,1)S(1)} collective-permute-done((bf16[40,896]{1,0:T(8,128)(2,1)S(1)}, bf16[40,896]{1,0:T(8,128)(2,1)S(1)}, u32[]{:S(2)}, u32[]{:S(2)}) %collective-permute-start.14) | collective-permute-done | bytes 71712 | tf_op jit(solution)/shard_map/ppermute | solution.py:252
  40.3 0.0 collective-permute-done.15.refs_7_
  40.3 0.0 collective-permute-done.16.refs_8_
  40.3 1.1 %combine.1 = bf16[64,1792]{1,0:T(8,128)(2,1)} custom-call(bf16[256,320]{1,0:T(8,128)(2,1)S(1)} %get-tuple-element.25.refs_0_, f32[128,128]{1,0:T(8,128)S(1)} %get-tuple-element.26.refs_1_, bf16[40,896]{1,0:T(8,128)(2,1)S(1)} %collective-permute-done.10.refs_2_, bf16[40,896]{1,0:T(8,128)(2,1)S(1)} %collective-permute-done.11.refs_3_, ...), custom_call_target="tpu_custom_call" | custom-call | tf_op jit(solution)/shard_map/combine/pallas_call | solution.py:337
Async XLA Ops:
  0.0 19.2 %copy-start = (bf16[1792,2048]{1,0:T(8,128)(2,1)S(1)}, bf16[1792,2048]{1,0:T(8,128)(2,1)}, u32[]{:S(2)}) copy-start(bf16[1792,2048]{1,0:T(8,128)(2,1)} %refs_1_.3) | copy-start | bytes 22020100
  0.0 19.2 %copy-start.1 = (bf16[1792,2048]{1,0:T(8,128)(2,1)S(1)}, bf16[1792,2048]{1,0:T(8,128)(2,1)}, u32[]{:S(2)}) copy-start(bf16[1792,2048]{1,0:T(8,128)(2,1)} %refs_2_.6) | copy-start | bytes 22020100
  0.0 19.2 %copy-start.2 = (bf16[2048,1792]{1,0:T(8,128)(2,1)S(1)}, bf16[2048,1792]{1,0:T(8,128)(2,1)}, u32[]{:S(2)}) copy-start(bf16[2048,1792]{1,0:T(8,128)(2,1)} %refs_2_.7) | copy-start | bytes 22020100
  1.5 10.0 %collective-permute-start = (bf16[40,896]{1,0:T(8,128)(2,1)S(1)}, bf16[40,896]{1,0:T(8,128)(2,1)S(1)}, u32[]{:S(2)}, u32[]{:S(2)}) collective-permute-start(bf16[40,896]{1,0:T(8,128)(2,1)S(1)} %get-tuple-element.27), channel_id=1, source_target_pairs={{0,12},{2,14},{4,8},{6,10},{8,4},{10,6},{12,0},{14,2},{1,13},{3,15... | collective-permute-start | bytes 215048 | tf_op jit(solution)/shard_map/ppermute | solution.py:252
  6.6 7.8 %collective-permute-start.1 = (bf16[40,896]{1,0:T(8,128)(2,1)S(1)}, bf16[40,896]{1,0:T(8,128)(2,1)S(1)}, u32[]{:S(2)}, u32[]{:S(2)}) collective-permute-start(bf16[40,896]{1,0:T(8,128)(2,1)S(1)} %get-tuple-element.28), channel_id=1, source_target_pairs={{0,2},{2,0},{4,6},{6,4},{8,10},{10,8},{12,14},{14,12},{1,3},{3,1},... | collective-permute-start | bytes 215048 | tf_op jit(solution)/shard_map/ppermute | solution.py:252
  8.1 6.8 %collective-permute-start.2 = (bf16[40,896]{1,0:T(8,128)(2,1)S(1)}, bf16[40,896]{1,0:T(8,128)(2,1)S(1)}, u32[]{:S(2)}, u32[]{:S(2)}) collective-permute-start(bf16[40,896]{1,0:T(8,128)(2,1)S(1)} %get-tuple-element.29), channel_id=1, source_target_pairs={{0,8},{2,10},{4,12},{6,14},{8,0},{10,2},{12,4},{14,6},{1,9},{3,11}... | collective-permute-start | bytes 215048 | tf_op jit(solution)/shard_map/ppermute | solution.py:252
  8.1 6.8 %collective-permute-start.3 = (bf16[40,896]{1,0:T(8,128)(2,1)S(1)}, bf16[40,896]{1,0:T(8,128)(2,1)S(1)}, u32[]{:S(2)}, u32[]{:S(2)}) collective-permute-start(bf16[40,896]{1,0:T(8,128)(2,1)S(1)} %get-tuple-element.30), channel_id=1, source_target_pairs={{0,6},{2,4},{4,2},{6,0},{8,14},{10,12},{12,10},{14,8},{1,7},{3,5},... | collective-permute-start | bytes 215048 | tf_op jit(solution)/shard_map/ppermute | solution.py:252
  8.7 9.4 %collective-permute-start.4 = (bf16[40,896]{1,0:T(8,128)(2,1)S(1)}, bf16[40,896]{1,0:T(8,128)(2,1)S(1)}, u32[]{:S(2)}, u32[]{:S(2)}) collective-permute-start(bf16[40,896]{1,0:T(8,128)(2,1)S(1)} %get-tuple-element.31), channel_id=1, source_target_pairs={{0,10},{2,8},{4,14},{6,12},{8,2},{10,0},{12,6},{14,4},{1,11},{3,9}... | collective-permute-start | bytes 215048 | tf_op jit(solution)/shard_map/ppermute | solution.py:252
  11.5 7.3 %collective-permute-start.5 = (bf16[40,896]{1,0:T(8,128)(2,1)S(1)}, bf16[40,896]{1,0:T(8,128)(2,1)S(1)}, u32[]{:S(2)}, u32[]{:S(2)}) collective-permute-start(bf16[40,896]{1,0:T(8,128)(2,1)S(1)} %get-tuple-element.32), channel_id=1, source_target_pairs={{0,14},{2,12},{4,10},{6,8},{8,6},{10,4},{12,2},{14,0},{1,15},{3,13... | collective-permute-start | bytes 215048 | tf_op jit(solution)/shard_map/ppermute | solution.py:252
  14.4 4.8 %collective-permute-start.6 = (bf16[40,896]{1,0:T(8,128)(2,1)S(1)}, bf16[40,896]{1,0:T(8,128)(2,1)S(1)}, u32[]{:S(2)}, u32[]{:S(2)}) collective-permute-start(bf16[40,896]{1,0:T(8,128)(2,1)S(1)} %get-tuple-element.33), channel_id=1, source_target_pairs={{0,4},{2,6},{4,0},{6,2},{8,12},{10,14},{12,8},{14,10},{1,5},{3,7},... | collective-permute-start | bytes 215048 | tf_op jit(solution)/shard_map/ppermute | solution.py:252
  20.6 2.7 %collective-permute-start.8 = (bf16[160,2048]{1,0:T(8,128)(2,1)S(1)}, bf16[160,2048]{1,0:T(8,128)(2,1)S(1)}, u32[]{:S(2)}, u32[]{:S(2)}) collective-permute-start(bf16[160,2048]{1,0:T(8,128)(2,1)S(1)} %get-tuple-element.36.refs_0_), channel_id=1, source_target_pairs={{0,1},{1,0},{2,3},{3,2},{4,5},{5,4},{6,7},{7,6},{8,9},{9,8},{10,11... | collective-permute-start | bytes 1966088 | tf_op jit(solution)/shard_map/ppermute | solution.py:252
  21.5 1.8 %collective-permute-start.9 = (bf16[160,1024]{1,0:T(8,128)(2,1)S(1)}, bf16[160,1024]{1,0:T(8,128)(2,1)S(1)}, u32[]{:S(2)}, u32[]{:S(2)}) collective-permute-start(bf16[160,1024]{1,0:T(8,128)(2,1)S(1)} %gate_up_next.3.refs_1_), channel_id=1, source_target_pairs={{0,1},{1,0},{2,3},{3,2},{4,5},{5,4},{6,7},{7,6},{8,9},{9,8},{10,11... | collective-permute-start | bytes 983048 | tf_op jit(solution)/shard_map/ppermute | solution.py:252
  22.8 13.1 %copy-start.3 = (s32[64,2]{0,1:T(2,128)S(1)}, s32[64,2]{0,1:T(2,128)}, u32[]{:S(2)}) copy-start(s32[64,2]{0,1:T(2,128)} %param.7) | copy-start | bytes 1540
  22.8 13.1 %copy-start.4 = (f32[64,2]{0,1:T(2,128)S(1)}, f32[64,2]{0,1:T(2,128)}, u32[]{:S(2)}) copy-start(f32[64,2]{0,1:T(2,128)} %param.8) | copy-start | bytes 1540
  22.8 1.7 %collective-permute-start.7 = (bf16[160,1024]{1,0:T(8,128)(2,1)S(1)}, bf16[160,1024]{1,0:T(8,128)(2,1)S(1)}, u32[]{:S(2)}, u32[]{:S(2)}) collective-permute-start(bf16[160,1024]{1,0:T(8,128)(2,1)S(1)} %gate_up_next.2.refs_0_), channel_id=1, source_target_pairs={{0,1},{1,0},{2,3},{3,2},{4,5},{5,4},{6,7},{7,6},{8,9},{9,8},{10,11... | collective-permute-start | bytes 983048 | tf_op jit(solution)/shard_map/ppermute | solution.py:252
  25.1 7.4 %collective-permute-start.10 = (bf16[40,896]{1,0:T(8,128)(2,1)S(1)}, bf16[40,896]{1,0:T(8,128)(2,1)S(1)}, u32[]{:S(2)}, u32[]{:S(2)}) collective-permute-start(bf16[40,896]{1,0:T(8,128)(2,1)S(1)} %get-tuple-element.37), channel_id=1, source_target_pairs={{0,12},{2,14},{4,8},{6,10},{8,4},{10,6},{12,0},{14,2},{1,13},{3,15... | collective-permute-start | bytes 215048 | tf_op jit(solution)/shard_map/ppermute | solution.py:252
  27.5 7.1 %collective-permute-start.11 = (bf16[40,896]{1,0:T(8,128)(2,1)S(1)}, bf16[40,896]{1,0:T(8,128)(2,1)S(1)}, u32[]{:S(2)}, u32[]{:S(2)}) collective-permute-start(bf16[40,896]{1,0:T(8,128)(2,1)S(1)} %get-tuple-element.38), channel_id=1, source_target_pairs={{0,2},{2,0},{4,6},{6,4},{8,10},{10,8},{12,14},{14,12},{1,3},{3,1},... | collective-permute-start | bytes 215048 | tf_op jit(solution)/shard_map/ppermute | solution.py:252
  28.3 8.4 %collective-permute-start.12 = (bf16[40,896]{1,0:T(8,128)(2,1)S(1)}, bf16[40,896]{1,0:T(8,128)(2,1)S(1)}, u32[]{:S(2)}, u32[]{:S(2)}) collective-permute-start(bf16[40,896]{1,0:T(8,128)(2,1)S(1)} %get-tuple-element.39), channel_id=1, source_target_pairs={{0,8},{2,10},{4,12},{6,14},{8,0},{10,2},{12,4},{14,6},{1,9},{3,11}... | collective-permute-start | bytes 215048 | tf_op jit(solution)/shard_map/ppermute | solution.py:252
  28.7 8.0 %collective-permute-start.13 = (bf16[40,896]{1,0:T(8,128)(2,1)S(1)}, bf16[40,896]{1,0:T(8,128)(2,1)S(1)}, u32[]{:S(2)}, u32[]{:S(2)}) collective-permute-start(bf16[40,896]{1,0:T(8,128)(2,1)S(1)} %get-tuple-element.40), channel_id=1, source_target_pairs={{0,6},{2,4},{4,2},{6,0},{8,14},{10,12},{12,10},{14,8},{1,7},{3,5},... | collective-permute-start | bytes 215048 | tf_op jit(solution)/shard_map/ppermute | solution.py:252
  31.0 9.3 %collective-permute-start.14 = (bf16[40,896]{1,0:T(8,128)(2,1)S(1)}, bf16[40,896]{1,0:T(8,128)(2,1)S(1)}, u32[]{:S(2)}, u32[]{:S(2)}) collective-permute-start(bf16[40,896]{1,0:T(8,128)(2,1)S(1)} %get-tuple-element.41), channel_id=1, source_target_pairs={{0,10},{2,8},{4,14},{6,12},{8,2},{10,0},{12,6},{14,4},{1,11},{3,9}... | collective-permute-start | bytes 215048 | tf_op jit(solution)/shard_map/ppermute | solution.py:252
  32.5 7.9 %collective-permute-start.15 = (bf16[40,896]{1,0:T(8,128)(2,1)S(1)}, bf16[40,896]{1,0:T(8,128)(2,1)S(1)}, u32[]{:S(2)}, u32[]{:S(2)}) collective-permute-start(bf16[40,896]{1,0:T(8,128)(2,1)S(1)} %get-tuple-element.42), channel_id=1, source_target_pairs={{0,14},{2,12},{4,10},{6,8},{8,6},{10,4},{12,2},{14,0},{1,15},{3,13... | collective-permute-start | bytes 215048 | tf_op jit(solution)/shard_map/ppermute | solution.py:252
  34.5 5.8 %collective-permute-start.16 = (bf16[40,896]{1,0:T(8,128)(2,1)S(1)}, bf16[40,896]{1,0:T(8,128)(2,1)S(1)}, u32[]{:S(2)}, u32[]{:S(2)}) collective-permute-start(bf16[40,896]{1,0:T(8,128)(2,1)S(1)} %get-tuple-element.43), channel_id=1, source_target_pairs={{0,4},{2,6},{4,0},{6,2},{8,12},{10,14},{12,8},{14,10},{1,5},{3,7},... | collective-permute-start | bytes 215048 | tf_op jit(solution)/shard_map/ppermute | solution.py:252

commit v6 on v5

--- a/solution.py
+++ b/solution.py
@@ -98,11 +98,12 @@
     ids_copy = pltpu.make_async_copy(ids_hbm, ids_ref, sems.at[0])
     tok_copies = [
         pltpu.make_async_copy(
-            tok_hbm.at[:, pl.ds(part * half, half)],
-            tok_ref.at[pl.ds(part * tok_rows, tok_rows), :],
-            sems.at[1 + part],
+            tok_hbm.at[pl.ds(row, tok_rows // 2), pl.ds(part * half, half)],
+            tok_ref.at[pl.ds(part * tok_rows + row, tok_rows // 2), :],
+            sems.at[1 + 2 * part + i],
         )
         for part in range(2)
+        for i, row in enumerate((0, tok_rows // 2))
     ]
     ids_copy.start()
     for copy in tok_copies:
@@ -156,11 +157,11 @@
     total, start = None, 0
     for i in range(count):
         width = own[i].shape[1] // 2
-        for low in range(0, width, 512):
-            hidden = hidden_of(own[i], other[i], low, 512)
-            term = jnp.dot(hidden, wd_ref[pl.ds(start, 512), :], preferred_element_type=F32)
+        for low in range(0, width, 256):
+            hidden = hidden_of(own[i], other[i], low, 256)
+            term = jnp.dot(hidden, wd_ref[pl.ds(start, 256), :], preferred_element_type=F32)
             total = term if total is None else total + term
-            start += 512
+            start += 256
     acc_ref[...] = total
 
 
@@ -315,7 +316,7 @@
         scratch=[
             pltpu.VMEM(ids.shape, ids.dtype),
             pltpu.VMEM((2 * tok_rows, half), tokens.dtype),
-            pltpu.SemaphoreType.DMA((3,)),
+            pltpu.SemaphoreType.DMA((5,)),
         ],
         cost=pl.CostEstimate(flops=20_000_000_000, bytes_accessed=2 * loaded, transcendentals=0),
         name="dispatch",

time: 41.6 us -> 41.5 us (level)
  no operation moved by 1% of the time
where the time goes in v6:
time: 41.5 us; the launch traced here: 41.3 us
  starting transfers between devices  24.4 us (59%)
  waiting for transfers between devices  9.5 us (23%)
  Pallas kernels  7.32 us (18%)
    ppermute x17, starting transfers between devices, swap(): lax.ppermute(x, axis, [(i, i ^ distance) for i in range(lax.axis_size(axi...  24.4 us
    ppermute x17, waiting for transfers between devices, swap(): lax.ppermute(x, axis, [(i, i ^ distance) for i in range(lax.axis_size(axi...  9.5 us
    pallas_call x7, Pallas kernels, call(): pl.pallas_call(kernel, out_shape=[pltpu.VMEM(o.shape, o.dtype) for o in (...  6.24 us
    pallas_call x1, Pallas kernels, one_expert_each(): pl.pallas_call(lambda *refs: combine_kernel(cap, PLACES, *refs), out_shap...  1.08 us
  transfers between devices with their start and end apart: 17, of which 8 were waited for; matrix products, arithmetic and copies ran while one was open for 0% of the time, Pallas kernels for 7%

profile of v6, /device:TPU:0, one launch (start us, length us, event | category | flops | bytes accessed | tf_op | source)
XLA Modules:
  0.0 41.3 jit_solution(6257417114328027427)
XLA Ops:
  0.0 0.0 copy-start
  0.0 0.0 copy-start.1
  0.0 0.0 copy-start.2
  0.0 1.4 %dispatch.1 = (bf16[40,896]{1,0:T(8,128)(2,1)S(1)}, bf16[40,896]{1,0:T(8,128)(2,1)S(1)}, bf16[40,896]{1,0:T(8,128)(2,1)S(1)}, bf16[40,896]{1,0:T(8,128)(2,1)S(1)...) custom-call(s32[1]{0:T(128)} %bitcast.refs_0_, ...), custom_call_target="tpu_custom_call" | custom-call | flops 20000000000 | bytes 44040192 | tf_op jit(solution)/shard_map/dispatch/pallas_call | solution.py:235
  1.4 5.1 %collective-permute-start = (bf16[40,896]{1,0:T(8,128)(2,1)S(1)}, bf16[40,896]{1,0:T(8,128)(2,1)S(1)}, u32[]{:S(2)}, u32[]{:S(2)}) collective-permute-start(bf16[40,896]{1,0:T(8,128)(2,1)S(1)} %get-tuple-element.27), channel_id=1, source_target_pairs={{0,12},{2,14},{4,8},{6,10},{8,4},{10,6},{12,0},{14,2},{1,13},{3,15... | collective-permute-start | bytes 215048 | tf_op jit(solution)/shard_map/ppermute | solution.py:253
  6.6 1.5 %collective-permute-start.1 = (bf16[40,896]{1,0:T(8,128)(2,1)S(1)}, bf16[40,896]{1,0:T(8,128)(2,1)S(1)}, u32[]{:S(2)}, u32[]{:S(2)}) collective-permute-start(bf16[40,896]{1,0:T(8,128)(2,1)S(1)} %get-tuple-element.28), channel_id=1, source_target_pairs={{0,2},{2,0},{4,6},{6,4},{8,10},{10,8},{12,14},{14,12},{1,3},{3,1},... | collective-permute-start | bytes 215048 | tf_op jit(solution)/shard_map/ppermute | solution.py:253
  8.0 0.0 collective-permute-start.2
  8.0 0.6 %collective-permute-start.3 = (bf16[40,896]{1,0:T(8,128)(2,1)S(1)}, bf16[40,896]{1,0:T(8,128)(2,1)S(1)}, u32[]{:S(2)}, u32[]{:S(2)}) collective-permute-start(bf16[40,896]{1,0:T(8,128)(2,1)S(1)} %get-tuple-element.30), channel_id=1, source_target_pairs={{0,6},{2,4},{4,2},{6,0},{8,14},{10,12},{12,10},{14,8},{1,7},{3,5},... | collective-permute-start | bytes 215048 | tf_op jit(solution)/shard_map/ppermute | solution.py:253
  8.7 2.8 %collective-permute-start.4 = (bf16[40,896]{1,0:T(8,128)(2,1)S(1)}, bf16[40,896]{1,0:T(8,128)(2,1)S(1)}, u32[]{:S(2)}, u32[]{:S(2)}) collective-permute-start(bf16[40,896]{1,0:T(8,128)(2,1)S(1)} %get-tuple-element.31), channel_id=1, source_target_pairs={{0,10},{2,8},{4,14},{6,12},{8,2},{10,0},{12,6},{14,4},{1,11},{3,9}... | collective-permute-start | bytes 215048 | tf_op jit(solution)/shard_map/ppermute | solution.py:253
  11.4 0.0 collective-permute-done.refs_0_
  11.4 3.0 %collective-permute-start.5 = (bf16[40,896]{1,0:T(8,128)(2,1)S(1)}, bf16[40,896]{1,0:T(8,128)(2,1)S(1)}, u32[]{:S(2)}, u32[]{:S(2)}) collective-permute-start(bf16[40,896]{1,0:T(8,128)(2,1)S(1)} %get-tuple-element.32), channel_id=1, source_target_pairs={{0,14},{2,12},{4,10},{6,8},{8,6},{10,4},{12,2},{14,0},{1,15},{3,13... | collective-permute-start | bytes 215048 | tf_op jit(solution)/shard_map/ppermute | solution.py:253
  14.4 0.0 collective-permute-done.1.refs_1_
  14.4 0.0 collective-permute-start.6
  14.4 0.5 %collective-permute-done.2.refs_2_ = bf16[40,896]{1,0:T(8,128)(2,1)S(1)} collective-permute-done((bf16[40,896]{1,0:T(8,128)(2,1)S(1)}, bf16[40,896]{1,0:T(8,128)(2,1)S(1)}, u32[]{:S(2)}, u32[]{:S(2)}) %collective-permute-start.2) | collective-permute-done | bytes 71712 | tf_op jit(solution)/shard_map/ppermute | solution.py:253
  14.9 0.0 collective-permute-done.3.refs_3_
  14.9 3.2 %collective-permute-done.4.refs_4_ = bf16[40,896]{1,0:T(8,128)(2,1)S(1)} collective-permute-done((bf16[40,896]{1,0:T(8,128)(2,1)S(1)}, bf16[40,896]{1,0:T(8,128)(2,1)S(1)}, u32[]{:S(2)}, u32[]{:S(2)}) %collective-permute-start.4) | collective-permute-done | bytes 71712 | tf_op jit(solution)/shard_map/ppermute | solution.py:253
  18.1 0.7 %collective-permute-done.5.refs_5_ = bf16[40,896]{1,0:T(8,128)(2,1)S(1)} collective-permute-done((bf16[40,896]{1,0:T(8,128)(2,1)S(1)}, bf16[40,896]{1,0:T(8,128)(2,1)S(1)}, u32[]{:S(2)}, u32[]{:S(2)}) %collective-permute-start.5) | collective-permute-done | bytes 71712 | tf_op jit(solution)/shard_map/ppermute | solution.py:253
  18.8 0.4 collective-permute-done.6.refs_6_
  19.2 0.0 copy-done
  19.2 0.0 copy-done.1
  19.2 0.0 copy-done.2
  19.2 1.4 %gate_up_first.1 = (bf16[160,2048]{1,0:T(8,128)(2,1)S(1)}, bf16[160,1792]{1,0:T(8,128)(2,1)S(1)}) custom-call(bf16[40,896]{1,0:T(8,128)(2,1)S(1)} %collective-permute-done.refs_0_, bf16[40,896]{1,0:T(8,128)(2,1)S(1)} %collective-permute-done.1.refs_1_, bf16[40,896]{1,0:T(8,128)(2,1)S(1)} %collective-permute-done.2.refs_2_, ...), custom_call_target="tpu_custom_call" | custom-call | flops 1 | tf_op jit(solution)/shard_map/gate_up_first/pallas_call | solution.py:235
  20.6 0.1 collective-permute-start.8
  20.7 0.8 %gate_up_next.3.refs_1_ = bf16[160,1024]{1,0:T(8,128)(2,1)S(1)} custom-call(bf16[160,1792]{1,0:T(8,128)(2,1)S(1)} %get-tuple-element.35.refs_0_, bf16[1792,2048]{1,0:T(8,128)(2,1)S(1)} %copy-done, bf16[1792,2048]{1,0:T(8,128)(2,1)S(1)} %copy-done.1), custom_call_target="tpu_custom_call" | custom-call | flops 1 | tf_op jit(solution)/shard_map/gate_up_next/pallas_call | solution.py:235
  21.4 0.6 %collective-permute-start.9 = (bf16[160,1024]{1,0:T(8,128)(2,1)S(1)}, bf16[160,1024]{1,0:T(8,128)(2,1)S(1)}, u32[]{:S(2)}, u32[]{:S(2)}) collective-permute-start(bf16[160,1024]{1,0:T(8,128)(2,1)S(1)} %gate_up_next.3.refs_1_), channel_id=1, source_target_pairs={{0,1},{1,0},{2,3},{3,2},{4,5},{5,4},{6,7},{7,6},{8,9},{9,8},{10,11... | collective-permute-start | bytes 983048 | tf_op jit(solution)/shard_map/ppermute | solution.py:253
  22.0 0.8 %gate_up_next.2.refs_0_ = bf16[160,1024]{1,0:T(8,128)(2,1)S(1)} custom-call(bf16[160,1792]{1,0:T(8,128)(2,1)S(1)} %get-tuple-element.35.refs_0_, bf16[1792,2048]{1,0:T(8,128)(2,1)S(1)} %copy-done, bf16[1792,2048]{1,0:T(8,128)(2,1)S(1)} %copy-done.1), custom_call_target="tpu_custom_call" | custom-call | flops 1 | tf_op jit(solution)/shard_map/gate_up_next/pallas_call | solution.py:235
  22.8 0.0 copy-start.3
  22.8 0.0 copy-start.4
  22.8 0.1 collective-permute-start.7
  22.9 0.4 collective-permute-done.9.refs_3_
  23.2 0.0 collective-permute-done.8.refs_2_
  23.2 1.1 %down_first.1.refs_3_ = f32[160,1792]{1,0:T(8,128)S(1)} custom-call(bf16[160,2048]{1,0:T(8,128)(2,1)S(1)} %get-tuple-element.36.refs_0_, bf16[160,1024]{1,0:T(8,128)(2,1)S(1)} %gate_up_next.3.refs_1_, bf16[160,2048]{1,0:T(8,128)(2,1)S(1)} %collective-permute-done.8.refs_2_, bf16[160,1024]{1,0:T(8,128)(2,1)S(1)} %collective-permute-done.9.refs_3_, ...), custom_call_target="tpu_custom_call" | custom-call | flops 1 | tf_op jit(solution)/shard_map/down_first/pallas_call | solution.py:235
  24.4 0.1 collective-permute-done.7.refs_1_
  24.5 0.6 %down_last.1 = (bf16[40,896]{1,0:T(8,128)(2,1)S(1)}, bf16[40,896]{1,0:T(8,128)(2,1)S(1)}, bf16[40,896]{1,0:T(8,128)(2,1)S(1)}, bf16[40,896]{1,0:T(8,128)(2,1)S(1...) custom-call(bf16[160,1024]{1,0:T(8,128)(2,1)S(1)} %gate_up_next.2.re, ...), custom_call_target="tpu_custom_call" | custom-call | flops 1 | tf_op jit(solution)/shard_map/down_last/pallas_call | solution.py:235
  25.1 2.4 %collective-permute-start.10 = (bf16[40,896]{1,0:T(8,128)(2,1)S(1)}, bf16[40,896]{1,0:T(8,128)(2,1)S(1)}, u32[]{:S(2)}, u32[]{:S(2)}) collective-permute-start(bf16[40,896]{1,0:T(8,128)(2,1)S(1)} %get-tuple-element.37), channel_id=1, source_target_pairs={{0,12},{2,14},{4,8},{6,10},{8,4},{10,6},{12,0},{14,2},{1,13},{3,15... | collective-permute-start | bytes 215048 | tf_op jit(solution)/shard_map/ppermute | solution.py:253
  27.4 0.8 %collective-permute-start.11 = (bf16[40,896]{1,0:T(8,128)(2,1)S(1)}, bf16[40,896]{1,0:T(8,128)(2,1)S(1)}, u32[]{:S(2)}, u32[]{:S(2)}) collective-permute-start(bf16[40,896]{1,0:T(8,128)(2,1)S(1)} %get-tuple-element.38), channel_id=1, source_target_pairs={{0,2},{2,0},{4,6},{6,4},{8,10},{10,8},{12,14},{14,12},{1,3},{3,1},... | collective-permute-start | bytes 215048 | tf_op jit(solution)/shard_map/ppermute | solution.py:253
  28.2 0.5 %collective-permute-start.12 = (bf16[40,896]{1,0:T(8,128)(2,1)S(1)}, bf16[40,896]{1,0:T(8,128)(2,1)S(1)}, u32[]{:S(2)}, u32[]{:S(2)}) collective-permute-start(bf16[40,896]{1,0:T(8,128)(2,1)S(1)} %get-tuple-element.39), channel_id=1, source_target_pairs={{0,8},{2,10},{4,12},{6,14},{8,0},{10,2},{12,4},{14,6},{1,9},{3,11}... | collective-permute-start | bytes 215048 | tf_op jit(solution)/shard_map/ppermute | solution.py:253
  28.7 2.3 %collective-permute-start.13 = (bf16[40,896]{1,0:T(8,128)(2,1)S(1)}, bf16[40,896]{1,0:T(8,128)(2,1)S(1)}, u32[]{:S(2)}, u32[]{:S(2)}) collective-permute-start(bf16[40,896]{1,0:T(8,128)(2,1)S(1)} %get-tuple-element.40), channel_id=1, source_target_pairs={{0,6},{2,4},{4,2},{6,0},{8,14},{10,12},{12,10},{14,8},{1,7},{3,5},... | collective-permute-start | bytes 215048 | tf_op jit(solution)/shard_map/ppermute | solution.py:253
  31.0 1.5 %collective-permute-start.14 = (bf16[40,896]{1,0:T(8,128)(2,1)S(1)}, bf16[40,896]{1,0:T(8,128)(2,1)S(1)}, u32[]{:S(2)}, u32[]{:S(2)}) collective-permute-start(bf16[40,896]{1,0:T(8,128)(2,1)S(1)} %get-tuple-element.41), channel_id=1, source_target_pairs={{0,10},{2,8},{4,14},{6,12},{8,2},{10,0},{12,6},{14,4},{1,11},{3,9}... | collective-permute-start | bytes 215048 | tf_op jit(solution)/shard_map/ppermute | solution.py:253
  32.4 0.0 collective-permute-done.10.refs_2_
  32.4 2.0 %collective-permute-start.15 = (bf16[40,896]{1,0:T(8,128)(2,1)S(1)}, bf16[40,896]{1,0:T(8,128)(2,1)S(1)}, u32[]{:S(2)}, u32[]{:S(2)}) collective-permute-start(bf16[40,896]{1,0:T(8,128)(2,1)S(1)} %get-tuple-element.42), channel_id=1, source_target_pairs={{0,14},{2,12},{4,10},{6,8},{8,6},{10,4},{12,2},{14,0},{1,15},{3,13... | collective-permute-start | bytes 215048 | tf_op jit(solution)/shard_map/ppermute | solution.py:253
  34.5 0.0 collective-permute-done.11.refs_3_
  34.5 1.3 %collective-permute-start.16 = (bf16[40,896]{1,0:T(8,128)(2,1)S(1)}, bf16[40,896]{1,0:T(8,128)(2,1)S(1)}, u32[]{:S(2)}, u32[]{:S(2)}) collective-permute-start(bf16[40,896]{1,0:T(8,128)(2,1)S(1)} %get-tuple-element.43), channel_id=1, source_target_pairs={{0,4},{2,6},{4,0},{6,2},{8,12},{10,14},{12,8},{14,10},{1,5},{3,7},... | collective-permute-start | bytes 215048 | tf_op jit(solution)/shard_map/ppermute | solution.py:253
  35.8 0.0 copy-done.3
  35.8 0.0 copy-done.4
  35.8 0.3 plan.1
  36.0 0.6 %collective-permute-done.12.refs_4_ = bf16[40,896]{1,0:T(8,128)(2,1)S(1)} collective-permute-done((bf16[40,896]{1,0:T(8,128)(2,1)S(1)}, bf16[40,896]{1,0:T(8,128)(2,1)S(1)}, u32[]{:S(2)}, u32[]{:S(2)}) %collective-permute-start.12) | collective-permute-done | bytes 71712 | tf_op jit(solution)/shard_map/ppermute | solution.py:253
  36.6 0.0 collective-permute-done.13.refs_5_
  36.6 3.6 %collective-permute-done.14.refs_6_ = bf16[40,896]{1,0:T(8,128)(2,1)S(1)} collective-permute-done((bf16[40,896]{1,0:T(8,128)(2,1)S(1)}, bf16[40,896]{1,0:T(8,128)(2,1)S(1)}, u32[]{:S(2)}, u32[]{:S(2)}) %collective-permute-start.14) | collective-permute-done | bytes 71712 | tf_op jit(solution)/shard_map/ppermute | solution.py:253
  40.2 0.0 collective-permute-done.15.refs_7_
  40.2 0.0 collective-permute-done.16.refs_8_
  40.3 1.1 %combine.1 = bf16[64,1792]{1,0:T(8,128)(2,1)} custom-call(bf16[256,320]{1,0:T(8,128)(2,1)S(1)} %get-tuple-element.25.refs_0_, f32[128,128]{1,0:T(8,128)S(1)} %get-tuple-element.26.refs_1_, bf16[40,896]{1,0:T(8,128)(2,1)S(1)} %collective-permute-done.10.refs_2_, bf16[40,896]{1,0:T(8,128)(2,1)S(1)} %collective-permute-done.11.refs_3_, ...), custom_call_target="tpu_custom_call" | custom-call | tf_op jit(solution)/shard_map/combine/pallas_call | solution.py:338
Async XLA Ops:
  0.0 19.2 %copy-start = (bf16[1792,2048]{1,0:T(8,128)(2,1)S(1)}, bf16[1792,2048]{1,0:T(8,128)(2,1)}, u32[]{:S(2)}) copy-start(bf16[1792,2048]{1,0:T(8,128)(2,1)} %refs_1_.3) | copy-start | bytes 22020100
  0.0 19.2 %copy-start.1 = (bf16[1792,2048]{1,0:T(8,128)(2,1)S(1)}, bf16[1792,2048]{1,0:T(8,128)(2,1)}, u32[]{:S(2)}) copy-start(bf16[1792,2048]{1,0:T(8,128)(2,1)} %refs_2_.6) | copy-start | bytes 22020100
  0.0 19.2 %copy-start.2 = (bf16[2048,1792]{1,0:T(8,128)(2,1)S(1)}, bf16[2048,1792]{1,0:T(8,128)(2,1)}, u32[]{:S(2)}) copy-start(bf16[2048,1792]{1,0:T(8,128)(2,1)} %refs_2_.7) | copy-start | bytes 22020100
  1.4 10.0 %collective-permute-start = (bf16[40,896]{1,0:T(8,128)(2,1)S(1)}, bf16[40,896]{1,0:T(8,128)(2,1)S(1)}, u32[]{:S(2)}, u32[]{:S(2)}) collective-permute-start(bf16[40,896]{1,0:T(8,128)(2,1)S(1)} %get-tuple-element.27), channel_id=1, source_target_pairs={{0,12},{2,14},{4,8},{6,10},{8,4},{10,6},{12,0},{14,2},{1,13},{3,15... | collective-permute-start | bytes 215048 | tf_op jit(solution)/shard_map/ppermute | solution.py:253
  6.6 7.8 %collective-permute-start.1 = (bf16[40,896]{1,0:T(8,128)(2,1)S(1)}, bf16[40,896]{1,0:T(8,128)(2,1)S(1)}, u32[]{:S(2)}, u32[]{:S(2)}) collective-permute-start(bf16[40,896]{1,0:T(8,128)(2,1)S(1)} %get-tuple-element.28), channel_id=1, source_target_pairs={{0,2},{2,0},{4,6},{6,4},{8,10},{10,8},{12,14},{14,12},{1,3},{3,1},... | collective-permute-start | bytes 215048 | tf_op jit(solution)/shard_map/ppermute | solution.py:253
  8.0 6.8 %collective-permute-start.2 = (bf16[40,896]{1,0:T(8,128)(2,1)S(1)}, bf16[40,896]{1,0:T(8,128)(2,1)S(1)}, u32[]{:S(2)}, u32[]{:S(2)}) collective-permute-start(bf16[40,896]{1,0:T(8,128)(2,1)S(1)} %get-tuple-element.29), channel_id=1, source_target_pairs={{0,8},{2,10},{4,12},{6,14},{8,0},{10,2},{12,4},{14,6},{1,9},{3,11}... | collective-permute-start | bytes 215048 | tf_op jit(solution)/shard_map/ppermute | solution.py:253
  8.0 6.8 %collective-permute-start.3 = (bf16[40,896]{1,0:T(8,128)(2,1)S(1)}, bf16[40,896]{1,0:T(8,128)(2,1)S(1)}, u32[]{:S(2)}, u32[]{:S(2)}) collective-permute-start(bf16[40,896]{1,0:T(8,128)(2,1)S(1)} %get-tuple-element.30), channel_id=1, source_target_pairs={{0,6},{2,4},{4,2},{6,0},{8,14},{10,12},{12,10},{14,8},{1,7},{3,5},... | collective-permute-start | bytes 215048 | tf_op jit(solution)/shard_map/ppermute | solution.py:253
  8.7 9.4 %collective-permute-start.4 = (bf16[40,896]{1,0:T(8,128)(2,1)S(1)}, bf16[40,896]{1,0:T(8,128)(2,1)S(1)}, u32[]{:S(2)}, u32[]{:S(2)}) collective-permute-start(bf16[40,896]{1,0:T(8,128)(2,1)S(1)} %get-tuple-element.31), channel_id=1, source_target_pairs={{0,10},{2,8},{4,14},{6,12},{8,2},{10,0},{12,6},{14,4},{1,11},{3,9}... | collective-permute-start | bytes 215048 | tf_op jit(solution)/shard_map/ppermute | solution.py:253
  11.4 7.3 %collective-permute-start.5 = (bf16[40,896]{1,0:T(8,128)(2,1)S(1)}, bf16[40,896]{1,0:T(8,128)(2,1)S(1)}, u32[]{:S(2)}, u32[]{:S(2)}) collective-permute-start(bf16[40,896]{1,0:T(8,128)(2,1)S(1)} %get-tuple-element.32), channel_id=1, source_target_pairs={{0,14},{2,12},{4,10},{6,8},{8,6},{10,4},{12,2},{14,0},{1,15},{3,13... | collective-permute-start | bytes 215048 | tf_op jit(solution)/shard_map/ppermute | solution.py:253
  14.4 4.8 %collective-permute-start.6 = (bf16[40,896]{1,0:T(8,128)(2,1)S(1)}, bf16[40,896]{1,0:T(8,128)(2,1)S(1)}, u32[]{:S(2)}, u32[]{:S(2)}) collective-permute-start(bf16[40,896]{1,0:T(8,128)(2,1)S(1)} %get-tuple-element.33), channel_id=1, source_target_pairs={{0,4},{2,6},{4,0},{6,2},{8,12},{10,14},{12,8},{14,10},{1,5},{3,7},... | collective-permute-start | bytes 215048 | tf_op jit(solution)/shard_map/ppermute | solution.py:253
  20.6 2.7 %collective-permute-start.8 = (bf16[160,2048]{1,0:T(8,128)(2,1)S(1)}, bf16[160,2048]{1,0:T(8,128)(2,1)S(1)}, u32[]{:S(2)}, u32[]{:S(2)}) collective-permute-start(bf16[160,2048]{1,0:T(8,128)(2,1)S(1)} %get-tuple-element.36.refs_0_), channel_id=1, source_target_pairs={{0,1},{1,0},{2,3},{3,2},{4,5},{5,4},{6,7},{7,6},{8,9},{9,8},{10,11... | collective-permute-start | bytes 1966088 | tf_op jit(solution)/shard_map/ppermute | solution.py:253
  21.4 1.8 %collective-permute-start.9 = (bf16[160,1024]{1,0:T(8,128)(2,1)S(1)}, bf16[160,1024]{1,0:T(8,128)(2,1)S(1)}, u32[]{:S(2)}, u32[]{:S(2)}) collective-permute-start(bf16[160,1024]{1,0:T(8,128)(2,1)S(1)} %gate_up_next.3.refs_1_), channel_id=1, source_target_pairs={{0,1},{1,0},{2,3},{3,2},{4,5},{5,4},{6,7},{7,6},{8,9},{9,8},{10,11... | collective-permute-start | bytes 983048 | tf_op jit(solution)/shard_map/ppermute | solution.py:253
  22.8 13.0 %copy-start.3 = (s32[64,2]{0,1:T(2,128)S(1)}, s32[64,2]{0,1:T(2,128)}, u32[]{:S(2)}) copy-start(s32[64,2]{0,1:T(2,128)} %param.7) | copy-start | bytes 1540
  22.8 13.0 %copy-start.4 = (f32[64,2]{0,1:T(2,128)S(1)}, f32[64,2]{0,1:T(2,128)}, u32[]{:S(2)}) copy-start(f32[64,2]{0,1:T(2,128)} %param.8) | copy-start | bytes 1540
  22.8 1.7 %collective-permute-start.7 = (bf16[160,1024]{1,0:T(8,128)(2,1)S(1)}, bf16[160,1024]{1,0:T(8,128)(2,1)S(1)}, u32[]{:S(2)}, u32[]{:S(2)}) collective-permute-start(bf16[160,1024]{1,0:T(8,128)(2,1)S(1)} %gate_up_next.2.refs_0_), channel_id=1, source_target_pairs={{0,1},{1,0},{2,3},{3,2},{4,5},{5,4},{6,7},{7,6},{8,9},{9,8},{10,11... | collective-permute-start | bytes 983048 | tf_op jit(solution)/shard_map/ppermute | solution.py:253
  25.1 7.4 %collective-permute-start.10 = (bf16[40,896]{1,0:T(8,128)(2,1)S(1)}, bf16[40,896]{1,0:T(8,128)(2,1)S(1)}, u32[]{:S(2)}, u32[]{:S(2)}) collective-permute-start(bf16[40,896]{1,0:T(8,128)(2,1)S(1)} %get-tuple-element.37), channel_id=1, source_target_pairs={{0,12},{2,14},{4,8},{6,10},{8,4},{10,6},{12,0},{14,2},{1,13},{3,15... | collective-permute-start | bytes 215048 | tf_op jit(solution)/shard_map/ppermute | solution.py:253
  27.4 7.1 %collective-permute-start.11 = (bf16[40,896]{1,0:T(8,128)(2,1)S(1)}, bf16[40,896]{1,0:T(8,128)(2,1)S(1)}, u32[]{:S(2)}, u32[]{:S(2)}) collective-permute-start(bf16[40,896]{1,0:T(8,128)(2,1)S(1)} %get-tuple-element.38), channel_id=1, source_target_pairs={{0,2},{2,0},{4,6},{6,4},{8,10},{10,8},{12,14},{14,12},{1,3},{3,1},... | collective-permute-start | bytes 215048 | tf_op jit(solution)/shard_map/ppermute | solution.py:253
  28.2 8.4 %collective-permute-start.12 = (bf16[40,896]{1,0:T(8,128)(2,1)S(1)}, bf16[40,896]{1,0:T(8,128)(2,1)S(1)}, u32[]{:S(2)}, u32[]{:S(2)}) collective-permute-start(bf16[40,896]{1,0:T(8,128)(2,1)S(1)} %get-tuple-element.39), channel_id=1, source_target_pairs={{0,8},{2,10},{4,12},{6,14},{8,0},{10,2},{12,4},{14,6},{1,9},{3,11}... | collective-permute-start | bytes 215048 | tf_op jit(solution)/shard_map/ppermute | solution.py:253
  28.7 7.9 %collective-permute-start.13 = (bf16[40,896]{1,0:T(8,128)(2,1)S(1)}, bf16[40,896]{1,0:T(8,128)(2,1)S(1)}, u32[]{:S(2)}, u32[]{:S(2)}) collective-permute-start(bf16[40,896]{1,0:T(8,128)(2,1)S(1)} %get-tuple-element.40), channel_id=1, source_target_pairs={{0,6},{2,4},{4,2},{6,0},{8,14},{10,12},{12,10},{14,8},{1,7},{3,5},... | collective-permute-start | bytes 215048 | tf_op jit(solution)/shard_map/ppermute | solution.py:253
  31.0 9.3 %collective-permute-start.14 = (bf16[40,896]{1,0:T(8,128)(2,1)S(1)}, bf16[40,896]{1,0:T(8,128)(2,1)S(1)}, u32[]{:S(2)}, u32[]{:S(2)}) collective-permute-start(bf16[40,896]{1,0:T(8,128)(2,1)S(1)} %get-tuple-element.41), channel_id=1, source_target_pairs={{0,10},{2,8},{4,14},{6,12},{8,2},{10,0},{12,6},{14,4},{1,11},{3,9}... | collective-permute-start | bytes 215048 | tf_op jit(solution)/shard_map/ppermute | solution.py:253
  32.4 7.8 %collective-permute-start.15 = (bf16[40,896]{1,0:T(8,128)(2,1)S(1)}, bf16[40,896]{1,0:T(8,128)(2,1)S(1)}, u32[]{:S(2)}, u32[]{:S(2)}) collective-permute-start(bf16[40,896]{1,0:T(8,128)(2,1)S(1)} %get-tuple-element.42), channel_id=1, source_target_pairs={{0,14},{2,12},{4,10},{6,8},{8,6},{10,4},{12,2},{14,0},{1,15},{3,13... | collective-permute-start | bytes 215048 | tf_op jit(solution)/shard_map/ppermute | solution.py:253
  34.5 5.8 %collective-permute-start.16 = (bf16[40,896]{1,0:T(8,128)(2,1)S(1)}, bf16[40,896]{1,0:T(8,128)(2,1)S(1)}, u32[]{:S(2)}, u32[]{:S(2)}) collective-permute-start(bf16[40,896]{1,0:T(8,128)(2,1)S(1)} %get-tuple-element.43), channel_id=1, source_target_pairs={{0,4},{2,6},{4,0},{6,2},{8,12},{10,14},{12,8},{14,10},{1,5},{3,7},... | collective-permute-start | bytes 215048 | tf_op jit(solution)/shard_map/ppermute | solution.py:253
